TPU v7x, 32 devices: a whole 2x2x4 slice. The times are simulated.
32 devices in a mesh: sta: 8 (over y, x, core), tm: 4 (over z).
Axes of the slice: x: 2, y: 2, z: 4, core: 2. Of those that a mesh axis runs over, the one named last changes fastest.
Arguments:
- waves: bfloat16 [3, 1024, 4, 512], P(None, 'sta', 'tm'), may hold values from -6 to 6
- partner: int32 [7, 8], replicated, may hold values from 0 to 7, as said below
- pair_count: int32 [8], P('sta'), may hold values from 192 to 256, as said below
- left_station: int32 [8, 256], P('sta'), may hold values from 0 to 127, as said below
- right_station: int32 [8, 256], P('sta'), may hold values from 0 to 127
- owner: int32 [8, 256], P('sta'), may hold values from 0 to 7, as said below
Outputs:
- stacks: float32 [4096, 2304], P('sta', 'tm')
Inputs may be any that keep to these rules, and one draw needn't show every extreme that they name: partner[k, i] = i XOR r_k, where r_0, ..., r_(6) are the numbers 1 to 7 in an order drawn from the seed. `pair_count`: each list's count is at least three quarters of 256; some list is full. Within one list the pairs (left_station, right_station) are all different. `owner`: among the first pair_count entries of a list, no block is named more than 64 times; one block, drawn from the seed, is named exactly 64 times in every list.
All inputs are finite; a program needn't handle non-finite values.
Results may differ from a plain program's by a relative error of at most 0.0032.
Values may be sent and summed in bfloat16 or wider, within the bound.
No kernel may reach another device: no remote copies, remote signals or barrier semaphores. Data moves between devices by JAX's collectives and lax.ppermute only.
A program may use at most 64 MiB of HBM per device.

v0:
```python
import math

import jax
import jax.numpy as jnp
from jax import lax
from jax.sharding import PartitionSpec as P

LAGS = 256
HALF_BAND = 21


epsilon = 1e-06


def partner_2(value, axis, stride):
    mask = 2**stride
    pairs = [(source, source ^ mask) for source in range(lax.axis_size(axis))]
    return lax.ppermute(value, axis, pairs)


def make_dft_table(samples, freq_count):
    sample_index = jnp.arange(samples, dtype=jnp.int32)[:, None]
    freq_index = jnp.arange(freq_count, dtype=jnp.int32)[None, :]
    phases = (
        2.0 * math.pi / samples * jnp.mod(sample_index * freq_index, samples).astype(jnp.float32)
    )
    return jnp.concatenate([jnp.cos(phases), -jnp.sin(phases)], axis=1).astype(jnp.bfloat16)


def make_lag_table(samples, freq_count, lag_count):
    freq_index = jnp.arange(freq_count, dtype=jnp.int32)[:, None]
    lag_index = jnp.arange(lag_count, dtype=jnp.int32)[None, :] - lag_count // 2
    phases = 2.0 * math.pi / samples * jnp.mod(freq_index * lag_index, samples).astype(jnp.float32)
    return jnp.concatenate([jnp.cos(phases), -jnp.sin(phases)], axis=0)


def make_band(freq_count, half_band):
    freq_index = jnp.arange(freq_count, dtype=jnp.int32)
    band_matrix = (jnp.abs(freq_index[:, None] - freq_index[None, :]) <= half_band).astype(
        jnp.float32
    )
    return (band_matrix, jnp.sum(band_matrix, axis=0))


def whiten(records, dft_table, band_matrix, band_count):
    dims_in = records.shape
    spectra = jnp.dot(
        records.reshape(-1, dims_in[-1]), dft_table, preferred_element_type=jnp.float32
    )
    spectra = spectra.reshape(dims_in[:-1] + (dft_table.shape[1],))
    freq_count = dft_table.shape[1] // 2
    magnitude = jnp.sqrt(spectra[..., :freq_count] ** 2 + spectra[..., freq_count:] ** 2)
    amplitude = jnp.sum(magnitude, axis=-4)
    smooth = jnp.dot(
        amplitude.reshape(-1, freq_count), band_matrix, precision=lax.Precision.HIGHEST
    )
    smooth = smooth.reshape(amplitude.shape) / (3.0 * band_count) + epsilon
    smooth = jnp.concatenate([smooth, smooth], axis=-1)
    return spectra / jnp.expand_dims(smooth, -4)


def correlate(left_white, right_white, left_index, right_index, lag_table, scale):
    precise = lax.Precision.HIGHEST
    left_rows = jnp.take(left_white, left_index, axis=1)
    right_rows = jnp.take(right_white, right_index, axis=1)
    freq_count = left_rows.shape[-1] // 2
    left_real, left_imag = (left_rows[..., :freq_count], left_rows[..., freq_count:])
    right_real, right_imag = (right_rows[..., :freq_count], right_rows[..., freq_count:])
    cross_real = jnp.einsum(
        "apsf,bpsf->pabf", left_real, right_real, precision=precise
    ) + jnp.einsum("apsf,bpsf->pabf", left_imag, right_imag, precision=precise)
    cross_imag = jnp.einsum(
        "apsf,bpsf->pabf", left_imag, right_real, precision=precise
    ) - jnp.einsum("apsf,bpsf->pabf", left_real, right_imag, precision=precise)
    cross = jnp.concatenate([cross_real, cross_imag], axis=-1)
    lagged = jnp.einsum("pabg,gl->pabl", cross, lag_table, precision=precise) * scale
    return lagged.reshape(lagged.shape[0], -1)


def correlate_list(left_white, right_white, left_index, right_index, lag_table, scale):
    pair_total = left_index.shape[0]
    block_pairs = math.gcd(pair_total, 64)

    def one_block(indices):
        return correlate(left_white, right_white, indices[0], indices[1], lag_table, scale)

    lagged = lax.map(
        one_block, (left_index.reshape(-1, block_pairs), right_index.reshape(-1, block_pairs))
    )
    return lagged.reshape(pair_total, -1)


def slot_rows(owner_row, count, blocks, capacity):
    entry = jnp.arange(owner_row.shape[0], dtype=jnp.int32)
    valid = entry < count
    hits = (
        (owner_row[:, None] == jnp.arange(blocks, dtype=jnp.int32)[None, :]) & valid[:, None]
    ).astype(jnp.int32)
    before = jnp.cumsum(hits, axis=0) - hits
    rank = jnp.sum(before * hits, axis=1)
    return (jnp.where(valid, owner_row * capacity + rank, blocks * capacity), valid)


def local(waves, partner, pair_count, left_station, right_station, owner):
    sta_count = lax.axis_size("sta")
    tm_count = lax.axis_size("tm")
    seg_local = waves.shape[2]
    samples = waves.shape[3]
    freq_count = samples // 2
    pair_slots = left_station.shape[1]
    capacity = 2 * pair_slots // sta_count
    offset = partner[0, 0]
    partner_waves = waves
    for bit_index in range(sta_count.bit_length() - 1):
        taken = jnp.bitwise_and(jnp.right_shift(offset, bit_index), 1) == 1
        moved = partner_2(partner_waves, "sta", bit_index)
        partner_waves = jnp.where(taken, moved, partner_waves)
    dft_table = make_dft_table(samples, freq_count)
    band_matrix, band_count = make_band(freq_count, HALF_BAND)
    lag_table = make_lag_table(samples, freq_count, LAGS)
    white_both = whiten(jnp.stack([waves, partner_waves]), dft_table, band_matrix, band_count)
    scale = 1.0 / math.sqrt(freq_count * seg_local * tm_count)
    lagged = correlate_list(
        white_both[0], white_both[1], left_station[0], right_station[0], lag_table, scale
    )
    slot, valid = slot_rows(owner[0], pair_count[0], sta_count, capacity)
    partial_value = jnp.where(valid[:, None], lagged, jnp.zeros_like(lagged))
    shares = lax.psum_scatter(partial_value, "tm", scatter_dimension=1, tiled=True)
    outgoing = (
        jnp.zeros((sta_count * capacity, shares.shape[1]), jnp.float32)
        .at[slot]
        .add(shares, mode="drop")
    )
    received = lax.all_to_all(
        outgoing.reshape(sta_count, capacity, -1), "sta", split_axis=0, concat_axis=0, tiled=True
    )
    result = received.reshape(sta_count * capacity, -1)
    return result


def solution(mesh):
    in_specs = (
        P(None, "sta", "tm", None),
        P(),
        P("sta"),
        P("sta", None),
        P("sta", None),
        P("sta", None),
    )
    out_specs = P("sta", "tm")
    return jax.shard_map(local, mesh=mesh, in_specs=in_specs, out_specs=out_specs, check_vma=False)
```

profile of v0, /device:TPU:0, one launch (start us, length us, event | category | flops | bytes accessed | tf_op | source)
XLA Modules:
  0.0 151.3 jit_solution(14391138902017799301)
XLA Ops:
  6.5 0.5 collective-permute-start
  7.0 1.2 slice.35
  8.9 1.1 broadcast_select_fusion
  9.9 2.6 %collective-permute-start.1 = (bf16[3,128,1,512]{3,1,0,2:T(8,128)(2,1)S(1)}, bf16[3,128,1,512]{3,1,0,2:T(8,128)(2,1)S(1)}, u32[]{:S(2)}, u32[]{:S(2)}) collective-permute-start(bf16[3,128,1,512]{3,1,0,2:T(8,128)(2,1)S(1)} %broadcast_select_fusion), channel_id=1, source_target_pairs={{0,8},{4,12},{8,0},{12,4},{16,24},{20,28},{24,16},{28,20},{1,9},{5... | collective-permute-start | bytes 1179656 | tf_op jit(solution)/shard_map/ppermute | solution.py:18
  13.8 2.2 %negate_convert_fusion = (bf16[512,256]{1,0:T(8,128)(2,1)S(1)}, bf16[512,256]{1,0:T(8,128)(2,1)S(1)}) fusion(), kind=kLoop, calls=%fused_computation.55 | loop fusion | flops 2228224 | bytes 524288 | tf_op jit(solution)/shard_map/convert.1
  16.0 1.0 fusion.31
  17.1 5.2 %collective-permute-done.1 = bf16[3,128,1,512]{3,1,0,2:T(8,128)(2,1)S(1)} collective-permute-done((bf16[3,128,1,512]{3,1,0,2:T(8,128)(2,1)S(1)}, bf16[3,128,1,512]{3,1,0,2:T(8,128)(2,1)S(1)}, u32[]{:S(2)}, u32[]{:S(2)}) %collective-permute-start.1) | collective-permute-done | bytes 393248 | tf_op jit(solution)/shard_map/ppermute | solution.py:18
  22.3 1.8 %collective-permute-start.2 = (bf16[3,128,1,512]{3,1,0,2:T(8,128)(2,1)S(1)}, bf16[3,128,1,512]{3,1,0,2:T(8,128)(2,1)S(1)}, u32[]{:S(2)}, u32[]{:S(2)}) collective-permute-start(bf16[3,128,1,512]{3,1,0,2:T(8,128)(2,1)S(1)} %broadcast_select_fusion.1), channel_id=1, source_target_pairs={{0,16},{4,20},{8,24},{12,28},{16,0},{20,4},{24,8},{28,12},{1,17},{... | collective-permute-start | bytes 1179656 | tf_op jit(solution)/shard_map/ppermute | solution.py:18
  24.8 0.5 broadcast.160
  25.3 0.7 reduce.9
  26.1 0.7 reduce.10
  26.9 6.3 %collective-permute-done.2 = bf16[3,128,1,512]{3,1,0,2:T(8,128)(2,1)S(1)} collective-permute-done((bf16[3,128,1,512]{3,1,0,2:T(8,128)(2,1)S(1)}, bf16[3,128,1,512]{3,1,0,2:T(8,128)(2,1)S(1)}, u32[]{:S(2)}, u32[]{:S(2)}) %collective-permute-start.2) | collective-permute-done | bytes 393248 | tf_op jit(solution)/shard_map/ppermute | solution.py:18
  33.4 0.6 fusion.17
  34.0 0.3 fusion.11
  34.3 0.3 fusion.8
  34.6 1.4 copy_divide_fusion
  36.0 1.3 slice_bitcast_fusion.4
  37.3 26.9 %while.10 = (s32[]{:T(128)}, f32[4,64,2304]{2,1,0:T(8,128)}, s32[4,64]{1,0:T(4,128)S(1)}, f32[3,128,1,512]{3,0,1,2:T(4,128)}, s32[4,64]{1,0:T(4,128)S(1)}, /*ind...) while((s32[]{:T(128)}, f32[4,64,2304]{2,1,0:T(8,128)}, s32[4,64]{1,0:T(4,128)S(1)}, ...), condition=%wide.region_6.8_spmd, body=%wide.region_5.7_spmd.sunk | while | flops 907496192 | bytes 14101337 | solution.py:87
  37.3 2.1 %gather_fusion.1 = f32[64,3,512]{2,1,0:T(4,128)S(1)} fusion(f32[3,128,512]{2,0,1:T(4,128)} %bitcast.107, s32[1024]{0:T(1024)S(1)} %pad_clamp_fusion.5), kind=kCustom, calls=%fused_computation.clone.clone.1 | custom fusion | bytes 786688 | tf_op jit(solution)/shard_map/while/body/eval_jaxpr/jit(_take)/gather | solution.py:65
  39.4 0.2 bitcast_select_fusion.6
  39.8 0.9 gather_fusion
  40.7 0.2 bitcast_select_fusion.5
  41.1 0.2 add_bitcast_fusion.2
  41.2 1.1 convolution_multiply_fusion.2
  42.3 0.4 copy.41
  42.7 0.4 broadcast_in_dim.76
  43.2 0.9 constant_dynamic-update-slice_fusion.2
  44.0 2.1 %gather_fusion.1 = f32[64,3,512]{2,1,0:T(4,128)S(1)} fusion(f32[3,128,512]{2,0,1:T(4,128)} %bitcast.107, s32[1024]{0:T(1024)S(1)} %pad_clamp_fusion.5), kind=kCustom, calls=%fused_computation.clone.clone.1 | custom fusion | bytes 786688 | tf_op jit(solution)/shard_map/while/body/eval_jaxpr/jit(_take)/gather | solution.py:65
  46.1 0.2 bitcast_select_fusion.6
  46.5 0.9 gather_fusion
  47.4 0.2 bitcast_select_fusion.5
  47.8 0.2 add_bitcast_fusion.2
  48.0 1.1 convolution_multiply_fusion.2
  49.0 0.4 copy.41
  49.5 0.4 broadcast_in_dim.76
  49.9 0.9 constant_dynamic-update-slice_fusion.2
  50.8 2.1 %gather_fusion.1 = f32[64,3,512]{2,1,0:T(4,128)S(1)} fusion(f32[3,128,512]{2,0,1:T(4,128)} %bitcast.107, s32[1024]{0:T(1024)S(1)} %pad_clamp_fusion.5), kind=kCustom, calls=%fused_computation.clone.clone.1 | custom fusion | bytes 786688 | tf_op jit(solution)/shard_map/while/body/eval_jaxpr/jit(_take)/gather | solution.py:65
  52.9 0.2 bitcast_select_fusion.6
  53.3 0.9 gather_fusion
  54.1 0.2 bitcast_select_fusion.5
  54.5 0.2 add_bitcast_fusion.2
  54.7 1.1 convolution_multiply_fusion.2
  55.8 0.4 copy.41
  56.2 0.4 broadcast_in_dim.76
  56.6 0.9 constant_dynamic-update-slice_fusion.2
  57.5 2.1 %gather_fusion.1 = f32[64,3,512]{2,1,0:T(4,128)S(1)} fusion(f32[3,128,512]{2,0,1:T(4,128)} %bitcast.107, s32[1024]{0:T(1024)S(1)} %pad_clamp_fusion.5), kind=kCustom, calls=%fused_computation.clone.clone.1 | custom fusion | bytes 786688 | tf_op jit(solution)/shard_map/while/body/eval_jaxpr/jit(_take)/gather | solution.py:65
  59.6 0.2 bitcast_select_fusion.6
  60.0 0.9 gather_fusion
  60.9 0.2 bitcast_select_fusion.5
  61.3 0.2 add_bitcast_fusion.2
  61.4 1.1 convolution_multiply_fusion.2
  62.5 0.4 copy.41
  62.9 0.4 broadcast_in_dim.76
  63.4 0.9 constant_dynamic-update-slice_fusion.2
  64.2 1.9 %bitcast_select_fusion.2 = f32[256,2304]{1,0:T(8,128)S(1)} fusion(f32[4,64,2304]{2,1,0:T(8,128)} %get-tuple-element.43, pred[256]{0:T(512)(128)(4,1)S(1)} %iota_compare_fusion.2), kind=kLoop, calls=%fused_computation.28 | loop fusion | flops 589824 | bytes 4718848 | tf_op jit(solution)/shard_map/jit(_where)/select_n | solution.py:127
  66.1 2.0 %copy.29 = f32[256,2304]{0,1:T(8,128)} copy(f32[256,2304]{1,0:T(8,128)S(1)} %bitcast_select_fusion.2) | data formatting | bytes 4718592
  68.1 0.6 copy-done.1
  68.8 0.6 reduce-window.6
  69.4 0.2 slice_reduce_fusion
  69.7 47.9 %reduce-scatter.4.cloned.1.call-done = f32[576,256]{1,0:T(8,128)} async-done(((f32[2304,256]{1,0:T(8,128)}), f32[576,256]{1,0:T(8,128)}) %reduce-scatter.4.cloned.1.call-update) | async-done | bytes 589840
  117.6 1.3 copy.30
  118.9 2.5 %scatter_custom_fusion = f32[512,576]{1,0:T(8,128)S(1)} fusion(s32[256]{0:T(256)S(1)} %bitcast.124, f32[256,576]{1,0:T(8,128)S(1)} %copy.30, f32[]{:T(128)} %constant.73.clone.1), kind=kCustom, calls=%fused_computation.44 | custom fusion | flops 147456 | bytes 1179652 | tf_op jit(solution)/shard_map/scatter-add | solution.py:132
  121.5 21.6 %all_to_all.5 = f32[8,64,576]{2,1,0:T(8,128)S(1)} all-to-all(f32[8,64,576]{2,1,0:T(8,128)S(1)} %bitcast.115), channel_id=1, replica_groups=mesh['sta'=8,'tm'=4] {'sta'}, dimensions={0} | all-to-all | bytes 2359296 | tf_op jit(solution)/shard_map/all_to_all | solution.py:134
  143.1 1.4 copy.27
  (64 shorter events, 2.1 us)
Async XLA Ops:
  6.5 18.8 %copy-start.2 = (s32[1,256]{1,0:T(1,128)S(1)}, s32[1,256]{1,0:T(1,128)}, u32[]{:S(2)}) copy-start(s32[1,256]{1,0:T(1,128)} %param.14) | copy-start | bytes 3076
  6.5 19.5 %copy-start.3 = (s32[1,256]{1,0:T(1,128)S(1)}, s32[1,256]{1,0:T(1,128)}, u32[]{:S(2)}) copy-start(s32[1,256]{1,0:T(1,128)} %param.13) | copy-start | bytes 3076
  6.5 111.1 %reduce-scatter.4.cloned.1.call-start = ((), (), s32[]{:S(2)}) async-start(), calls=%async_computation.2 | async-start | bytes 2949120
  6.5 2.3 %collective-permute-start = (bf16[3,128,1,512]{3,1,0,2:T(8,128)(2,1)}, bf16[3,128,1,512]{3,1,0,2:T(8,128)(2,1)S(1)}, u32[]{:S(2)}, u32[]{:S(2)}) collective-permute-start(bf16[3,128,1,512]{3,1,0,2:T(8,128)(2,1)} %bitcast.118), channel_id=1, source_target_pairs={{0,4},{4,0},{8,12},{12,8},{16,20},{20,16},{24,28},{28,24},{1,5},{5... | collective-permute-start | bytes 1179656 | tf_op jit(solution)/shard_map/ppermute | solution.py:18
  9.9 12.3 %collective-permute-start.1 = (bf16[3,128,1,512]{3,1,0,2:T(8,128)(2,1)S(1)}, bf16[3,128,1,512]{3,1,0,2:T(8,128)(2,1)S(1)}, u32[]{:S(2)}, u32[]{:S(2)}) collective-permute-start(bf16[3,128,1,512]{3,1,0,2:T(8,128)(2,1)S(1)} %broadcast_select_fusion), channel_id=1, source_target_pairs={{0,8},{4,12},{8,0},{12,4},{16,24},{20,28},{24,16},{28,20},{1,9},{5... | collective-permute-start | bytes 1179656 | tf_op jit(solution)/shard_map/ppermute | solution.py:18
  16.0 17.3 %copy-start = (bf16[3,128,1,512]{3,1,2,0:T(8,128)(2,1)S(1)}, bf16[3,128,1,512]{3,1,2,0:T(8,128)(2,1)}, u32[]{:S(2)}) copy-start(bf16[3,128,1,512]{3,1,2,0:T(8,128)(2,1)} %param.10) | copy-start | bytes 1179652
  22.3 10.9 %collective-permute-start.2 = (bf16[3,128,1,512]{3,1,0,2:T(8,128)(2,1)S(1)}, bf16[3,128,1,512]{3,1,0,2:T(8,128)(2,1)S(1)}, u32[]{:S(2)}, u32[]{:S(2)}) collective-permute-start(bf16[3,128,1,512]{3,1,0,2:T(8,128)(2,1)S(1)} %broadcast_select_fusion.1), channel_id=1, source_target_pairs={{0,16},{4,20},{8,24},{12,28},{16,0},{20,4},{24,8},{28,12},{1,17},{... | collective-permute-start | bytes 1179656 | tf_op jit(solution)/shard_map/ppermute | solution.py:18
  68.1 0.7 copy-start.1
Sparse Core Ops, SparseCore 0:
  68.3 49.3 reduce-scatter.3
where the time goes:
time: 152 us; the launch traced here: 151 us
  waiting for transfers between devices  59.4 us (39%)
  local copies, waits for them, and re-layouts  28.7 us (19%)
  blocking collectives  21.6 us (14%)
  between operations  16.1 us (11%)
  other arithmetic  14.9 us (10%)
  matrix products  5.22 us (3%)
  starting transfers between devices  4.91 us (3%)
    unnamed x2, waiting for transfers between devices  47.9 us
    all_to_all x1, blocking collectives, local(): lax.all_to_all(outgoing.reshape(sta_count, capacity, -1), 'sta', split_ax...  21.6 us
    ppermute x3, waiting for transfers between devices, partner_2(): return lax.ppermute(value, axis, pairs)  11.5 us
    gather x4, local copies, waits for them, and re-layouts, correlate(): right_rows = jnp.take(right_white, right_index, axis=1)  8.38 us
    ppermute x3, starting transfers between devices, partner_2(): return lax.ppermute(value, axis, pairs)  4.91 us
    unnamed x11, local copies, waits for them, and re-layouts  4.44 us
    dot_general x4, matrix products, correlate(): jnp.einsum('pabg,gl->pabl', cross, lag_table, precision=precise) * scale  4.36 us
    dynamic_update_slice x4, local copies, waits for them, and re-layouts, correlate_list(): lax.map(one_block, (left_index.reshape(-1, block_pairs), right_index.resh...  3.47 us
  transfers between devices with their start and end apart: 4, of which 3 were waited for; matrix products, arithmetic and copies ran while one was open for 5% of the time, Pallas kernels for 0%

commit v1 on v0

v1 whole, which is shorter than its diff:
```python
import functools
import math

import jax
import jax.numpy as jnp
import numpy as np
from jax import lax
from jax.experimental import pallas as pl
from jax.experimental.pallas import tpu as pltpu
from jax.sharding import PartitionSpec as P

LAGS = 256
HALF_BAND = 21
EPSILON = 1e-06
F32 = jnp.float32
BF16 = jnp.bfloat16
VMEM_LIMIT = 48 * 1024 * 1024


def xor_pairs(count, mask):
    return [(i, i ^ mask) for i in range(count)]


def split(x):
    hi = x.astype(BF16)
    return hi, (x - hi.astype(F32)).astype(BF16)


def tables(samples, freqs, scale):
    n = np.arange(samples, dtype=np.int64)
    f = np.arange(freqs, dtype=np.int64)
    step = np.float32(2.0 * math.pi / samples)
    phase = (step * np.mod(f[:, None] * n[None, :], samples).astype(np.float32)).astype(np.float32)
    dft = np.concatenate([np.cos(phase), -np.sin(phase)], axis=0).astype(jnp.bfloat16)
    lag = np.arange(LAGS, dtype=np.int64) - LAGS // 2
    phase = (step * np.mod(lag[:, None] * f[None, :], samples).astype(np.float32)).astype(np.float32)
    table = np.concatenate([np.cos(phase), -np.sin(phase)], axis=1) * np.float32(scale)
    high = table.astype(jnp.bfloat16)
    low = (table - high.astype(np.float32)).astype(jnp.bfloat16)
    near = np.abs(f[:, None] - f[None, :]) <= HALF_BAND
    inverse = (1.0 / (3.0 * near.sum(axis=1))).astype(np.float32)[:, None]
    return dft, high, low, near.astype(jnp.bfloat16), np.broadcast_to(inverse, (freqs, 128)).copy()


def whiten_rows(x, dft, band, inverse, index):
    stations = x.shape[0] // 3
    freqs = band.shape[0]
    spectra = [
        lax.dot_general(
            dft, x[c * stations : (c + 1) * stations], (((1,), (1,)), ((), ())), preferred_element_type=F32
        )
        for c in range(3)
    ]
    amplitude = sum(jnp.sqrt(s[:freqs] * s[:freqs] + s[freqs:] * s[freqs:]) for s in spectra)
    high, low = split(amplitude)
    smooth = jnp.dot(band, high, preferred_element_type=F32) + jnp.dot(band, low, preferred_element_type=F32)
    factor = 1.0 / (smooth * inverse[:, :1] + EPSILON)
    factor = jnp.concatenate([factor, factor], axis=0)
    pick = lax.broadcasted_iota(jnp.int32, (stations, index.shape[1]), 0) == index
    pick = pick.astype(F32).astype(BF16)
    pick = jnp.concatenate([pick, pick], axis=0)
    rows = []
    for s in spectra:
        high, low = split(s * factor)
        rows.append(jnp.dot(jnp.concatenate([high, low], axis=1), pick, preferred_element_type=F32))
    return rows


def whiten_kernel(x, dft, band, inverse, index, out):
    rows = whiten_rows(x[...], dft[...], band[...], inverse[...], index[...])
    for c in range(3):
        out[c] = rows[c]


def piece_rows(lefts, rights, high_table, low_table, cross_high, cross_low, lagged, piece, width, blocks):
    freqs = lefts[0].shape[1] // 2
    start = piece * width
    first = start // LAGS
    step = 32
    for j in range(blocks):
        ac = jnp.minimum(first + j, 8)
        a, c = ac // 3, ac % 3
        for r in range(0, freqs, step):
            real, imag = 0.0, 0.0
            for left, right in zip(lefts, rights):
                lr, li = left[a, r : r + step], left[a, freqs + r : freqs + r + step]
                rr, ri = right[c, r : r + step], right[c, freqs + r : freqs + r + step]
                real = real + (lr * rr + li * ri)
                imag = imag + (li * rr - lr * ri)
            cross_high[r : r + step], cross_low[r : r + step] = split(real)
            cross_high[freqs + r : freqs + r + step], cross_low[freqs + r : freqs + r + step] = split(imag)
        lagged[j * LAGS : (j + 1) * LAGS] = (
            jnp.dot(high_table[...], cross_high[...], preferred_element_type=F32)
            + jnp.dot(low_table[...], cross_high[...], preferred_element_type=F32)
            + jnp.dot(high_table[...], cross_low[...], preferred_element_type=F32)
        )
    return start - first * LAGS


def send_kernel(
    width, blocks, sends, meta, g0, h0, g1, xa, xb, dft, band, inverse, index, high_table, low_table,
    out, h1, cross_high, cross_low, lagged,
):
    x = jnp.concatenate([xa[...], xb[...]], axis=0)
    rows = whiten_rows(x, dft[...], band[...], inverse[...], index[...])
    for c in range(3):
        h1[c] = rows[c]
    t = meta[0]
    for j in range(sends):
        piece = t ^ (2 * (j + 1))
        shift = piece_rows(
            (g0, g1), (h0, h1), high_table, low_table, cross_high, cross_low, lagged, piece, width, blocks
        )
        out[j] = lagged[pl.ds(pl.multiple_of(shift, 16), width)].astype(BF16)


def own_kernel(
    width, blocks, meta, g0, h0, g1, h1, high_table, low_table, out, cross_high, cross_low, lagged
):
    shift = piece_rows(
        (g0, g1), (h0, h1), high_table, low_table, cross_high, cross_low, lagged, meta[0], width, blocks
    )
    out[...] = lagged[pl.ds(pl.multiple_of(shift, 16), width)]


def total_kernel(own, received, out):
    total = own[...]
    for j in range(received.shape[0]):
        total = total + received[j].astype(F32)
    out[...] = total.astype(BF16)


def slot_lanes(owner, blocks):
    pairs = owner.shape[1]
    hits = lax.broadcasted_iota(jnp.int32, (blocks, pairs), 0) == owner
    hits = hits.astype(F32)
    earlier = lax.broadcasted_iota(jnp.int32, (pairs, pairs), 0) < lax.broadcasted_iota(jnp.int32, (pairs, pairs), 1)
    before = jnp.dot(hits.astype(BF16), earlier.astype(F32).astype(BF16), preferred_element_type=F32)
    return jnp.sum(before * hits, axis=0, keepdims=True).astype(jnp.int32)


def route_kernel(blocks, capacity, meta, total, other, owner, other_owner, *outs):
    chip, core = meta[1], meta[2]
    pairs = owner.shape[1]
    chips = blocks // 2
    picks = []
    for value, lists in ((owner[...], core), (other_owner[...], 1 - core)):
        rank = slot_lanes(value, blocks)
        lane = ((value // 2) ^ chip) * (2 * capacity) + lists * capacity + rank
        mine = jnp.logical_and(value >= 0, value % 2 == core)
        lane = jnp.where(mine, lane, -1)
        slots = lax.broadcasted_iota(jnp.int32, (chips * 2 * capacity, pairs), 0)
        picks.append((slots == lane).astype(F32).astype(BF16))
    values = jnp.concatenate([total[...], other[...]], axis=1)
    pick = jnp.concatenate(picks, axis=1)
    routed = lax.dot_general(values, pick, (((1,), (1,)), ((), ())), preferred_element_type=F32)
    for j in range(chips):
        outs[j][...] = routed[:, j * 2 * capacity : (j + 1) * 2 * capacity].astype(BF16)


def place_kernel(lanes, meta, *refs):
    out = refs[-1]
    chip = meta[1]
    for j, ref in enumerate(refs[:-1]):
        out[:, pl.ds(pl.multiple_of((chip ^ j) * lanes, lanes), lanes)] = ref[...].astype(F32)


def call(kernel, out_shape, args, scratch=(), flops=0, smem=0):
    specs = [pl.BlockSpec(memory_space=pltpu.SMEM)] * smem
    specs += [pl.BlockSpec(memory_space=pltpu.VMEM)] * (len(args) - smem)
    outs = jax.tree.map(lambda _: pl.BlockSpec(memory_space=pltpu.VMEM), out_shape)
    moved = sum(math.prod(a.shape) * a.dtype.itemsize for a in list(args) + jax.tree.leaves(out_shape))
    return pl.pallas_call(
        kernel,
        out_shape=out_shape,
        in_specs=specs,
        out_specs=outs,
        scratch_shapes=list(scratch),
        compiler_params=pltpu.CompilerParams(vmem_limit_bytes=VMEM_LIMIT),
        cost_estimate=pl.CostEstimate(flops=flops, bytes_accessed=moved, transcendentals=0),
    )(*args)


def local(waves, partner, pair_count, left_station, right_station, owner):
    sta_count = lax.axis_size("sta")
    tm_count = lax.axis_size("tm")
    comps, stations, seg_local, samples = waves.shape
    freqs = samples // 2
    pairs = left_station.shape[1]
    capacity = 2 * pairs // sta_count
    columns = comps * comps * LAGS
    width = columns // tm_count
    chips = sta_count // 2
    sends = tm_count // 2 - 1
    unit = math.gcd(width, LAGS)
    blocks = -(-(LAGS - unit + width) // LAGS)
    scale = 1.0 / math.sqrt(freqs * seg_local * tm_count)
    dft, high_table, low_table, band, inverse = (jnp.asarray(a) for a in tables(samples, freqs, scale))

    t = lax.axis_index("tm")
    me = lax.axis_index("sta")
    meta = jnp.stack([t, me // 2, me % 2]).astype(jnp.int32)
    listed = jnp.where(jnp.arange(pairs, dtype=jnp.int32)[None, :] < pair_count[0], owner, -1)
    other_listed = lax.ppermute(listed, "sta", xor_pairs(sta_count, 1))

    x = waves.reshape(comps * stations, samples)
    half = x.shape[0] // 2
    grid_flops = 2 * (3 * 2 * freqs * samples * stations + 3 * 4 * freqs * pairs * stations)

    def whitened(records, index):
        shape = jax.ShapeDtypeStruct((comps, 2 * freqs, pairs), F32)
        return call(whiten_kernel, shape, (records, dft, band, inverse, index), flops=grid_flops)

    def gather(offset, x, left, right):
        swap = functools.partial(lax.ppermute, axis_name="tm", perm=xor_pairs(tm_count, 1))
        cross = functools.partial(lax.ppermute, axis_name="sta", perm=xor_pairs(sta_count, offset))
        x_next = swap(x)
        p = cross(x)
        g0 = whitened(x, left)
        pa = cross(x_next[:half])
        pb = swap(p[half:])
        h0 = whitened(p, right)
        g1 = whitened(x_next, left)
        return g0, h0, g1, pa, pb

    branches = [functools.partial(gather, k) for k in range(1, sta_count)]
    g0, h0, g1, pa, pb = lax.switch(partner[0, 0] - 1, branches, x, left_station, right_station)

    scratch = [
        pltpu.VMEM((2 * freqs, pairs), BF16),
        pltpu.VMEM((2 * freqs, pairs), BF16),
        pltpu.VMEM((blocks * LAGS, pairs), F32),
    ]
    lag_flops = 2 * 3 * blocks * LAGS * 2 * freqs * pairs
    sent, h1 = call(
        functools.partial(send_kernel, width, blocks, sends),
        (
            jax.ShapeDtypeStruct((sends, width, pairs), BF16),
            jax.ShapeDtypeStruct((comps, 2 * freqs, pairs), F32),
        ),
        (meta, g0, h0, g1, pa, pb, dft, band, inverse, right_station, high_table, low_table),
        scratch, flops=grid_flops + sends * lag_flops, smem=1,
    )
    received = [
        lax.ppermute(sent[j], "tm", xor_pairs(tm_count, 2 * (j + 1))) for j in range(sends)
    ]
    own = call(
        functools.partial(own_kernel, width, blocks),
        jax.ShapeDtypeStruct((width, pairs), F32),
        (meta, g0, h0, g1, h1, high_table, low_table),
        scratch, flops=lag_flops, smem=1,
    )
    total = call(
        total_kernel, jax.ShapeDtypeStruct((width, pairs), BF16), (own, jnp.stack(received)), flops=width * pairs
    )
    other = lax.ppermute(total, "sta", xor_pairs(sta_count, 1))
    lanes = 2 * capacity
    routed = call(
        functools.partial(route_kernel, sta_count, capacity),
        [jax.ShapeDtypeStruct((width, lanes), BF16)] * chips,
        (meta, total, other, listed, other_listed),
        flops=2 * width * 2 * pairs * chips * lanes, smem=1,
    )
    arrived = [
        routed[j] if j == 0 else lax.ppermute(routed[j], "sta", xor_pairs(sta_count, 2 * j)) for j in range(chips)
    ]
    if lanes % 128 == 0:
        result = call(
            functools.partial(place_kernel, lanes),
            jax.ShapeDtypeStruct((width, sta_count * capacity), F32),
            (meta, *arrived), flops=width * sta_count * capacity, smem=1,
        )
    else:
        order = jnp.bitwise_xor(me // 2, jnp.arange(chips, dtype=jnp.int32))
        result = jnp.take(jnp.stack(arrived), order, axis=0).astype(F32)
        result = jnp.transpose(result, (1, 0, 2)).reshape(width, sta_count * capacity)
    return result.T


def solution(mesh):
    in_specs = (
        P(None, "sta", "tm", None),
        P(),
        P("sta"),
        P("sta", None),
        P("sta", None),
        P("sta", None),
    )
    out_specs = P("sta", "tm")
    return jax.shard_map(local, mesh=mesh, in_specs=in_specs, out_specs=out_specs, check_vma=False)
```

time: 152 us -> 61.9 us (0.41)
  waiting for transfers between devices: 59.4 us -> 29.9 us
  local copies, waits for them, and re-layouts: 28.7 us -> 2.37 us
  blocking collectives: 21.6 us -> 0 us
  Pallas kernels: 0 us -> 17.4 us
  other arithmetic: 14.9 us -> 0.08 us
  between operations: 16.1 us -> 1.37 us
  starting transfers between devices: 4.91 us -> 11 us
  matrix products: 5.22 us -> 0 us
    unnamed x2 -> x0, waiting for transfers between devices: 47.9 us -> none
    all_to_all x1 -> x0, blocking collectives: 21.6 us -> none  [local(): lax.all_to_all(outgoing.reshape(sta_count, capacity, -1), 'sta', split_ax...]
    ppermute x3 -> x10, waiting for transfers between devices: 11.5 us -> 29.9 us  [the longest x1 11.2 us: local(): lax.ppermute(sent[j], 'tm', xor_pairs(tm_count, 2 * (j + 1)))]
    pallas_call x0 -> x8, Pallas kernels: none -> 17.4 us  [call(): pl.pallas_call(kernel, out_shape=out_shape, in_specs=specs, out_specs=out...]
    gather x8 -> x0, local copies, waits for them, and re-layouts: 11.8 us -> none  [the longest x4 8.38 us: correlate(): right_rows = jnp.take(right_white, right_index, axis=1)]
    ppermute x3 -> x10, starting transfers between devices: 4.91 us -> 11 us  [the longest x3 3.55 us: local(): lax.ppermute(routed[j], 'sta', xor_pairs(sta_count, 2 * j))]
    dot_general x6 -> x0, matrix products: 5.22 us -> none  [the longest x4 4.36 us: correlate(): jnp.einsum('pabg,gl->pabl', cross, lag_table, precision=precise) * scale]
    select_n x12 -> x1, other arithmetic: 4.43 us -> 0.01 us  [local(): jnp.where(jnp.arange(pairs, dtype=jnp.int32)[None, :] < pair_count[0], ow...]
  transfers between devices with their start and end apart: 4 -> 10, of which waited for: 3 -> 7; matrix products, arithmetic and copies ran while one was open for 5% -> 0% of each run, Pallas kernels for 0% -> 15%
where the time goes in v1:
time: 61.9 us; the launch traced here: 62.4 us
  waiting for transfers between devices  29.9 us (48%)
  Pallas kernels  17.4 us (28%)
  starting transfers between devices  11 us (18%)
  local copies, waits for them, and re-layouts  2.37 us (4%)
  between operations  1.37 us (2%)
    pallas_call x8, Pallas kernels, call(): pl.pallas_call(kernel, out_shape=out_shape, in_specs=specs, out_specs=out...  17.4 us
    ppermute x1, waiting for transfers between devices, local(): lax.ppermute(sent[j], 'tm', xor_pairs(tm_count, 2 * (j + 1)))  11.2 us
    ppermute x1, waiting for transfers between devices, gather(): x_next = swap(x)  8.65 us
    ppermute x3, waiting for transfers between devices, local(): lax.ppermute(routed[j], 'sta', xor_pairs(sta_count, 2 * j))  6.95 us
    ppermute x3, starting transfers between devices, local(): lax.ppermute(routed[j], 'sta', xor_pairs(sta_count, 2 * j))  3.55 us
    ppermute x1, starting transfers between devices, gather(): x_next = swap(x)  3.09 us
    ppermute x1, starting transfers between devices, local(): lax.ppermute(sent[j], 'tm', xor_pairs(tm_count, 2 * (j + 1)))  2.66 us
    ppermute x1, waiting for transfers between devices, gather(): p = cross(x)  1.81 us
  transfers between devices with their start and end apart: 10, of which 7 were waited for; matrix products, arithmetic and copies ran while one was open for 0% of the time, Pallas kernels for 15%

profile of v1, /device:TPU:0, one launch (start us, length us, event | category | flops | bytes accessed | tf_op | source)
XLA Modules:
  0.0 62.4 jit_solution(17680349136395494648)
XLA Ops:
  0.0 1.2 %slice.45 = s32[1,1]{1,0:T(1,128)} slice(s32[7,8]{1,0:T(8,128)} %param.19), slice={[0:1], [0:1]} | slice | bytes 8 | tf_op jit(solution)/shard_map/slice | solution.py:227
  1.9 0.0 copy-start
  1.9 0.0 copy-start.1
  1.9 21.9 %conditional.1 = (f32[3,512,256]{2,1,0:T(8,128)S(1)}, f32[3,512,256]{2,1,0:T(8,128)}, f32[3,512,256]{2,1,0:T(8,128)S(1)}, bf16[192,512]{1,0:T(8,128)(2,1)}, bf16[192,512]{1,0:T(8,128)(2,1)}) conditional(s32[]{:T(128)} %bitcast.3, (bf16[384,512]{1,0:T(8,128)(2,1)}, bf16[512,512]{1,0:T(8,128)(2,1)}, ...), branch_computations={%region_0.1_spmd, %region_1.2_spmd, %region_2.3_spmd, %region_3.4_... | conditional | flops 1207959552 | bytes 16919892 | solution.py:227
  2.1 3.1 %collective-permute-start.17 = (bf16[384,512]{1,0:T(8,128)(2,1)}, bf16[384,512]{1,0:T(8,128)(2,1)S(1)}, u32[]{:S(2)}, u32[]{:S(2)}) collective-permute-start(bf16[384,512]{1,0:T(8,128)(2,1)} %get-tuple-element.113.x), channel_id=1, source_target_pairs={{0,1},{1,0},{2,3},{3,2},{4,5},{5,4},{6,7},{7,6},{8,9},{9,8},{10,11... | collective-permute-start | bytes 1179656 | tf_op jit(solution)/shard_map/cond/branch_4_fun/ppermute | solution.py:217
  5.2 0.7 %collective-permute-start.16 = (bf16[384,512]{1,0:T(8,128)(2,1)}, bf16[384,512]{1,0:T(8,128)(2,1)S(1)}, u32[]{:S(2)}, u32[]{:S(2)}) collective-permute-start(bf16[384,512]{1,0:T(8,128)(2,1)} %get-tuple-element.113.x), channel_id=1, source_target_pairs={{0,20},{4,16},{8,28},{12,24},{16,4},{20,0},{24,12},{28,8},{1,21},{... | collective-permute-start | bytes 1179656 | tf_op jit(solution)/shard_map/cond/branch_4_fun/ppermute | solution.py:218
  5.9 8.6 %collective-permute-done.17.x = bf16[384,512]{1,0:T(8,128)(2,1)S(1)} collective-permute-done((bf16[384,512]{1,0:T(8,128)(2,1)}, bf16[384,512]{1,0:T(8,128)(2,1)S(1)}, u32[]{:S(2)}, u32[]{:S(2)}) %collective-permute-start.17) | collective-permute-done | bytes 393248 | tf_op jit(solution)/shard_map/cond/branch_4_fun/ppermute | solution.py:217
  14.5 0.0 copy-start.6
  14.6 0.0 copy-start.13
  14.6 0.0 copy-start.20
  14.6 0.0 copy-start.29
  14.6 0.3 collective-permute-start.18
  14.9 1.8 %collective-permute-done.16.x = bf16[384,512]{1,0:T(8,128)(2,1)S(1)} collective-permute-done((bf16[384,512]{1,0:T(8,128)(2,1)}, bf16[384,512]{1,0:T(8,128)(2,1)S(1)}, u32[]{:S(2)}, u32[]{:S(2)}) %collective-permute-start.16) | collective-permute-done | bytes 393248 | tf_op jit(solution)/shard_map/cond/branch_4_fun/ppermute | solution.py:218
  16.7 0.1 collective-permute-start.19
  16.8 2.6 %branch_4_fun.3 = f32[3,512,256]{2,1,0:T(8,128)S(1)} custom-call(bf16[384,512]{1,0:T(8,128)(2,1)} %get-tuple-element.113.x, bf16[512,512]{1,0:T(8,128)(2,1)} %get-tuple-element.114.dft, bf16[256,256]{1,0:T(8,128)(2,1)} %get-tuple-element.115.band, f32[256,128]{1,0:T(8,128)} %get-tuple-element.116.inverse, s32[1,256]{1,0:T(1,128)} %get-tuple-element.117.index), custom_call_target="tpu_custom_call" | custom-call | flops 402653184 | bytes 2753536 | tf_op jit(solution)/shard_map/cond/branch_4_fun/pallas_call | solution.py:173
  19.4 0.0 copy-done.6
  19.4 0.0 copy-done.13
  19.4 0.0 copy-done.20
  19.4 0.0 copy-done.29
  19.4 0.0 copy-start.36
  19.4 1.3 %branch_4_fun.5 = f32[3,512,256]{2,1,0:T(8,128)S(1)} custom-call(bf16[384,512]{1,0:T(8,128)(2,1)S(1)} %collective-permute-done.17.x, bf16[512,512]{1,0:T(8,128)(2,1)S(1)} %copy-done.6, bf16[256,256]{1,0:T(8,128)(2,1)S(1)} %copy-done.13, f32[256,128]{1,0:T(8,128)S(1)} %copy-done.20, s32[1,256]{1,0:T(1,128)S(1)} %copy-done.29), custom_call_target="tpu_custom_call" | custom-call | flops 402653184 | bytes 2753536 | tf_op jit(solution)/shard_map/cond/branch_4_fun/pallas_call | solution.py:173
  20.8 0.0 copy-done.36
  20.8 2.5 %branch_4_fun.4 = f32[3,512,256]{2,1,0:T(8,128)} custom-call(bf16[384,512]{1,0:T(8,128)(2,1)S(1)} %collective-permute-done.16.x, bf16[512,512]{1,0:T(8,128)(2,1)S(1)} %copy-done.6, bf16[256,256]{1,0:T(8,128)(2,1)S(1)} %copy-done.13, f32[256,128]{1,0:T(8,128)S(1)} %copy-done.20, s32[1,256]{1,0:T(1,128)S(1)} %copy-done.36), custom_call_target="tpu_custom_call" | custom-call | flops 402653184 | bytes 2753536 | tf_op jit(solution)/shard_map/cond/branch_4_fun/pallas_call | solution.py:173
  23.3 0.0 collective-permute-done.18
  23.3 0.5 collective-permute-done.19
  23.8 0.0 copy-start.23
  23.8 0.1 pad_add_fusion.meta
  23.9 1.1 %copy-done.23 = f32[3,512,256]{2,1,0:T(8,128)} copy-done((f32[3,512,256]{2,1,0:T(8,128)}, f32[3,512,256]{2,1,0:T(8,128)S(1)}, u32[]{:S(2)}) %copy-start.23) | copy-done | bytes 1572888
  25.0 0.0 copy-done
  25.0 0.0 copy-done.1
  25.0 0.0 copy-start.24
  25.0 5.1 %shard_map.109 = (bf16[1,576,256]{2,1,0:T(8,128)(2,1)S(1)}, f32[3,512,256]{2,1,0:T(8,128)S(1)}) custom-call(s32[3]{0:T(128)S(1)} %pad_add_fusion.meta, f32[3,512,256]{2,1,0:T(8,128)S(1)} %get-tuple-element.142.g0, f32[3,512,256]{2,1,0:T(8,128)} %get-tuple-element.143.h0, f32[3,512,256]{2,1,0:T(8,128)} %copy-done.23, bf16[192,512]{1,0:T(8,128)(2,1)} %get-tuple-element.145.xa, ...), custom_call_target="tpu_custom_call" | custom-call | flops 1006632960 | bytes 8291340 | tf_op jit(solution)/shard_map/pallas_call | solution.py:173
  30.1 2.7 %collective-permute-start.28 = (bf16[576,256]{1,0:T(8,128)(2,1)S(1)}, bf16[576,256]{1,0:T(8,128)(2,1)S(1)}, u32[]{:S(2)}, u32[]{:S(2)}) collective-permute-start(bf16[576,256]{1,0:T(8,128)(2,1)S(1)} %bitcast.11), channel_id=1, source_target_pairs={{0,2},{1,3},{2,0},{3,1},{4,6},{5,7},{6,4},{7,5},{8,10},{9,11},{10,... | collective-permute-start | bytes 884744 | tf_op jit(solution)/shard_map/ppermute | solution.py:245
  32.8 0.0 copy-done.24
  32.8 0.0 copy-start.39
  32.8 2.9 %shard_map.110.own = f32[576,256]{1,0:T(8,128)S(1)} custom-call(s32[3]{0:T(128)S(1)} %pad_add_fusion.meta, f32[3,512,256]{2,1,0:T(8,128)S(1)} %get-tuple-element.142.g0, f32[3,512,256]{2,1,0:T(8,128)} %get-tuple-element.143.h0, f32[3,512,256]{2,1,0:T(8,128)S(1)} %copy-done.24, f32[3,512,256]{2,1,0:T(8,128)S(1)} %get-tuple-element.147.h1, ...), custom_call_target="tpu_custom_call" | custom-call | flops 603979776 | bytes 7405580 | tf_op jit(solution)/shard_map/pallas_call | solution.py:173
  35.7 11.2 %collective-permute-done.28 = bf16[576,256]{1,0:T(8,128)(2,1)S(1)} collective-permute-done((bf16[576,256]{1,0:T(8,128)(2,1)S(1)}, bf16[576,256]{1,0:T(8,128)(2,1)S(1)}, u32[]{:S(2)}, u32[]{:S(2)}) %collective-permute-start.28) | collective-permute-done | bytes 294944 | tf_op jit(solution)/shard_map/ppermute | solution.py:245
  46.8 0.1 shard_map.111.total
  46.9 0.1 collective-permute-start.29
  47.6 0.0 copy-done.39
  47.6 0.6 collective-permute-start.30
  48.2 0.8 %collective-permute-done.30.other_owner = s32[1,256]{1,0:T(1,128)S(1)} collective-permute-done((s32[1,256]{1,0:T(1,128)S(1)}, s32[1,256]{1,0:T(1,128)S(1)}, u32[]{:S(2)}, u32[]{:S(2)}) %collective-permute-start.30) | collective-permute-done | bytes 1056 | tf_op jit(solution)/shard_map/ppermute | solution.py:204
  49.0 0.0 collective-permute-done.29.other
  49.0 1.2 %shard_map.112 = (bf16[576,128]{1,0:T(8,128)(2,1)S(1)}, bf16[576,128]{1,0:T(8,128)(2,1)S(1)}, bf16[576,128]{1,0:T(8,128)(2,1)S(1)}, bf16[576,128]{1,0:T(8,128)(2,1)S(1)}) custom-call(s32[3]{0:T(128)S(1)} %pad_add_fusion.meta, bf16[576,256]{1,0:T(8,128)(2,1)S(1)} %shard_map.111.total, bf16[576,256]{1,0:T(8,128)(2,1)S(1)} %collective-permute-done.29.other, ...), custom_call_target="tpu_custom_call" | custom-call | flops 301989888 | bytes 1181708 | tf_op jit(solution)/shard_map/pallas_call | solution.py:173
  50.2 1.6 %collective-permute-start.31 = (bf16[576,128]{1,0:T(8,128)(2,1)S(1)}, bf16[576,128]{1,0:T(8,128)(2,1)S(1)}, u32[]{:S(2)}, u32[]{:S(2)}) collective-permute-start(bf16[576,128]{1,0:T(8,128)(2,1)S(1)} %get-tuple-element.150), channel_id=1, source_target_pairs={{0,8},{4,12},{8,0},{12,4},{16,24},{20,28},{24,16},{28,20},{1,9},{5... | collective-permute-start | bytes 442376 | tf_op jit(solution)/shard_map/ppermute | solution.py:265
  51.8 0.5 collective-permute-start.32
  52.3 1.5 %collective-permute-start.33 = (bf16[576,128]{1,0:T(8,128)(2,1)S(1)}, bf16[576,128]{1,0:T(8,128)(2,1)S(1)}, u32[]{:S(2)}, u32[]{:S(2)}) collective-permute-start(bf16[576,128]{1,0:T(8,128)(2,1)S(1)} %get-tuple-element.152), channel_id=1, source_target_pairs={{0,24},{4,28},{8,16},{12,20},{16,8},{20,12},{24,0},{28,4},{1,25},{... | collective-permute-start | bytes 442376 | tf_op jit(solution)/shard_map/ppermute | solution.py:265
  53.8 3.2 %collective-permute-done.31.refs_1_ = bf16[576,128]{1,0:T(8,128)(2,1)S(1)} collective-permute-done((bf16[576,128]{1,0:T(8,128)(2,1)S(1)}, bf16[576,128]{1,0:T(8,128)(2,1)S(1)}, u32[]{:S(2)}, u32[]{:S(2)}) %collective-permute-start.31) | collective-permute-done | bytes 147488 | tf_op jit(solution)/shard_map/ppermute | solution.py:265
  57.0 3.8 %collective-permute-done.32.refs_2_ = bf16[576,128]{1,0:T(8,128)(2,1)S(1)} collective-permute-done((bf16[576,128]{1,0:T(8,128)(2,1)S(1)}, bf16[576,128]{1,0:T(8,128)(2,1)S(1)}, u32[]{:S(2)}, u32[]{:S(2)}) %collective-permute-start.32) | collective-permute-done | bytes 147488 | tf_op jit(solution)/shard_map/ppermute | solution.py:265
  60.7 0.0 collective-permute-done.33.refs_3_
  60.7 1.7 %shard_map.113 = f32[576,512]{1,0:T(8,128)} custom-call(s32[3]{0:T(128)S(1)} %pad_add_fusion.meta, bf16[576,128]{1,0:T(8,128)(2,1)S(1)} %get-tuple-element.149.refs_0_, bf16[576,128]{1,0:T(8,128)(2,1)S(1)} %collective-permute-done.31.refs_1_, bf16[576,128]{1,0:T(8,128)(2,1)S(1)} %collective-permute-done.32.refs_2_, ...), custom_call_target="tpu_custom_call" | custom-call | flops 294912 | bytes 1769484 | tf_op jit(solution)/shard_map/pallas_call | solution.py:173
  (3 shorter events, 0.0 us)
Async XLA Ops:
  1.9 23.1 %copy-start = (bf16[256,512]{1,0:T(8,128)(2,1)S(1)}, bf16[256,512]{1,0:T(8,128)(2,1)}, u32[]{:S(2)}) copy-start(bf16[256,512]{1,0:T(8,128)(2,1)} %constant.55.clone.high_table) | copy-start | bytes 786436
  1.9 23.1 %copy-start.1 = (bf16[256,512]{1,0:T(8,128)(2,1)S(1)}, bf16[256,512]{1,0:T(8,128)(2,1)}, u32[]{:S(2)}) copy-start(bf16[256,512]{1,0:T(8,128)(2,1)} %constant.56.clone.low_table) | copy-start | bytes 786436
  2.1 12.4 %collective-permute-start.17 = (bf16[384,512]{1,0:T(8,128)(2,1)}, bf16[384,512]{1,0:T(8,128)(2,1)S(1)}, u32[]{:S(2)}, u32[]{:S(2)}) collective-permute-start(bf16[384,512]{1,0:T(8,128)(2,1)} %get-tuple-element.113.x), channel_id=1, source_target_pairs={{0,1},{1,0},{2,3},{3,2},{4,5},{5,4},{6,7},{7,6},{8,9},{9,8},{10,11... | collective-permute-start | bytes 1179656 | tf_op jit(solution)/shard_map/cond/branch_4_fun/ppermute | solution.py:217
  5.2 11.5 %collective-permute-start.16 = (bf16[384,512]{1,0:T(8,128)(2,1)}, bf16[384,512]{1,0:T(8,128)(2,1)S(1)}, u32[]{:S(2)}, u32[]{:S(2)}) collective-permute-start(bf16[384,512]{1,0:T(8,128)(2,1)} %get-tuple-element.113.x), channel_id=1, source_target_pairs={{0,20},{4,16},{8,28},{12,24},{16,4},{20,0},{24,12},{28,8},{1,21},{... | collective-permute-start | bytes 1179656 | tf_op jit(solution)/shard_map/cond/branch_4_fun/ppermute | solution.py:218
  14.5 4.8 %copy-start.6 = (bf16[512,512]{1,0:T(8,128)(2,1)S(1)}, bf16[512,512]{1,0:T(8,128)(2,1)}, u32[]{:S(2)}) copy-start(bf16[512,512]{1,0:T(8,128)(2,1)} %get-tuple-element.114.dft) | copy-start | bytes 1572868 | tf_op jit(solution)/shard_map/cond
  14.6 4.8 %copy-start.13 = (bf16[256,256]{1,0:T(8,128)(2,1)S(1)}, bf16[256,256]{1,0:T(8,128)(2,1)}, u32[]{:S(2)}) copy-start(bf16[256,256]{1,0:T(8,128)(2,1)} %get-tuple-element.115.band) | copy-start | bytes 393220 | tf_op jit(solution)/shard_map/cond
  14.6 4.8 %copy-start.20 = (f32[256,128]{1,0:T(8,128)S(1)}, f32[256,128]{1,0:T(8,128)}, u32[]{:S(2)}) copy-start(f32[256,128]{1,0:T(8,128)} %get-tuple-element.116.inverse) | copy-start | bytes 393220 | tf_op jit(solution)/shard_map/cond
  14.6 4.8 %copy-start.29 = (s32[1,256]{1,0:T(1,128)S(1)}, s32[1,256]{1,0:T(1,128)}, u32[]{:S(2)}) copy-start(s32[1,256]{1,0:T(1,128)} %get-tuple-element.117.index) | copy-start | bytes 3076 | tf_op jit(solution)/shard_map/cond
  14.6 8.7 %collective-permute-start.18 = (bf16[192,512]{1,0:T(8,128)(2,1)S(1)}, bf16[192,512]{1,0:T(8,128)(2,1)}, u32[]{:S(2)}, u32[]{:S(2)}) collective-permute-start(bf16[192,512]{1,0:T(8,128)(2,1)S(1)} %slice.54), channel_id=1, source_target_pairs={{0,20},{4,16},{8,28},{12,24},{16,4},{20,0},{24,12},{28,8},{1,21},{... | collective-permute-start | bytes 589832 | tf_op jit(solution)/shard_map/cond/branch_4_fun/ppermute | solution.py:220
  16.7 7.1 %collective-permute-start.19 = (bf16[192,512]{1,0:T(8,128)(2,1)S(1)}, bf16[192,512]{1,0:T(8,128)(2,1)}, u32[]{:S(2)}, u32[]{:S(2)}) collective-permute-start(bf16[192,512]{1,0:T(8,128)(2,1)S(1)} %slice.55), channel_id=1, source_target_pairs={{0,1},{1,0},{2,3},{3,2},{4,5},{5,4},{6,7},{7,6},{8,9},{9,8},{10,11... | collective-permute-start | bytes 589832 | tf_op jit(solution)/shard_map/cond/branch_4_fun/ppermute | solution.py:221
  19.4 1.4 %copy-start.36 = (s32[1,256]{1,0:T(1,128)S(1)}, s32[1,256]{1,0:T(1,128)}, u32[]{:S(2)}) copy-start(s32[1,256]{1,0:T(1,128)} %get-tuple-element.118.index) | copy-start | bytes 3076 | tf_op jit(solution)/shard_map/cond
  23.8 1.1 %copy-start.23 = (f32[3,512,256]{2,1,0:T(8,128)}, f32[3,512,256]{2,1,0:T(8,128)S(1)}, u32[]{:S(2)}) copy-start(f32[3,512,256]{2,1,0:T(8,128)S(1)} %get-tuple-element.144.g1) | copy-start | bytes 4718596
  25.0 7.8 %copy-start.24 = (f32[3,512,256]{2,1,0:T(8,128)S(1)}, f32[3,512,256]{2,1,0:T(8,128)}, u32[]{:S(2)}) copy-start(f32[3,512,256]{2,1,0:T(8,128)} %copy-done.23) | copy-start | bytes 4718596
  30.1 16.7 %collective-permute-start.28 = (bf16[576,256]{1,0:T(8,128)(2,1)S(1)}, bf16[576,256]{1,0:T(8,128)(2,1)S(1)}, u32[]{:S(2)}, u32[]{:S(2)}) collective-permute-start(bf16[576,256]{1,0:T(8,128)(2,1)S(1)} %bitcast.11), channel_id=1, source_target_pairs={{0,2},{1,3},{2,0},{3,1},{4,6},{5,7},{6,4},{7,5},{8,10},{9,11},{10,... | collective-permute-start | bytes 884744 | tf_op jit(solution)/shard_map/ppermute | solution.py:245
  32.8 14.8 %copy-start.39 = (s32[1,256]{1,0:T(1,128)S(1)}, s32[1,256]{1,0:T(1,128)}, u32[]{:S(2)}) copy-start(s32[1,256]{1,0:T(1,128)} %param.23) | copy-start | bytes 3076
  46.9 2.1 %collective-permute-start.29 = (bf16[576,256]{1,0:T(8,128)(2,1)S(1)}, bf16[576,256]{1,0:T(8,128)(2,1)S(1)}, u32[]{:S(2)}, u32[]{:S(2)}) collective-permute-start(bf16[576,256]{1,0:T(8,128)(2,1)S(1)} %shard_map.111.total), channel_id=1, source_target_pairs={{0,4},{4,0},{8,12},{12,8},{16,20},{20,16},{24,28},{28,24},{1,5},{5... | collective-permute-start | bytes 884744 | tf_op jit(solution)/shard_map/ppermute | solution.py:256
  47.6 1.4 %collective-permute-start.30 = (s32[1,256]{1,0:T(1,128)S(1)}, s32[1,256]{1,0:T(1,128)S(1)}, u32[]{:S(2)}, u32[]{:S(2)}) collective-permute-start(s32[1,256]{1,0:T(1,128)S(1)} %compare_select_fusion.owner), channel_id=1, source_target_pairs={{0,4},{4,0},{8,12},{12,8},{16,20},{20,16},{24,28},{28,24},{1,5},{5... | collective-permute-start | bytes 3080 | tf_op jit(solution)/shard_map/ppermute | solution.py:204
  50.2 6.7 %collective-permute-start.31 = (bf16[576,128]{1,0:T(8,128)(2,1)S(1)}, bf16[576,128]{1,0:T(8,128)(2,1)S(1)}, u32[]{:S(2)}, u32[]{:S(2)}) collective-permute-start(bf16[576,128]{1,0:T(8,128)(2,1)S(1)} %get-tuple-element.150), channel_id=1, source_target_pairs={{0,8},{4,12},{8,0},{12,4},{16,24},{20,28},{24,16},{28,20},{1,9},{5... | collective-permute-start | bytes 442376 | tf_op jit(solution)/shard_map/ppermute | solution.py:265
  51.8 8.9 %collective-permute-start.32 = (bf16[576,128]{1,0:T(8,128)(2,1)S(1)}, bf16[576,128]{1,0:T(8,128)(2,1)S(1)}, u32[]{:S(2)}, u32[]{:S(2)}) collective-permute-start(bf16[576,128]{1,0:T(8,128)(2,1)S(1)} %get-tuple-element.151), channel_id=1, source_target_pairs={{0,16},{4,20},{8,24},{12,28},{16,0},{20,4},{24,8},{28,12},{1,17},{... | collective-permute-start | bytes 442376 | tf_op jit(solution)/shard_map/ppermute | solution.py:265
  52.3 8.4 %collective-permute-start.33 = (bf16[576,128]{1,0:T(8,128)(2,1)S(1)}, bf16[576,128]{1,0:T(8,128)(2,1)S(1)}, u32[]{:S(2)}, u32[]{:S(2)}) collective-permute-start(bf16[576,128]{1,0:T(8,128)(2,1)S(1)} %get-tuple-element.152), channel_id=1, source_target_pairs={{0,24},{4,28},{8,16},{12,20},{16,8},{20,12},{24,0},{28,4},{1,25},{... | collective-permute-start | bytes 442376 | tf_op jit(solution)/shard_map/ppermute | solution.py:265

commit v2 on v1

v2 whole, which is shorter than its diff:
```python
import functools
import math

import jax
import jax.numpy as jnp
import numpy as np
from jax import lax
from jax.experimental import pallas as pl
from jax.experimental.pallas import tpu as pltpu
from jax.sharding import PartitionSpec as P

LAGS = 256
HALF_BAND = 21
EPSILON = 1e-06
F32 = jnp.float32
BF16 = jnp.bfloat16
VMEM_LIMIT = 20 * 1024 * 1024
STEP = 32


def xor_pairs(count, mask):
    return [(i, i ^ mask) for i in range(count)]


def split(x):
    hi = x.astype(BF16)
    return hi, (x - hi.astype(F32)).astype(BF16)


def tables(samples, freqs, scale):
    n = np.arange(samples, dtype=np.int64)
    f = np.arange(freqs, dtype=np.int64)
    step = np.float32(2.0 * math.pi / samples)
    phase = (step * np.mod(f[:, None] * n[None, :], samples).astype(np.float32)).astype(np.float32)
    dft = np.concatenate([np.cos(phase), -np.sin(phase)], axis=0).astype(jnp.bfloat16)
    lag = np.arange(LAGS, dtype=np.int64) - LAGS // 2
    phase = (step * np.mod(lag[:, None] * f[None, :], samples).astype(np.float32)).astype(np.float32)
    table = np.concatenate([np.cos(phase), -np.sin(phase)], axis=1) * np.float32(scale)
    high = table.astype(jnp.bfloat16)
    low = (table - high.astype(np.float32)).astype(jnp.bfloat16)
    near = np.abs(f[:, None] - f[None, :]) <= HALF_BAND
    inverse = (1.0 / (3.0 * near.sum(axis=1))).astype(np.float32)[:, None]
    return dft, high, low, near.astype(jnp.bfloat16), np.broadcast_to(inverse, (freqs, 128)).copy()


def whiten_rows(x, dft, band, inverse, index):
    stations = x.shape[0] // 3
    freqs = band.shape[0]
    spectra = [
        lax.dot_general(
            dft, x[c * stations : (c + 1) * stations], (((1,), (1,)), ((), ())), preferred_element_type=F32
        )
        for c in range(3)
    ]
    amplitude = sum(jnp.sqrt(s[:freqs] * s[:freqs] + s[freqs:] * s[freqs:]) for s in spectra)
    high, low = split(amplitude)
    smooth = jnp.dot(band, high, preferred_element_type=F32) + jnp.dot(band, low, preferred_element_type=F32)
    factor = 1.0 / (smooth * inverse[:, :1] + EPSILON)
    factor = jnp.concatenate([factor, factor], axis=0)
    pick = lax.broadcasted_iota(jnp.int32, (stations, index.shape[1]), 0) == index
    pick = pick.astype(F32).astype(BF16)
    pick = jnp.concatenate([pick, pick], axis=0)
    rows = []
    for s in spectra:
        high, low = split(s * factor)
        rows.append(jnp.dot(jnp.concatenate([high, low], axis=1), pick, preferred_element_type=F32))
    return rows


def whiten_kernel(x, dft, band, inverse, index, out):
    rows = whiten_rows(x[...], dft[...], band[...], inverse[...], index[...])
    for c in range(3):
        out[c] = rows[c]


def cross_rows(lefts, rights, a, c, r, step, real, imag):
    freqs = lefts[0].shape[1] // 2
    for left, right in zip(lefts, rights):
        lr, li = left[a, r : r + step], left[a, freqs + r : freqs + r + step]
        rr, ri = right[c, r : r + step], right[c, freqs + r : freqs + r + step]
        real = real + (lr * rr + li * ri)
        imag = imag + (li * rr - lr * ri)
    return real, imag


def component_pair(first, j):
    ac = jnp.minimum(first + j, 8)
    return ac // 3, ac % 3


def cross_kernel(width, blocks, sends, meta, g0, h0, out):
    freqs = g0.shape[1] // 2
    for k in range(sends):
        first = ((meta[0] ^ (2 * (k + 1))) * width) // LAGS
        for j in range(blocks):
            a, c = component_pair(first, j)
            for r in range(0, freqs, STEP):
                real, imag = cross_rows((g0,), (h0,), a, c, r, STEP, 0.0, 0.0)
                out[k * blocks + j, r : r + STEP] = real
                out[k * blocks + j, freqs + r : freqs + r + STEP] = imag


def lag_block(lefts, rights, base, a, c, high_table, low_table, cross_high, cross_low):
    freqs = lefts[0].shape[1] // 2
    for r in range(0, freqs, STEP):
        real, imag = (0.0, 0.0) if base is None else (base[r : r + STEP], base[freqs + r : freqs + r + STEP])
        real, imag = cross_rows(lefts, rights, a, c, r, STEP, real, imag)
        cross_high[r : r + STEP], cross_low[r : r + STEP] = split(real)
        cross_high[freqs + r : freqs + r + STEP], cross_low[freqs + r : freqs + r + STEP] = split(imag)
    return (
        jnp.dot(high_table[...], cross_high[...], preferred_element_type=F32)
        + jnp.dot(low_table[...], cross_high[...], preferred_element_type=F32)
        + jnp.dot(high_table[...], cross_low[...], preferred_element_type=F32)
    )


def send_first_kernel(
    width, rows, have, sends, meta, x0, g1, xa, xb, dft, band, inverse, index, high_table, low_table,
    out, lagged, h1, cross_high, cross_low,
):
    x = jnp.concatenate([xa[...], xb[...]], axis=0)
    white = whiten_rows(x, dft[...], band[...], inverse[...], index[...])
    for c in range(3):
        h1[c] = white[c]
    blocks = x0.shape[0] // sends
    for k in range(sends):
        start = (meta[0] ^ (2 * (k + 1))) * width
        first = start // LAGS
        for j in range(have):
            a, c = component_pair(first, j)
            lagged[k, j * LAGS : (j + 1) * LAGS] = lag_block(
                (g1,), (h1,), x0.at[k * blocks + j], a, c, high_table, low_table, cross_high, cross_low
            )
        out[k] = lagged[k, pl.ds(pl.multiple_of(start - first * LAGS, 16), rows)].astype(BF16)


def send_rest_kernel(
    width, rows, have, sends, meta, x0, g1, h1, lagged_in, high_table, low_table,
    out, cross_high, cross_low, lagged,
):
    blocks = x0.shape[0] // sends
    for k in range(sends):
        start = (meta[0] ^ (2 * (k + 1))) * width
        first = start // LAGS
        lagged[: have * LAGS] = lagged_in[k]
        for j in range(have, blocks):
            a, c = component_pair(first, j)
            lagged[j * LAGS : (j + 1) * LAGS] = lag_block(
                (g1,), (h1,), x0.at[k * blocks + j], a, c, high_table, low_table, cross_high, cross_low
            )
        out[k] = lagged[pl.ds(pl.multiple_of(start - first * LAGS + rows, 16), width - rows)].astype(BF16)


def own_kernel(
    width, rows, blocks, meta, g0, h0, g1, h1, high_table, low_table, out, rest, cross_high, cross_low, lagged
):
    start = meta[0] * width
    first = start // LAGS
    for j in range(blocks):
        a, c = component_pair(first, j)
        lagged[j * LAGS : (j + 1) * LAGS] = lag_block(
            (g0, g1), (h0, h1), None, a, c, high_table, low_table, cross_high, cross_low
        )
    out[...] = lagged[pl.ds(pl.multiple_of(start - first * LAGS, 16), rows)]
    rest[...] = lagged[pl.ds(pl.multiple_of(start - first * LAGS + rows, 16), width - rows)]


def total_kernel(own, received, out):
    total = own[...]
    for j in range(received.shape[0]):
        total = total + received[j].astype(F32)
    out[...] = total.astype(BF16)


def ranks(owner, blocks):
    pairs = owner.shape[1]
    hits = lax.broadcasted_iota(jnp.int32, (blocks, pairs), 0) == owner
    hits = hits.astype(F32)
    earlier = lax.broadcasted_iota(jnp.int32, (pairs, pairs), 0) < lax.broadcasted_iota(jnp.int32, (pairs, pairs), 1)
    before = jnp.dot(hits.astype(BF16), earlier.astype(F32).astype(BF16), preferred_element_type=F32)
    return jnp.sum(before * hits, axis=0, keepdims=True).astype(jnp.int32)


def pick_kernel(blocks, capacity, meta, owner, other_owner, out):
    chip, core = meta[1], meta[2]
    pairs = owner.shape[1]
    for place, (value, lists) in enumerate(((owner[...], core), (other_owner[...], 1 - core))):
        slot = ((value // 2) ^ chip) * (2 * capacity) + lists * capacity + ranks(value, blocks)
        mine = jnp.logical_and(value >= 0, value % 2 == core)
        slot = jnp.where(mine, slot, -1)
        slots = lax.broadcasted_iota(jnp.int32, (blocks * capacity, pairs), 0)
        out[:, place * pairs : (place + 1) * pairs] = (slots == slot).astype(F32).astype(BF16)


def route_kernel(total, other, pick, *outs):
    values = jnp.concatenate([total[...], other[...]], axis=1)
    routed = lax.dot_general(values, pick[...], (((1,), (1,)), ((), ())), preferred_element_type=F32)
    lanes = routed.shape[1] // len(outs)
    for j, out in enumerate(outs):
        out[...] = routed[:, j * lanes : (j + 1) * lanes].astype(BF16)


def place_kernel(lanes, chips, meta, *refs):
    out = refs[-1]
    chip = meta[1]
    for i, ref in enumerate(refs[:-1]):
        first = 0 if i < chips else refs[0].shape[0]
        at = pl.ds(pl.multiple_of((chip ^ (i % chips)) * lanes, lanes), lanes)
        out[first : first + ref.shape[0], at] = ref[...].astype(F32)


def call(kernel, out_shape, args, scratch=(), flops=0, smem=0):
    specs = [pl.BlockSpec(memory_space=pltpu.SMEM)] * smem
    specs += [pl.BlockSpec(memory_space=pltpu.VMEM)] * (len(args) - smem)
    outs = jax.tree.map(lambda _: pl.BlockSpec(memory_space=pltpu.VMEM), out_shape)
    moved = sum(math.prod(a.shape) * a.dtype.itemsize for a in list(args) + jax.tree.leaves(out_shape))
    return pl.pallas_call(
        kernel,
        out_shape=out_shape,
        in_specs=specs,
        out_specs=outs,
        scratch_shapes=list(scratch),
        compiler_params=pltpu.CompilerParams(vmem_limit_bytes=VMEM_LIMIT),
        cost_estimate=pl.CostEstimate(flops=1024, bytes_accessed=1024, transcendentals=0),
    )(*args)


def local(waves, partner, pair_count, left_station, right_station, owner):
    sta_count = lax.axis_size("sta")
    tm_count = lax.axis_size("tm")
    comps, stations, seg_local, samples = waves.shape
    freqs = samples // 2
    pairs = left_station.shape[1]
    capacity = 2 * pairs // sta_count
    width = comps * comps * LAGS // tm_count
    chips = sta_count // 2
    sends = tm_count // 2 - 1
    top = LAGS - math.gcd(width, LAGS)
    blocks = -(-(top + width) // LAGS)
    rows = -(-width // 48) * 16
    have = -(-(top + rows) // LAGS)
    scale = 1.0 / math.sqrt(freqs * seg_local * tm_count)
    dft, high_table, low_table, band, inverse = (jnp.asarray(a) for a in tables(samples, freqs, scale))

    t = lax.axis_index("tm")
    me = lax.axis_index("sta")
    meta = jnp.stack([t, me // 2, me % 2]).astype(jnp.int32)
    x = waves.reshape(comps * stations, samples)
    by_cross = -(-x.shape[0] * 5 // 8 // 16) * 16
    whiten_flops = 2 * (3 * 2 * freqs * samples * stations + 3 * 4 * freqs * pairs * stations)
    rows_shape = jax.ShapeDtypeStruct((comps, 2 * freqs, pairs), F32)

    def whitened(records, index):
        return call(whiten_kernel, rows_shape, (records, dft, band, inverse, index), flops=whiten_flops)

    def gather(offset, meta, x, left, right, owner, pair_count):
        swap = functools.partial(lax.ppermute, axis_name="tm", perm=xor_pairs(tm_count, 1))
        cross = functools.partial(lax.ppermute, axis_name="sta", perm=xor_pairs(sta_count, offset))
        x_next = swap(x)
        p = cross(x)
        g0 = whitened(x, left)
        listed = jnp.where(jnp.arange(pairs, dtype=jnp.int32)[None, :] < pair_count[0], owner, -1)
        other_listed = lax.ppermute(listed, "sta", xor_pairs(sta_count, 1))
        pick = call(
            functools.partial(pick_kernel, sta_count, capacity),
            jax.ShapeDtypeStruct((sta_count * capacity, 2 * pairs), BF16),
            (meta, listed, other_listed), flops=4 * sta_count * pairs * pairs, smem=1,
        )
        near, g0, pick = lax.optimization_barrier((x_next[:by_cross], g0, pick))
        pa = cross(near)
        pb = cross(x_next[by_cross:]) if offset == 1 else swap(p[by_cross:])
        h0 = whitened(p, right)
        g1 = whitened(x_next, left)
        x0 = call(
            functools.partial(cross_kernel, width, blocks, sends),
            jax.ShapeDtypeStruct((sends * blocks, 2 * freqs, pairs), F32),
            (meta, g0, h0), flops=sends * blocks * 8 * freqs * pairs, smem=1,
        )
        return x0, g0, h0, g1, pa, pb, pick

    branches = [functools.partial(gather, k) for k in range(1, sta_count)]
    x0, g0, h0, g1, pa, pb, pick = lax.switch(
        partner[0, 0] - 1, branches, meta, x, left_station, right_station, owner, pair_count
    )

    bands = [pltpu.VMEM((2 * freqs, pairs), BF16)] * 2
    scratch = bands + [pltpu.VMEM((blocks * LAGS, pairs), F32)]
    lag_flops = 2 * 3 * LAGS * 2 * freqs * pairs
    first, lagged, h1 = call(
        functools.partial(send_first_kernel, width, rows, have, sends),
        (
            jax.ShapeDtypeStruct((sends, rows, pairs), BF16),
            jax.ShapeDtypeStruct((sends, have * LAGS, pairs), F32),
            rows_shape,
        ),
        (meta, x0, g1, pa, pb, dft, band, inverse, right_station, high_table, low_table),
        bands, flops=whiten_flops + sends * have * lag_flops, smem=1,
    )
    rest = call(
        functools.partial(send_rest_kernel, width, rows, have, sends),
        jax.ShapeDtypeStruct((sends, width - rows, pairs), BF16),
        (meta, x0, g1, h1, lagged, high_table, low_table),
        scratch, flops=sends * (blocks - have) * lag_flops, smem=1,
    )
    own = call(
        functools.partial(own_kernel, width, rows, blocks),
        (jax.ShapeDtypeStruct((rows, pairs), F32), jax.ShapeDtypeStruct((width - rows, pairs), F32)),
        (meta, g0, h0, g1, h1, high_table, low_table),
        scratch, flops=blocks * lag_flops, smem=1,
    )
    lanes = 2 * capacity
    arrived = []
    routed = None
    for part, mine in zip((first, rest), own):
        if routed is not None:
            mine, *arrived = lax.optimization_barrier((mine, *arrived))
        received = [lax.ppermute(part[j], "tm", xor_pairs(tm_count, 2 * (j + 1))) for j in range(sends)]
        size = mine.shape[0]
        total = call(
            total_kernel, jax.ShapeDtypeStruct((size, pairs), BF16), (mine, jnp.stack(received)), flops=size * pairs
        )
        other = lax.ppermute(total, "sta", xor_pairs(sta_count, 1))
        routed = call(
            route_kernel,
            [jax.ShapeDtypeStruct((size, lanes), BF16)] * chips,
            (total, other, pick),
            flops=2 * size * 2 * pairs * chips * lanes,
        )
        moved = [lax.ppermute(routed[j], "sta", xor_pairs(sta_count, 2 * j)) for j in range(chips - 1, 0, -1)]
        arrived += [routed[0]] + moved[::-1]
    if lanes % 128 == 0:
        result = call(
            functools.partial(place_kernel, lanes, chips),
            jax.ShapeDtypeStruct((width, sta_count * capacity), F32),
            (meta, *arrived), flops=width * sta_count * capacity, smem=1,
        )
    else:
        order = jnp.bitwise_xor(me // 2, jnp.arange(chips, dtype=jnp.int32))
        parts = []
        for part in (arrived[:chips], arrived[chips:]):
            part = jnp.take(jnp.stack(part), order, axis=0).astype(F32)
            parts.append(jnp.transpose(part, (1, 0, 2)).reshape(part.shape[1], sta_count * capacity))
        result = jnp.concatenate(parts, axis=0)
    return result.T


def solution(mesh):
    in_specs = (
        P(None, "sta", "tm", None),
        P(),
        P("sta"),
        P("sta", None),
        P("sta", None),
        P("sta", None),
    )
    out_specs = P("sta", "tm")
    return jax.shard_map(local, mesh=mesh, in_specs=in_specs, out_specs=out_specs, check_vma=False)
```

time: 61.9 us -> 59.1 us (0.955)
  the two profiles are of different devices: /device:TPU:0 before, /device:TPU:24 now
where the time goes in v2:
time: 59.1 us; the launch traced here: 58.8 us
  waiting for transfers between devices  20.5 us (35%)
  Pallas kernels  20.1 us (34%)
  starting transfers between devices  14.2 us (24%)
  other arithmetic  1.41 us (2%)
  local copies, waits for them, and re-layouts  1.33 us (2%)
  between operations  0.8 us (1%)
    pallas_call x13, Pallas kernels, call(): pl.pallas_call(kernel, out_shape=out_shape, in_specs=specs, out_specs=out...  20.1 us
    ppermute x6, waiting for transfers between devices, local(): lax.ppermute(routed[j], 'sta', xor_pairs(sta_count, 2 * j))  7.92 us
    ppermute x6, starting transfers between devices, local(): lax.ppermute(routed[j], 'sta', xor_pairs(sta_count, 2 * j))  7.11 us
    ppermute x2, waiting for transfers between devices, local(): lax.ppermute(part[j], 'tm', xor_pairs(tm_count, 2 * (j + 1)))  4.76 us
    ppermute x1, waiting for transfers between devices, gather(): x_next = swap(x)  4.06 us
    ppermute x2, starting transfers between devices, local(): lax.ppermute(part[j], 'tm', xor_pairs(tm_count, 2 * (j + 1)))  3.06 us
    ppermute x2, waiting for transfers between devices, local(): other = lax.ppermute(total, 'sta', xor_pairs(sta_count, 1))  2.72 us
    ppermute x1, starting transfers between devices, gather(): pb = cross(x_next[by_cross:]) if offset == 1 else swap(p[by_cross:])  1.64 us
  transfers between devices with their start and end apart: 15, of which 12 were waited for; matrix products, arithmetic and copies ran while one was open for 2% of the time, Pallas kernels for 24%

profile of v2, /device:TPU:24, one launch (start us, length us, event | category | flops | bytes accessed | tf_op | source)
XLA Modules:
  0.0 58.8 jit_solution(7200211558719830003)
XLA Ops:
  0.0 1.3 %slice.45 = s32[1,1]{1,0:T(1,128)} slice(s32[7,8]{1,0:T(8,128)} %param.19), slice={[0:1], [0:1]} | slice | bytes 8 | tf_op jit(solution)/shard_map/slice | solution.py:283
  1.9 0.1 pad_add_fusion.meta
  2.0 0.0 copy-start
  2.0 0.0 copy-start.1
  2.0 19.9 %conditional.1 = (f32[3,512,256]{2,1,0:T(8,128)S(1)}, f32[3,512,256]{2,1,0:T(8,128)}, f32[3,512,256]{2,1,0:T(8,128)}, f32[3,512,256]{2,1,0:T(8,128)S(1)}, bf16[2...) conditional(s32[]{:T(128)} %bitcast.10, ...), branch_computations={%region_0.1_spmd, %region_1.2_spmd, %region_2.3_spmd, %region_3.4_... | conditional | flops 5632 | bytes 14962092 | solution.py:282
  2.2 0.5 collective-permute-start.20
  2.7 0.7 %collective-permute-start.22 = (bf16[384,512]{1,0:T(8,128)(2,1)}, bf16[384,512]{1,0:T(8,128)(2,1)S(1)}, u32[]{:S(2)}, u32[]{:S(2)}) collective-permute-start(bf16[384,512]{1,0:T(8,128)(2,1)} %get-tuple-element.180.x), channel_id=1, source_target_pairs={{0,20},{4,16},{8,28},{12,24},{16,4},{20,0},{24,12},{28,8},{1,21},{... | collective-permute-start | bytes 1179656 | tf_op jit(solution)/shard_map/cond/branch_4_fun/ppermute | solution.py:260
  3.4 1.3 %compare_select_fusion.4.owner = s32[1,256]{1,0:T(1,128)S(1)} fusion(s32[1,256]{1,0:T(1,128)} %get-tuple-element.186, s32[]{:T(128)} %bitcast.4), kind=kLoop, calls=%fused_computation.4 | loop fusion | flops 512 | bytes 2052 | tf_op jit(solution)/shard_map/cond/branch_4_fun/jit(_where)/select_n | solution.py:262
  4.7 1.0 %collective-permute-start.21 = (s32[1,256]{1,0:T(1,128)S(1)}, s32[1,256]{1,0:T(1,128)S(1)}, u32[]{:S(2)}, u32[]{:S(2)}) collective-permute-start(s32[1,256]{1,0:T(1,128)S(1)} %compare_select_fusion.4.owner), channel_id=1, source_target_pairs={{0,4},{4,0},{8,12},{12,8},{16,20},{20,16},{24,28},{28,24},{1,5},{5... | collective-permute-start | bytes 3080 | tf_op jit(solution)/shard_map/cond/branch_4_fun/ppermute | solution.py:263
  5.7 0.0 copy-start.6
  5.7 0.0 copy-start.21
  5.7 0.0 copy-start.28
  5.7 0.0 copy-start.43
  5.7 2.6 %branch_4_fun.5.g0 = f32[3,512,256]{2,1,0:T(8,128)S(1)} custom-call(bf16[384,512]{1,0:T(8,128)(2,1)} %get-tuple-element.180.x, bf16[512,512]{1,0:T(8,128)(2,1)} %get-tuple-element.181.dft, bf16[256,256]{1,0:T(8,128)(2,1)} %get-tuple-element.182.band, f32[256,128]{1,0:T(8,128)} %get-tuple-element.183.inverse, s32[1,256]{1,0:T(1,128)} %get-tuple-element.184.index), custom_call_target="tpu_custom_call" | custom-call | flops 1024 | bytes 1024 | tf_op jit(solution)/shard_map/cond/branch_4_fun/pallas_call | solution.py:217
  8.3 0.0 copy-start.13
  8.4 0.0 collective-permute-done.21.other_owner
  8.4 0.9 %branch_4_fun.6 = bf16[512,512]{1,0:T(8,128)(2,1)S(1)} custom-call(s32[3]{0:T(128)S(1)} %get-tuple-element.179.meta, s32[1,256]{1,0:T(1,128)S(1)} %compare_select_fusion.4.owner, s32[1,256]{1,0:T(1,128)S(1)} %collective-permute-done.21.other_owner), custom_call_target="tpu_custom_call" | custom-call | flops 1024 | bytes 1024 | tf_op jit(solution)/shard_map/cond/branch_4_fun/pallas_call | solution.py:217
  9.3 4.1 %collective-permute-done.20.x = bf16[384,512]{1,0:T(8,128)(2,1)S(1)} collective-permute-done((bf16[384,512]{1,0:T(8,128)(2,1)}, bf16[384,512]{1,0:T(8,128)(2,1)S(1)}, u32[]{:S(2)}, u32[]{:S(2)}) %collective-permute-start.20) | collective-permute-done | bytes 393248 | tf_op jit(solution)/shard_map/cond/branch_4_fun/ppermute | solution.py:259
  13.4 0.2 collective-permute-start.23
  13.5 0.7 %collective-permute-done.22.x = bf16[384,512]{1,0:T(8,128)(2,1)S(1)} collective-permute-done((bf16[384,512]{1,0:T(8,128)(2,1)}, bf16[384,512]{1,0:T(8,128)(2,1)S(1)}, u32[]{:S(2)}, u32[]{:S(2)}) %collective-permute-start.22) | collective-permute-done | bytes 393248 | tf_op jit(solution)/shard_map/cond/branch_4_fun/ppermute | solution.py:260
  14.3 1.6 %collective-permute-start.24 = (bf16[144,512]{1,0:T(8,128)(2,1)S(1)}, bf16[144,512]{1,0:T(8,128)(2,1)}, u32[]{:S(2)}, u32[]{:S(2)}) collective-permute-start(bf16[144,512]{1,0:T(8,128)(2,1)S(1)} %slice.55), channel_id=1, source_target_pairs={{0,1},{1,0},{2,3},{3,2},{4,5},{5,4},{6,7},{7,6},{8,9},{9,8},{10,11... | collective-permute-start | bytes 442376 | tf_op jit(solution)/shard_map/cond/branch_4_fun/ppermute | solution.py:271
  15.9 0.0 copy-done.6
  15.9 0.0 copy-done.21
  15.9 0.0 copy-done.28
  15.9 0.0 copy-done.43
  15.9 2.5 %branch_4_fun.7.h0 = f32[3,512,256]{2,1,0:T(8,128)} custom-call(bf16[384,512]{1,0:T(8,128)(2,1)S(1)} %collective-permute-done.22.x, bf16[512,512]{1,0:T(8,128)(2,1)S(1)} %copy-done.6, bf16[256,256]{1,0:T(8,128)(2,1)S(1)} %copy-done.28, f32[256,128]{1,0:T(8,128)S(1)} %copy-done.21, s32[1,256]{1,0:T(1,128)S(1)} %copy-done.43), custom_call_target="tpu_custom_call" | custom-call | flops 1024 | bytes 1024 | tf_op jit(solution)/shard_map/cond/branch_4_fun/pallas_call | solution.py:217
  18.4 0.0 copy-done.13
  18.4 0.0 copy-start.36
  18.4 1.6 %branch_4_fun.8 = f32[3,512,256]{2,1,0:T(8,128)S(1)} custom-call(s32[3]{0:T(128)S(1)} %get-tuple-element.179.meta, f32[3,512,256]{2,1,0:T(8,128)S(1)} %branch_4_fun.5.g0, f32[3,512,256]{2,1,0:T(8,128)} %branch_4_fun.7.h0), custom_call_target="tpu_custom_call" | custom-call | flops 1024 | bytes 1024 | tf_op jit(solution)/shard_map/cond/branch_4_fun/pallas_call | solution.py:217
  20.1 0.0 copy-done.36
  20.1 1.3 %branch_4_fun.9 = f32[3,512,256]{2,1,0:T(8,128)S(1)} custom-call(bf16[384,512]{1,0:T(8,128)(2,1)S(1)} %collective-permute-done.20.x, bf16[512,512]{1,0:T(8,128)(2,1)S(1)} %copy-done.6, bf16[256,256]{1,0:T(8,128)(2,1)S(1)} %copy-done.28, f32[256,128]{1,0:T(8,128)S(1)} %copy-done.21, s32[1,256]{1,0:T(1,128)S(1)} %copy-done.36), custom_call_target="tpu_custom_call" | custom-call | flops 1024 | bytes 1024 | tf_op jit(solution)/shard_map/cond/branch_4_fun/pallas_call | solution.py:217
  21.4 0.0 collective-permute-done.24
  21.4 0.3 collective-permute-done.23
  21.9 0.0 copy-start.31
  21.9 0.0 copy-done
  21.9 0.0 copy-done.1
  22.0 3.9 %shard_map.109 = (bf16[1,192,256]{2,1,0:T(8,128)(2,1)S(1)}, f32[1,512,256]{2,1,0:T(8,128)S(1)}, f32[3,512,256]{2,1,0:T(8,128)S(1)}) custom-call(s32[3]{0:T(128)S(1)} %pad_add_fusion.meta, f32[3,512,256]{2,1,0:T(8,128)S(1)} %get-tuple-element.243.x0, f32[3,512,256]{2,1,0:T(8,128)S(1)} %get-tuple-element.242.g1, bf16[240,512]{1,0:T(8,128)(2,1)} %get-tuple-element.244.xa, ...), custom_call_target="tpu_custom_call" | custom-call | flops 1024 | bytes 1024 | tf_op jit(solution)/shard_map/pallas_call | solution.py:217
  25.9 0.0 copy-done.31
  25.9 0.4 collective-permute-start.35
  26.3 2.0 %shard_map.113 = bf16[1,384,256]{2,1,0:T(8,128)(2,1)S(1)} custom-call(s32[3]{0:T(128)S(1)} %pad_add_fusion.meta, f32[3,512,256]{2,1,0:T(8,128)} %copy-done.31, f32[3,512,256]{2,1,0:T(8,128)S(1)} %get-tuple-element.242.g1, f32[3,512,256]{2,1,0:T(8,128)S(1)} %get-tuple-element.246.h1, f32[1,512,256]{2,1,0:T(8,128)S(1)} %get-tuple-element.260.lagged_in, ...), custom_call_target="tpu_custom_call" | custom-call | flops 1024 | bytes 1024 | tf_op jit(solution)/shard_map/pallas_call | solution.py:217
  28.3 2.7 %collective-permute-start.40 = (bf16[384,256]{1,0:T(8,128)(2,1)S(1)}, bf16[384,256]{1,0:T(8,128)(2,1)S(1)}, u32[]{:S(2)}, u32[]{:S(2)}) collective-permute-start(bf16[384,256]{1,0:T(8,128)(2,1)S(1)} %bitcast.17), channel_id=1, source_target_pairs={{0,2},{1,3},{2,0},{3,1},{4,6},{5,7},{6,4},{7,5},{8,10},{9,11},{10,... | collective-permute-start | bytes 589832 | tf_op jit(solution)/shard_map/ppermute | solution.py:317
  31.0 0.0 copy-done.16
  31.0 2.7 %shard_map.110 = (f32[192,256]{1,0:T(8,128)S(1)}, f32[384,256]{1,0:T(8,128)S(1)}) custom-call(s32[3]{0:T(128)S(1)} %pad_add_fusion.meta, f32[3,512,256]{2,1,0:T(8,128)S(1)} %copy-done.16, f32[3,512,256]{2,1,0:T(8,128)} %get-tuple-element.241.h0, f32[3,512,256]{2,1,0:T(8,128)S(1)} %get-tuple-element.242.g1, f32[3,512,256]{2,1,0:T(8,128)S(1)} %get-tuple-element.246.h1, ...), custom_call_target="tpu_custom_call" | custom-call | flops 1024 | bytes 1024 | tf_op jit(solution)/shard_map/pallas_call | solution.py:217
  33.7 4.8 %collective-permute-done.35 = bf16[192,256]{1,0:T(8,128)(2,1)S(1)} collective-permute-done((bf16[192,256]{1,0:T(8,128)(2,1)S(1)}, bf16[192,256]{1,0:T(8,128)(2,1)S(1)}, u32[]{:S(2)}, u32[]{:S(2)}) %collective-permute-start.35) | collective-permute-done | bytes 98336 | tf_op jit(solution)/shard_map/ppermute | solution.py:317
  38.5 0.1 collective-permute-start.36
  38.5 1.3 %collective-permute-done.36.other = bf16[192,256]{1,0:T(8,128)(2,1)S(1)} collective-permute-done((bf16[192,256]{1,0:T(8,128)(2,1)S(1)}, bf16[192,256]{1,0:T(8,128)(2,1)S(1)}, u32[]{:S(2)}, u32[]{:S(2)}) %collective-permute-start.36) | collective-permute-done | bytes 98336 | tf_op jit(solution)/shard_map/ppermute | solution.py:322
  39.8 0.3 shard_map.112
  40.1 1.6 %collective-permute-start.37 = (bf16[192,128]{1,0:T(8,128)(2,1)S(1)}, bf16[192,128]{1,0:T(8,128)(2,1)S(1)}, u32[]{:S(2)}, u32[]{:S(2)}) collective-permute-start(bf16[192,128]{1,0:T(8,128)(2,1)S(1)} %get-tuple-element.252), channel_id=1, source_target_pairs={{0,8},{4,12},{8,0},{12,4},{16,24},{20,28},{24,16},{28,20},{1,9},{5... | collective-permute-start | bytes 147464 | tf_op jit(solution)/shard_map/ppermute | solution.py:329
  41.7 0.6 %collective-permute-start.38 = (bf16[192,128]{1,0:T(8,128)(2,1)S(1)}, bf16[192,128]{1,0:T(8,128)(2,1)S(1)}, u32[]{:S(2)}, u32[]{:S(2)}) collective-permute-start(bf16[192,128]{1,0:T(8,128)(2,1)S(1)} %get-tuple-element.253), channel_id=1, source_target_pairs={{0,16},{4,20},{8,24},{12,28},{16,0},{20,4},{24,8},{28,12},{1,17},{... | collective-permute-start | bytes 147464 | tf_op jit(solution)/shard_map/ppermute | solution.py:329
  42.3 1.4 %collective-permute-start.39 = (bf16[192,128]{1,0:T(8,128)(2,1)S(1)}, bf16[192,128]{1,0:T(8,128)(2,1)S(1)}, u32[]{:S(2)}, u32[]{:S(2)}) collective-permute-start(bf16[192,128]{1,0:T(8,128)(2,1)S(1)} %get-tuple-element.254), channel_id=1, source_target_pairs={{0,24},{4,28},{8,16},{12,20},{16,8},{20,12},{24,0},{28,4},{1,25},{... | collective-permute-start | bytes 147464 | tf_op jit(solution)/shard_map/ppermute | solution.py:329
  43.7 0.6 %collective-permute-done.37.refs_1_ = bf16[192,128]{1,0:T(8,128)(2,1)S(1)} collective-permute-done((bf16[192,128]{1,0:T(8,128)(2,1)S(1)}, bf16[192,128]{1,0:T(8,128)(2,1)S(1)}, u32[]{:S(2)}, u32[]{:S(2)}) %collective-permute-start.37) | collective-permute-done | bytes 49184 | tf_op jit(solution)/shard_map/ppermute | solution.py:329
  44.3 2.0 %collective-permute-done.38.refs_2_ = bf16[192,128]{1,0:T(8,128)(2,1)S(1)} collective-permute-done((bf16[192,128]{1,0:T(8,128)(2,1)S(1)}, bf16[192,128]{1,0:T(8,128)(2,1)S(1)}, u32[]{:S(2)}, u32[]{:S(2)}) %collective-permute-start.38) | collective-permute-done | bytes 49184 | tf_op jit(solution)/shard_map/ppermute | solution.py:329
  46.3 1.0 %collective-permute-done.39.refs_3_ = bf16[192,128]{1,0:T(8,128)(2,1)S(1)} collective-permute-done((bf16[192,128]{1,0:T(8,128)(2,1)S(1)}, bf16[192,128]{1,0:T(8,128)(2,1)S(1)}, u32[]{:S(2)}, u32[]{:S(2)}) %collective-permute-start.39) | collective-permute-done | bytes 49184 | tf_op jit(solution)/shard_map/ppermute | solution.py:329
  47.3 0.0 collective-permute-done.40
  47.4 0.1 collective-permute-start.41
  47.4 1.4 %collective-permute-done.41.other = bf16[384,256]{1,0:T(8,128)(2,1)S(1)} collective-permute-done((bf16[384,256]{1,0:T(8,128)(2,1)S(1)}, bf16[384,256]{1,0:T(8,128)(2,1)S(1)}, u32[]{:S(2)}, u32[]{:S(2)}) %collective-permute-start.41) | collective-permute-done | bytes 196640 | tf_op jit(solution)/shard_map/ppermute | solution.py:322
  48.9 0.4 shard_map.115
  49.3 0.6 %collective-permute-start.42 = (bf16[384,128]{1,0:T(8,128)(2,1)S(1)}, bf16[384,128]{1,0:T(8,128)(2,1)S(1)}, u32[]{:S(2)}, u32[]{:S(2)}) collective-permute-start(bf16[384,128]{1,0:T(8,128)(2,1)S(1)} %get-tuple-element.262), channel_id=1, source_target_pairs={{0,8},{4,12},{8,0},{12,4},{16,24},{20,28},{24,16},{28,20},{1,9},{5... | collective-permute-start | bytes 294920 | tf_op jit(solution)/shard_map/ppermute | solution.py:329
  49.9 1.4 %collective-permute-start.43 = (bf16[384,128]{1,0:T(8,128)(2,1)S(1)}, bf16[384,128]{1,0:T(8,128)(2,1)S(1)}, u32[]{:S(2)}, u32[]{:S(2)}) collective-permute-start(bf16[384,128]{1,0:T(8,128)(2,1)S(1)} %get-tuple-element.263), channel_id=1, source_target_pairs={{0,16},{4,20},{8,24},{12,28},{16,0},{20,4},{24,8},{28,12},{1,17},{... | collective-permute-start | bytes 294920 | tf_op jit(solution)/shard_map/ppermute | solution.py:329
  51.3 1.6 %collective-permute-start.44 = (bf16[384,128]{1,0:T(8,128)(2,1)S(1)}, bf16[384,128]{1,0:T(8,128)(2,1)S(1)}, u32[]{:S(2)}, u32[]{:S(2)}) collective-permute-start(bf16[384,128]{1,0:T(8,128)(2,1)S(1)} %get-tuple-element.264), channel_id=1, source_target_pairs={{0,24},{4,28},{8,16},{12,20},{16,8},{20,12},{24,0},{28,4},{1,25},{... | collective-permute-start | bytes 294920 | tf_op jit(solution)/shard_map/ppermute | solution.py:329
  52.8 2.1 %collective-permute-done.42.refs_5_ = bf16[384,128]{1,0:T(8,128)(2,1)S(1)} collective-permute-done((bf16[384,128]{1,0:T(8,128)(2,1)S(1)}, bf16[384,128]{1,0:T(8,128)(2,1)S(1)}, u32[]{:S(2)}, u32[]{:S(2)}) %collective-permute-start.42) | collective-permute-done | bytes 98336 | tf_op jit(solution)/shard_map/ppermute | solution.py:329
  54.9 0.6 %collective-permute-done.43.refs_6_ = bf16[384,128]{1,0:T(8,128)(2,1)S(1)} collective-permute-done((bf16[384,128]{1,0:T(8,128)(2,1)S(1)}, bf16[384,128]{1,0:T(8,128)(2,1)S(1)}, u32[]{:S(2)}, u32[]{:S(2)}) %collective-permute-start.43) | collective-permute-done | bytes 98336 | tf_op jit(solution)/shard_map/ppermute | solution.py:329
  55.6 1.6 %collective-permute-done.44.refs_7_ = bf16[384,128]{1,0:T(8,128)(2,1)S(1)} collective-permute-done((bf16[384,128]{1,0:T(8,128)(2,1)S(1)}, bf16[384,128]{1,0:T(8,128)(2,1)S(1)}, u32[]{:S(2)}, u32[]{:S(2)}) %collective-permute-start.44) | collective-permute-done | bytes 98336 | tf_op jit(solution)/shard_map/ppermute | solution.py:329
  57.1 1.7 %shard_map.116 = f32[576,512]{1,0:T(8,128)} custom-call(s32[3]{0:T(128)S(1)} %pad_add_fusion.meta, bf16[192,128]{1,0:T(8,128)(2,1)S(1)} %get-tuple-element.255.refs_0_, bf16[192,128]{1,0:T(8,128)(2,1)S(1)} %collective-permute-done.37.refs_1_, bf16[192,128]{1,0:T(8,128)(2,1)S(1)} %collective-permute-done.38.refs_2_, ...), custom_call_target="tpu_custom_call" | custom-call | flops 1024 | bytes 1024 | tf_op jit(solution)/shard_map/pallas_call | solution.py:217
  (5 shorter events, 0.1 us)
Async XLA Ops:
  2.0 19.9 %copy-start = (bf16[256,512]{1,0:T(8,128)(2,1)S(1)}, bf16[256,512]{1,0:T(8,128)(2,1)}, u32[]{:S(2)}) copy-start(bf16[256,512]{1,0:T(8,128)(2,1)} %constant.69.clone.low_table) | copy-start | bytes 786436
  2.0 19.9 %copy-start.1 = (bf16[256,512]{1,0:T(8,128)(2,1)S(1)}, bf16[256,512]{1,0:T(8,128)(2,1)}, u32[]{:S(2)}) copy-start(bf16[256,512]{1,0:T(8,128)(2,1)} %constant.68.clone.high_table) | copy-start | bytes 786436
  2.2 11.1 %collective-permute-start.20 = (bf16[384,512]{1,0:T(8,128)(2,1)}, bf16[384,512]{1,0:T(8,128)(2,1)S(1)}, u32[]{:S(2)}, u32[]{:S(2)}) collective-permute-start(bf16[384,512]{1,0:T(8,128)(2,1)} %get-tuple-element.180.x), channel_id=1, source_target_pairs={{0,1},{1,0},{2,3},{3,2},{4,5},{5,4},{6,7},{7,6},{8,9},{9,8},{10,11... | collective-permute-start | bytes 1179656 | tf_op jit(solution)/shard_map/cond/branch_4_fun/ppermute | solution.py:259
  2.7 11.5 %collective-permute-start.22 = (bf16[384,512]{1,0:T(8,128)(2,1)}, bf16[384,512]{1,0:T(8,128)(2,1)S(1)}, u32[]{:S(2)}, u32[]{:S(2)}) collective-permute-start(bf16[384,512]{1,0:T(8,128)(2,1)} %get-tuple-element.180.x), channel_id=1, source_target_pairs={{0,20},{4,16},{8,28},{12,24},{16,4},{20,0},{24,12},{28,8},{1,21},{... | collective-permute-start | bytes 1179656 | tf_op jit(solution)/shard_map/cond/branch_4_fun/ppermute | solution.py:260
  4.7 3.6 %collective-permute-start.21 = (s32[1,256]{1,0:T(1,128)S(1)}, s32[1,256]{1,0:T(1,128)S(1)}, u32[]{:S(2)}, u32[]{:S(2)}) collective-permute-start(s32[1,256]{1,0:T(1,128)S(1)} %compare_select_fusion.4.owner), channel_id=1, source_target_pairs={{0,4},{4,0},{8,12},{12,8},{16,20},{20,16},{24,28},{28,24},{1,5},{5... | collective-permute-start | bytes 3080 | tf_op jit(solution)/shard_map/cond/branch_4_fun/ppermute | solution.py:263
  5.7 10.2 %copy-start.6 = (bf16[512,512]{1,0:T(8,128)(2,1)S(1)}, bf16[512,512]{1,0:T(8,128)(2,1)}, u32[]{:S(2)}) copy-start(bf16[512,512]{1,0:T(8,128)(2,1)} %get-tuple-element.181.dft) | copy-start | bytes 1572868 | tf_op jit(solution)/shard_map/cond
  5.7 10.2 %copy-start.21 = (f32[256,128]{1,0:T(8,128)S(1)}, f32[256,128]{1,0:T(8,128)}, u32[]{:S(2)}) copy-start(f32[256,128]{1,0:T(8,128)} %get-tuple-element.183.inverse) | copy-start | bytes 393220 | tf_op jit(solution)/shard_map/cond
  5.7 10.2 %copy-start.28 = (bf16[256,256]{1,0:T(8,128)(2,1)S(1)}, bf16[256,256]{1,0:T(8,128)(2,1)}, u32[]{:S(2)}) copy-start(bf16[256,256]{1,0:T(8,128)(2,1)} %get-tuple-element.182.band) | copy-start | bytes 393220 | tf_op jit(solution)/shard_map/cond
  5.7 10.2 %copy-start.43 = (s32[1,256]{1,0:T(1,128)S(1)}, s32[1,256]{1,0:T(1,128)}, u32[]{:S(2)}) copy-start(s32[1,256]{1,0:T(1,128)} %get-tuple-element.188.index) | copy-start | bytes 3076 | tf_op jit(solution)/shard_map/cond
  8.3 10.1 %copy-start.13 = (f32[3,512,256]{2,1,0:T(8,128)}, f32[3,512,256]{2,1,0:T(8,128)S(1)}, u32[]{:S(2)}) copy-start(f32[3,512,256]{2,1,0:T(8,128)S(1)} %branch_4_fun.5.g0) | copy-start | bytes 4718596 | tf_op jit(solution)/shard_map/cond
  13.4 8.3 %collective-permute-start.23 = (bf16[240,512]{1,0:T(8,128)(2,1)S(1)}, bf16[240,512]{1,0:T(8,128)(2,1)}, u32[]{:S(2)}, u32[]{:S(2)}) collective-permute-start(bf16[240,512]{1,0:T(8,128)(2,1)S(1)} %slice.54), channel_id=1, source_target_pairs={{0,20},{4,16},{8,28},{12,24},{16,4},{20,0},{24,12},{28,8},{1,21},{... | collective-permute-start | bytes 737288 | tf_op jit(solution)/shard_map/cond/branch_4_fun/ppermute | solution.py:270
  14.3 7.2 %collective-permute-start.24 = (bf16[144,512]{1,0:T(8,128)(2,1)S(1)}, bf16[144,512]{1,0:T(8,128)(2,1)}, u32[]{:S(2)}, u32[]{:S(2)}) collective-permute-start(bf16[144,512]{1,0:T(8,128)(2,1)S(1)} %slice.55), channel_id=1, source_target_pairs={{0,1},{1,0},{2,3},{3,2},{4,5},{5,4},{6,7},{7,6},{8,9},{9,8},{10,11... | collective-permute-start | bytes 442376 | tf_op jit(solution)/shard_map/cond/branch_4_fun/ppermute | solution.py:271
  18.4 1.6 %copy-start.36 = (s32[1,256]{1,0:T(1,128)S(1)}, s32[1,256]{1,0:T(1,128)}, u32[]{:S(2)}) copy-start(s32[1,256]{1,0:T(1,128)} %get-tuple-element.184.index) | copy-start | bytes 3076 | tf_op jit(solution)/shard_map/cond
  21.9 4.0 %copy-start.31 = (f32[3,512,256]{2,1,0:T(8,128)}, f32[3,512,256]{2,1,0:T(8,128)S(1)}, u32[]{:S(2)}) copy-start(f32[3,512,256]{2,1,0:T(8,128)S(1)} %get-tuple-element.243.x0) | copy-start | bytes 4718596
  25.9 12.5 %collective-permute-start.35 = (bf16[192,256]{1,0:T(8,128)(2,1)S(1)}, bf16[192,256]{1,0:T(8,128)(2,1)S(1)}, u32[]{:S(2)}, u32[]{:S(2)}) collective-permute-start(bf16[192,256]{1,0:T(8,128)(2,1)S(1)} %bitcast.20), channel_id=1, source_target_pairs={{0,2},{1,3},{2,0},{3,1},{4,6},{5,7},{6,4},{7,5},{8,10},{9,11},{10,... | collective-permute-start | bytes 294920 | tf_op jit(solution)/shard_map/ppermute | solution.py:317
  26.3 4.7 %copy-start.16 = (f32[3,512,256]{2,1,0:T(8,128)S(1)}, f32[3,512,256]{2,1,0:T(8,128)}, u32[]{:S(2)}) copy-start(f32[3,512,256]{2,1,0:T(8,128)} %get-tuple-element.240.g0) | copy-start | bytes 4718596
  28.3 19.0 %collective-permute-start.40 = (bf16[384,256]{1,0:T(8,128)(2,1)S(1)}, bf16[384,256]{1,0:T(8,128)(2,1)S(1)}, u32[]{:S(2)}, u32[]{:S(2)}) collective-permute-start(bf16[384,256]{1,0:T(8,128)(2,1)S(1)} %bitcast.17), channel_id=1, source_target_pairs={{0,2},{1,3},{2,0},{3,1},{4,6},{5,7},{6,4},{7,5},{8,10},{9,11},{10,... | collective-permute-start | bytes 589832 | tf_op jit(solution)/shard_map/ppermute | solution.py:317
  38.5 1.4 %collective-permute-start.36 = (bf16[192,256]{1,0:T(8,128)(2,1)S(1)}, bf16[192,256]{1,0:T(8,128)(2,1)S(1)}, u32[]{:S(2)}, u32[]{:S(2)}) collective-permute-start(bf16[192,256]{1,0:T(8,128)(2,1)S(1)} %shard_map.111.total), channel_id=1, source_target_pairs={{0,4},{4,0},{8,12},{12,8},{16,20},{20,16},{24,28},{28,24},{1,5},{5... | collective-permute-start | bytes 294920 | tf_op jit(solution)/shard_map/ppermute | solution.py:322
  40.1 4.2 %collective-permute-start.37 = (bf16[192,128]{1,0:T(8,128)(2,1)S(1)}, bf16[192,128]{1,0:T(8,128)(2,1)S(1)}, u32[]{:S(2)}, u32[]{:S(2)}) collective-permute-start(bf16[192,128]{1,0:T(8,128)(2,1)S(1)} %get-tuple-element.252), channel_id=1, source_target_pairs={{0,8},{4,12},{8,0},{12,4},{16,24},{20,28},{24,16},{28,20},{1,9},{5... | collective-permute-start | bytes 147464 | tf_op jit(solution)/shard_map/ppermute | solution.py:329
  41.7 4.6 %collective-permute-start.38 = (bf16[192,128]{1,0:T(8,128)(2,1)S(1)}, bf16[192,128]{1,0:T(8,128)(2,1)S(1)}, u32[]{:S(2)}, u32[]{:S(2)}) collective-permute-start(bf16[192,128]{1,0:T(8,128)(2,1)S(1)} %get-tuple-element.253), channel_id=1, source_target_pairs={{0,16},{4,20},{8,24},{12,28},{16,0},{20,4},{24,8},{28,12},{1,17},{... | collective-permute-start | bytes 147464 | tf_op jit(solution)/shard_map/ppermute | solution.py:329
  42.3 5.0 %collective-permute-start.39 = (bf16[192,128]{1,0:T(8,128)(2,1)S(1)}, bf16[192,128]{1,0:T(8,128)(2,1)S(1)}, u32[]{:S(2)}, u32[]{:S(2)}) collective-permute-start(bf16[192,128]{1,0:T(8,128)(2,1)S(1)} %get-tuple-element.254), channel_id=1, source_target_pairs={{0,24},{4,28},{8,16},{12,20},{16,8},{20,12},{24,0},{28,4},{1,25},{... | collective-permute-start | bytes 147464 | tf_op jit(solution)/shard_map/ppermute | solution.py:329
  47.4 1.5 %collective-permute-start.41 = (bf16[384,256]{1,0:T(8,128)(2,1)S(1)}, bf16[384,256]{1,0:T(8,128)(2,1)S(1)}, u32[]{:S(2)}, u32[]{:S(2)}) collective-permute-start(bf16[384,256]{1,0:T(8,128)(2,1)S(1)} %shard_map.114.total), channel_id=1, source_target_pairs={{0,4},{4,0},{8,12},{12,8},{16,20},{20,16},{24,28},{28,24},{1,5},{5... | collective-permute-start | bytes 589832 | tf_op jit(solution)/shard_map/ppermute | solution.py:322
  49.3 5.6 %collective-permute-start.42 = (bf16[384,128]{1,0:T(8,128)(2,1)S(1)}, bf16[384,128]{1,0:T(8,128)(2,1)S(1)}, u32[]{:S(2)}, u32[]{:S(2)}) collective-permute-start(bf16[384,128]{1,0:T(8,128)(2,1)S(1)} %get-tuple-element.262), channel_id=1, source_target_pairs={{0,8},{4,12},{8,0},{12,4},{16,24},{20,28},{24,16},{28,20},{1,9},{5... | collective-permute-start | bytes 294920 | tf_op jit(solution)/shard_map/ppermute | solution.py:329
  49.9 5.7 %collective-permute-start.43 = (bf16[384,128]{1,0:T(8,128)(2,1)S(1)}, bf16[384,128]{1,0:T(8,128)(2,1)S(1)}, u32[]{:S(2)}, u32[]{:S(2)}) collective-permute-start(bf16[384,128]{1,0:T(8,128)(2,1)S(1)} %get-tuple-element.263), channel_id=1, source_target_pairs={{0,16},{4,20},{8,24},{12,28},{16,0},{20,4},{24,8},{28,12},{1,17},{... | collective-permute-start | bytes 294920 | tf_op jit(solution)/shard_map/ppermute | solution.py:329
  51.3 5.9 %collective-permute-start.44 = (bf16[384,128]{1,0:T(8,128)(2,1)S(1)}, bf16[384,128]{1,0:T(8,128)(2,1)S(1)}, u32[]{:S(2)}, u32[]{:S(2)}) collective-permute-start(bf16[384,128]{1,0:T(8,128)(2,1)S(1)} %get-tuple-element.264), channel_id=1, source_target_pairs={{0,24},{4,28},{8,16},{12,20},{16,8},{20,12},{24,0},{28,4},{1,25},{... | collective-permute-start | bytes 294920 | tf_op jit(solution)/shard_map/ppermute | solution.py:329

commit v3 on v2

v3 whole, which is shorter than its diff:
```python
import functools
import math

import jax
import jax.numpy as jnp
import numpy as np
from jax import lax
from jax.experimental import pallas as pl
from jax.experimental.pallas import tpu as pltpu
from jax.sharding import PartitionSpec as P

LAGS = 256
HALF_BAND = 21
EPSILON = 1e-06
F32 = jnp.float32
BF16 = jnp.bfloat16
VMEM_LIMIT = 14 * 1024 * 1024
STEP = 32


def xor_pairs(count, mask):
    return [(i, i ^ mask) for i in range(count)]


def split(x):
    hi = x.astype(BF16)
    return hi, (x - hi.astype(F32)).astype(BF16)


def tables(samples, freqs, scale):
    n = np.arange(samples, dtype=np.int64)
    f = np.arange(freqs, dtype=np.int64)
    step = np.float32(2.0 * math.pi / samples)
    phase = (step * np.mod(f[:, None] * n[None, :], samples).astype(np.float32)).astype(np.float32)
    dft = np.concatenate([np.cos(phase), -np.sin(phase)], axis=0).astype(jnp.bfloat16)
    lag = np.arange(LAGS, dtype=np.int64) - LAGS // 2
    phase = (step * np.mod(lag[:, None] * f[None, :], samples).astype(np.float32)).astype(np.float32)
    table = np.concatenate([np.cos(phase), -np.sin(phase)], axis=1) * np.float32(scale)
    high = table.astype(jnp.bfloat16)
    low = (table - high.astype(np.float32)).astype(jnp.bfloat16)
    near = np.abs(f[:, None] - f[None, :]) <= HALF_BAND
    inverse = (1.0 / (3.0 * near.sum(axis=1))).astype(np.float32)[:, None]
    return dft, high, low, near.astype(jnp.bfloat16), np.broadcast_to(inverse, (freqs, 128)).copy()


def whiten_factor(amplitude, band, inverse):
    high, low = split(amplitude)
    smooth = jnp.dot(band, high, preferred_element_type=F32) + jnp.dot(band, low, preferred_element_type=F32)
    return 1.0 / (smooth * inverse[:, :1] + EPSILON)


def one_hot(index, stations):
    pick = lax.broadcasted_iota(jnp.int32, (stations, index.shape[1]), 0) == index
    pick = pick.astype(F32).astype(BF16)
    return jnp.concatenate([pick, pick], axis=0)


def whiten_rows(x, dft, band, inverse, index):
    stations = x.shape[0] // 3
    freqs = band.shape[0]
    spectra = lax.dot_general(dft, x, (((1,), (1,)), ((), ())), preferred_element_type=F32)
    spectra = [spectra[:, c * stations : (c + 1) * stations] for c in range(3)]
    amplitude = sum(jnp.sqrt(s[:freqs] * s[:freqs] + s[freqs:] * s[freqs:]) for s in spectra)
    factor = whiten_factor(amplitude, band, inverse)
    factor = jnp.concatenate([factor, factor], axis=0)
    pick = one_hot(index, stations)
    rows = []
    for s in spectra:
        high, low = split(s * factor)
        rows.append(jnp.dot(jnp.concatenate([high, low], axis=1), pick, preferred_element_type=F32))
    return rows


def whiten_kernel(x, dft, band, inverse, index, out, spectra):
    stations = x.shape[0] // 3
    freqs = band.shape[0]

    def transform(c, amplitude):
        at = pl.ds(pl.multiple_of(c * stations, stations), stations)
        s = lax.dot_general(dft[...], x[at], (((1,), (1,)), ((), ())), preferred_element_type=F32)
        spectra[c] = s
        return amplitude + jnp.sqrt(s[:freqs] * s[:freqs] + s[freqs:] * s[freqs:])

    amplitude = lax.fori_loop(0, 3, transform, jnp.zeros((freqs, stations), F32))
    factor = whiten_factor(amplitude, band[...], inverse[...])
    factor = jnp.concatenate([factor, factor], axis=0)
    pick = one_hot(index[...], stations)

    def gather(c, carry):
        high, low = split(spectra[c] * factor)
        out[c] = jnp.dot(jnp.concatenate([high, low], axis=1), pick, preferred_element_type=F32)
        return carry

    lax.fori_loop(0, 3, gather, 0)


def cross_rows(lefts, rights, a, c, r, real, imag):
    freqs = lefts[0].shape[1] // 2
    near, far = pl.ds(r, STEP), pl.ds(freqs + r, STEP)
    for left, right in zip(lefts, rights):
        lr, li = left[a, near], left[a, far]
        rr, ri = right[c, near], right[c, far]
        real = real + (lr * rr + li * ri)
        imag = imag + (li * rr - lr * ri)
    return real, imag


def component_pair(first, j):
    ac = jnp.minimum(first + j, 8)
    return ac // 3, ac % 3


def over_rows(freqs, body):
    def step(i, carry):
        body(pl.multiple_of(i * STEP, STEP))
        return carry

    lax.fori_loop(0, freqs // STEP, step, 0)


def cross_kernel(width, blocks, sends, g0, h0, out):
    freqs = g0.shape[1] // 2

    def block(i, carry):
        first = ((lax.axis_index("tm") ^ (2 * (i // blocks + 1))) * width) // LAGS
        a, c = component_pair(first, i % blocks)

        def rows(r):
            real, imag = cross_rows((g0,), (h0,), a, c, r, 0.0, 0.0)
            out[i, pl.ds(r, STEP)] = real
            out[i, pl.ds(freqs + r, STEP)] = imag

        over_rows(freqs, rows)
        return carry

    lax.fori_loop(0, sends * blocks, block, 0)


def lag_block(lefts, rights, base, a, c, high_table, low_table, cross_high, cross_low):
    freqs = lefts[0].shape[1] // 2

    def rows(r):
        near, far = pl.ds(r, STEP), pl.ds(freqs + r, STEP)
        real, imag = (0.0, 0.0) if base is None else (base[near], base[far])
        real, imag = cross_rows(lefts, rights, a, c, r, real, imag)
        cross_high[near], cross_low[near] = split(real)
        cross_high[far], cross_low[far] = split(imag)

    over_rows(freqs, rows)
    return (
        jnp.dot(high_table[...], cross_high[...], preferred_element_type=F32)
        + jnp.dot(low_table[...], cross_high[...], preferred_element_type=F32)
        + jnp.dot(high_table[...], cross_low[...], preferred_element_type=F32)
    )


def piece(k_piece, width, blocks, lefts, rights, base, lagged, high_table, low_table, cross_high, cross_low):
    start = k_piece * width
    first = start // LAGS

    def block(j, carry):
        a, c = component_pair(first, j)
        lagged[pl.ds(pl.multiple_of(j * LAGS, LAGS), LAGS)] = lag_block(
            lefts, rights, None if base is None else base.at[j], a, c, high_table, low_table, cross_high, cross_low
        )
        return carry

    lax.fori_loop(0, blocks, block, 0)
    return start - first * LAGS


def send_kernel(
    width, blocks, sends, x0, g1, xa, xb, dft, band, inverse, index, high_table, low_table,
    out, rest, h1, cross_high, cross_low, lagged,
):
    x = jnp.concatenate([xa[...], xb[...]], axis=0)
    white = whiten_rows(x, dft[...], band[...], inverse[...], index[...])
    for c in range(3):
        h1[c] = white[c]
    rows = out.shape[1]
    for k in range(sends):
        base = x0.at[k * blocks : (k + 1) * blocks]
        shift = piece(
            lax.axis_index("tm") ^ (2 * (k + 1)), width, blocks, (g1,), (h1,), base, lagged,
            high_table, low_table, cross_high, cross_low,
        )
        out[k] = lagged[pl.ds(pl.multiple_of(shift, 16), rows)].astype(BF16)
        rest[k] = lagged[pl.ds(pl.multiple_of(shift + rows, 16), width - rows)].astype(BF16)


def own_kernel(
    width, blocks, g0, h0, g1, h1, high_table, low_table, out, rest, cross_high, cross_low, lagged
):
    shift = piece(
        lax.axis_index("tm"), width, blocks, (g0, g1), (h0, h1), None, lagged, high_table, low_table, cross_high, cross_low
    )
    rows = out.shape[0]
    out[...] = lagged[pl.ds(pl.multiple_of(shift, 16), rows)]
    rest[...] = lagged[pl.ds(pl.multiple_of(shift + rows, 16), width - rows)]


def total_kernel(own, received, out):
    total = own[...]
    for j in range(received.shape[0]):
        total = total + received[j].astype(F32)
    out[...] = total.astype(BF16)


def ranks(owner, blocks):
    pairs = owner.shape[1]
    hits = lax.broadcasted_iota(jnp.int32, (blocks, pairs), 0) == owner
    hits = hits.astype(F32)
    earlier = lax.broadcasted_iota(jnp.int32, (pairs, pairs), 0) < lax.broadcasted_iota(jnp.int32, (pairs, pairs), 1)
    before = jnp.dot(hits.astype(BF16), earlier.astype(F32).astype(BF16), preferred_element_type=F32)
    return jnp.sum(before * hits, axis=0, keepdims=True).astype(jnp.int32)


def pick_kernel(blocks, capacity, owner, other_owner, out):
    me = lax.axis_index("sta")
    chip, core = me // 2, me % 2
    pairs = owner.shape[1]
    for place, (value, lists) in enumerate(((owner[...], core), (other_owner[...], 1 - core))):
        slot = ((value // 2) ^ chip) * (2 * capacity) + lists * capacity + ranks(value, blocks)
        mine = jnp.logical_and(value >= 0, value % 2 == core)
        slot = jnp.where(mine, slot, -1)
        slots = lax.broadcasted_iota(jnp.int32, (blocks * capacity, pairs), 0)
        out[:, place * pairs : (place + 1) * pairs] = (slots == slot).astype(F32).astype(BF16)


def route_kernel(total, other, pick, *outs):
    values = jnp.concatenate([total[...], other[...]], axis=1)
    routed = lax.dot_general(values, pick[...], (((1,), (1,)), ((), ())), preferred_element_type=F32)
    lanes = routed.shape[1] // len(outs)
    for j, out in enumerate(outs):
        out[...] = routed[:, j * lanes : (j + 1) * lanes].astype(BF16)


def place_kernel(lanes, top, *refs):
    out, rows, sems = refs[-3:]
    chip = lax.axis_index("sta") // 2
    copies = []
    for j in range(rows.shape[0]):
        at = pl.ds(pl.multiple_of((chip ^ j) * lanes, lanes), lanes)
        rows[j] = refs[j][...].astype(F32)
        copies.append(pltpu.make_async_copy(rows.at[j], out.at[pl.ds(top, rows.shape[1]), at], sems.at[j]))
        copies[-1].start()
    for copy in copies:
        copy.wait()


def place(lanes, top, shape, arrived, before):
    chips = len(arrived)
    args = list(arrived) + ([] if before is None else [before])
    anywhere = pl.BlockSpec(memory_space=pl.ANY)
    return pl.pallas_call(
        functools.partial(place_kernel, lanes, top),
        out_shape=shape,
        in_specs=[pl.BlockSpec(memory_space=pltpu.VMEM)] * chips + [anywhere] * (before is not None),
        out_specs=anywhere,
        scratch_shapes=[pltpu.VMEM((chips, arrived[0].shape[0], lanes), F32), pltpu.SemaphoreType.DMA((chips,))],
        input_output_aliases={} if before is None else {chips: 0},
        compiler_params=pltpu.CompilerParams(vmem_limit_bytes=VMEM_LIMIT),
        cost_estimate=pl.CostEstimate(flops=1024, bytes_accessed=1024, transcendentals=0),
    )(*args)


def call(kernel, out_shape, args, scratch=()):
    outs = jax.tree.map(lambda _: pl.BlockSpec(memory_space=pltpu.VMEM), out_shape)
    return pl.pallas_call(
        kernel,
        out_shape=out_shape,
        in_specs=[pl.BlockSpec(memory_space=pltpu.VMEM)] * len(args),
        out_specs=outs,
        scratch_shapes=list(scratch),
        compiler_params=pltpu.CompilerParams(vmem_limit_bytes=VMEM_LIMIT),
        cost_estimate=pl.CostEstimate(flops=1024, bytes_accessed=1024, transcendentals=0),
    )(*args)


def local(waves, partner, pair_count, left_station, right_station, owner):
    sta_count = lax.axis_size("sta")
    tm_count = lax.axis_size("tm")
    comps, stations, seg_local, samples = waves.shape
    freqs = samples // 2
    pairs = left_station.shape[1]
    capacity = 2 * pairs // sta_count
    width = comps * comps * LAGS // tm_count
    chips = sta_count // 2
    sends = tm_count // 2 - 1
    top = LAGS - math.gcd(width, LAGS)
    blocks = -(-(top + width) // LAGS)
    rows = -(-width // 48) * 16
    scale = 1.0 / math.sqrt(freqs * seg_local * tm_count)
    dft, high_table, low_table, band, inverse = (jnp.asarray(a) for a in tables(samples, freqs, scale))

    x = waves.reshape(comps * stations, samples)
    by_cross = -(-x.shape[0] * 5 // 8 // 16) * 16
    rows_shape = jax.ShapeDtypeStruct((comps, 2 * freqs, pairs), F32)

    def whitened(records, index):
        return call(
            whiten_kernel, rows_shape, (records, dft, band, inverse, index),
            [pltpu.VMEM((comps, 2 * freqs, stations), F32)],
        )

    def gather(offset, x, left, right, owner, pair_count):
        swap = functools.partial(lax.ppermute, axis_name="tm", perm=xor_pairs(tm_count, 1))
        cross = functools.partial(lax.ppermute, axis_name="sta", perm=xor_pairs(sta_count, offset))
        p = cross(x)
        x_next = swap(x)
        g0 = whitened(x, left)
        listed = jnp.where(jnp.arange(pairs, dtype=jnp.int32)[None, :] < pair_count[0], owner, -1)
        other_listed = lax.ppermute(listed, "sta", xor_pairs(sta_count, 1))
        pick = call(
            functools.partial(pick_kernel, sta_count, capacity),
            jax.ShapeDtypeStruct((sta_count * capacity, 2 * pairs), BF16),
            (listed, other_listed),
        )
        near, g0, pick = lax.optimization_barrier((x_next[:by_cross], g0, pick))
        pa = cross(near)
        pb = cross(x_next[by_cross:]) if offset == 1 else swap(p[by_cross:])
        g1 = whitened(x_next, left)
        p, g1 = lax.optimization_barrier((p, g1))
        h0 = whitened(p, right)
        x0 = call(
            functools.partial(cross_kernel, width, blocks, sends),
            jax.ShapeDtypeStruct((sends * blocks, 2 * freqs, pairs), F32),
            (g0, h0),
        )
        first, rest, h1 = call(
            functools.partial(send_kernel, width, blocks, sends),
            (
                jax.ShapeDtypeStruct((sends, rows, pairs), BF16),
                jax.ShapeDtypeStruct((sends, width - rows, pairs), BF16),
                rows_shape,
            ),
            (x0, g1, pa, pb, dft, band, inverse, right, high_table, low_table),
            scratch,
        )
        received = exchange(first)
        own = call(
            functools.partial(own_kernel, width, blocks),
            (jax.ShapeDtypeStruct((rows, pairs), F32), jax.ShapeDtypeStruct((width - rows, pairs), F32)),
            (g0, h0, g1, h1, high_table, low_table),
            scratch,
        )
        return received, rest, own, pick

    def exchange(part):
        return [lax.ppermute(part[j], "tm", xor_pairs(tm_count, 2 * (j + 1))) for j in range(sends)]

    scratch = [pltpu.VMEM((2 * freqs, pairs), BF16)] * 2 + [pltpu.VMEM((blocks * LAGS, pairs), F32)]
    branches = [functools.partial(gather, k) for k in range(1, sta_count)]
    received, rest, own, pick = lax.switch(
        partner[0, 0] - 1, branches, x, left_station, right_station, owner, pair_count
    )
    received = [received, exchange(rest)]
    lanes = 2 * capacity
    shape = jax.ShapeDtypeStruct((width, sta_count * capacity), F32)
    parts, arrived, result = [], [], None
    for got, mine in zip(received, own):
        mine = lax.optimization_barrier((mine, *arrived))[0]
        size = mine.shape[0]
        total = call(total_kernel, jax.ShapeDtypeStruct((size, pairs), BF16), (mine, jnp.stack(got)))
        other = lax.ppermute(total, "sta", xor_pairs(sta_count, 1))
        routed = call(route_kernel, [jax.ShapeDtypeStruct((size, lanes), BF16)] * chips, (total, other, pick))
        arrived = [lax.ppermute(routed[j], "sta", xor_pairs(sta_count, 2 * j)) for j in range(chips - 1, 0, -1)]
        arrived = [routed[0]] + arrived[::-1]
        if lanes % 128 == 0:
            result = place(lanes, 0 if result is None else rows, shape, arrived, result)
        else:
            order = jnp.bitwise_xor(lax.axis_index("sta") // 2, jnp.arange(chips, dtype=jnp.int32))
            arrived = jnp.take(jnp.stack(arrived), order, axis=0).astype(F32)
            parts.append(jnp.transpose(arrived, (1, 0, 2)).reshape(size, sta_count * capacity))
            result = jnp.concatenate(parts, axis=0)
    return result.T


def solution(mesh):
    in_specs = (
        P(None, "sta", "tm", None),
        P(),
        P("sta"),
        P("sta", None),
        P("sta", None),
        P("sta", None),
    )
    out_specs = P("sta", "tm")
    return jax.shard_map(local, mesh=mesh, in_specs=in_specs, out_specs=out_specs, check_vma=False)
```

time: 59.1 us -> 56.6 us (0.958)
  the two profiles are of different devices: /device:TPU:24 before, /device:TPU:0 now
where the time goes in v3:
time: 56.6 us; the launch traced here: 56.4 us
  waiting for transfers between devices  18.7 us (33%)
  starting transfers between devices  17.8 us (31%)
  Pallas kernels  15.9 us (28%)
  other arithmetic  1.33 us (2%)
  local copies, waits for them, and re-layouts  1.26 us (2%)
  between operations  0.92 us (2%)
    pallas_call x11, Pallas kernels, call(): pl.pallas_call(kernel, out_shape=out_shape, in_specs=[pl.BlockSpec(memory...  14.2 us
    ppermute x6, starting transfers between devices, local(): lax.ppermute(routed[j], 'sta', xor_pairs(sta_count, 2 * j))  7.1 us
    ppermute x6, waiting for transfers between devices, local(): lax.ppermute(routed[j], 'sta', xor_pairs(sta_count, 2 * j))  6.37 us
    ppermute x2, waiting for transfers between devices, exchange(): lax.ppermute(part[j], 'tm', xor_pairs(tm_count, 2 * (j + 1)))  4.41 us
    ppermute x2, starting transfers between devices, exchange(): lax.ppermute(part[j], 'tm', xor_pairs(tm_count, 2 * (j + 1)))  3.57 us
    ppermute x1, starting transfers between devices, gather(): x_next = swap(x)  3.09 us
    ppermute x2, waiting for transfers between devices, local(): other = lax.ppermute(total, 'sta', xor_pairs(sta_count, 1))  2.72 us
    ppermute x1, waiting for transfers between devices, gather(): x_next = swap(x)  1.88 us
  transfers between devices with their start and end apart: 15, of which 12 were waited for; matrix products, arithmetic and copies ran while one was open for 2% of the time, Pallas kernels for 21%

profile of v3, /device:TPU:0, one launch (start us, length us, event | category | flops | bytes accessed | tf_op | source)
XLA Modules:
  0.0 56.4 jit_solution(7455134562380185023)
XLA Ops:
  0.0 1.2 %slice.45 = s32[1,1]{1,0:T(1,128)} slice(s32[7,8]{1,0:T(8,128)} %param.19), slice={[0:1], [0:1]} | slice | bytes 8 | tf_op jit(solution)/shard_map/slice | solution.py:355
  1.9 32.9 %conditional.1 = (bf16[1,384,256]{2,1,0:T(8,128)(2,1)S(1)}, f32[192,256]{1,0:T(8,128)S(1)}, f32[384,256]{1,0:T(8,128)S(1)}, bf16[512,512]{1,0:T(8,128)(2,1)S(1)}, bf16[1,192,256]{2,1,0:T(8,128)(2,1)}) conditional(s32[]{:T(128)} %bitcast.21, (bf16[384,512]{1,0:T(8,128)(2,1)}, bf16[512,512]{1,0:T(8,128)(2,1)}, ...), branch_computations={%region_0.1_spmd, %region_1.2_spmd, %region_2.3_spmd, %region_3.4_... | conditional | flops 7680 | bytes 11163104 | solution.py:354
  2.1 3.1 %collective-permute-start.36 = (bf16[384,512]{1,0:T(8,128)(2,1)}, bf16[384,512]{1,0:T(8,128)(2,1)S(1)}, u32[]{:S(2)}, u32[]{:S(2)}) collective-permute-start(bf16[384,512]{1,0:T(8,128)(2,1)} %get-tuple-element.266.x), channel_id=1, source_target_pairs={{0,1},{1,0},{2,3},{3,2},{4,5},{5,4},{6,7},{7,6},{8,9},{9,8},{10,11... | collective-permute-start | bytes 1179656 | tf_op jit(solution)/shard_map/cond/branch_6_fun/ppermute | solution.py:310
  5.2 1.6 %collective-permute-start.38 = (bf16[384,512]{1,0:T(8,128)(2,1)}, bf16[384,512]{1,0:T(8,128)(2,1)S(1)}, u32[]{:S(2)}, u32[]{:S(2)}) collective-permute-start(bf16[384,512]{1,0:T(8,128)(2,1)} %get-tuple-element.266.x), channel_id=1, source_target_pairs={{0,28},{4,24},{8,20},{12,16},{16,12},{20,8},{24,4},{28,0},{1,29},{... | collective-permute-start | bytes 1179656 | tf_op jit(solution)/shard_map/cond/branch_6_fun/ppermute | solution.py:309
  6.8 1.3 %compare_select_fusion.6.owner = s32[1,256]{1,0:T(1,128)S(1)} fusion(s32[1,256]{1,0:T(1,128)} %get-tuple-element.272, s32[]{:T(128)} %bitcast.18), kind=kLoop, calls=%fused_computation.6 | loop fusion | flops 512 | bytes 2052 | tf_op jit(solution)/shard_map/cond/branch_6_fun/jit(_where)/select_n | solution.py:312
  8.1 1.0 %collective-permute-start.37 = (s32[1,256]{1,0:T(1,128)S(1)}, s32[1,256]{1,0:T(1,128)S(1)}, u32[]{:S(2)}, u32[]{:S(2)}) collective-permute-start(s32[1,256]{1,0:T(1,128)S(1)} %compare_select_fusion.6.owner), channel_id=1, source_target_pairs={{0,4},{4,0},{8,12},{12,8},{16,20},{20,16},{24,28},{28,24},{1,5},{5... | collective-permute-start | bytes 3080 | tf_op jit(solution)/shard_map/cond/branch_6_fun/ppermute | solution.py:313
  9.1 0.0 copy-start.6
  9.1 0.0 copy-start.13
  9.1 0.0 copy-start.20
  9.1 0.0 copy-start.41
  9.1 3.1 %branch_6_fun.7.g0 = f32[3,512,256]{2,1,0:T(8,128)S(1)} custom-call(bf16[384,512]{1,0:T(8,128)(2,1)} %get-tuple-element.266.x, bf16[512,512]{1,0:T(8,128)(2,1)} %get-tuple-element.267.dft, bf16[256,256]{1,0:T(8,128)(2,1)} %get-tuple-element.268.band, f32[256,128]{1,0:T(8,128)} %get-tuple-element.269.inverse, s32[1,256]{1,0:T(1,128)} %get-tuple-element.270.index), custom_call_target="tpu_custom_call" | custom-call | flops 1024 | bytes 1024 | tf_op jit(solution)/shard_map/cond/branch_6_fun/pallas_call | solution.py:269
  12.3 0.0 collective-permute-done.37.other_owner
  12.3 0.4 branch_6_fun.8
  12.7 1.9 %collective-permute-done.36.x = bf16[384,512]{1,0:T(8,128)(2,1)S(1)} collective-permute-done((bf16[384,512]{1,0:T(8,128)(2,1)}, bf16[384,512]{1,0:T(8,128)(2,1)S(1)}, u32[]{:S(2)}, u32[]{:S(2)}) %collective-permute-start.36) | collective-permute-done | bytes 393248 | tf_op jit(solution)/shard_map/cond/branch_6_fun/ppermute | solution.py:310
  14.6 0.0 copy-start.48
  14.6 1.2 %collective-permute-start.39 = (bf16[240,512]{1,0:T(8,128)(2,1)S(1)}, bf16[240,512]{1,0:T(8,128)(2,1)S(1)}, u32[]{:S(2)}, u32[]{:S(2)}) collective-permute-start(bf16[240,512]{1,0:T(8,128)(2,1)S(1)} %slice.58), channel_id=1, source_target_pairs={{0,28},{4,24},{8,20},{12,16},{16,12},{20,8},{24,4},{28,0},{1,29},{... | collective-permute-start | bytes 737288 | tf_op jit(solution)/shard_map/cond/branch_6_fun/ppermute | solution.py:320
  15.8 1.8 %collective-permute-done.38.x = bf16[384,512]{1,0:T(8,128)(2,1)S(1)} collective-permute-done((bf16[384,512]{1,0:T(8,128)(2,1)}, bf16[384,512]{1,0:T(8,128)(2,1)S(1)}, u32[]{:S(2)}, u32[]{:S(2)}) %collective-permute-start.38) | collective-permute-done | bytes 393248 | tf_op jit(solution)/shard_map/cond/branch_6_fun/ppermute | solution.py:309
  17.6 0.1 collective-permute-start.40
  17.7 0.0 copy-done.6
  17.7 0.0 copy-done.13
  17.7 0.0 copy-done.20
  17.7 0.0 copy-done.41
  17.7 1.9 %branch_6_fun.9.g1 = f32[3,512,256]{2,1,0:T(8,128)S(1)} custom-call(bf16[384,512]{1,0:T(8,128)(2,1)S(1)} %collective-permute-done.36.x, bf16[512,512]{1,0:T(8,128)(2,1)S(1)} %copy-done.6, bf16[256,256]{1,0:T(8,128)(2,1)S(1)} %copy-done.20, f32[256,128]{1,0:T(8,128)S(1)} %copy-done.13, s32[1,256]{1,0:T(1,128)S(1)} %copy-done.41), custom_call_target="tpu_custom_call" | custom-call | flops 1024 | bytes 1024 | tf_op jit(solution)/shard_map/cond/branch_6_fun/pallas_call | solution.py:269
  19.6 0.0 copy-done.48
  19.6 1.9 %branch_6_fun.10.h0 = f32[3,512,256]{2,1,0:T(8,128)S(1)} custom-call(bf16[384,512]{1,0:T(8,128)(2,1)S(1)} %collective-permute-done.38.x, bf16[512,512]{1,0:T(8,128)(2,1)S(1)} %copy-done.6, bf16[256,256]{1,0:T(8,128)(2,1)S(1)} %copy-done.20, f32[256,128]{1,0:T(8,128)S(1)} %copy-done.13, s32[1,256]{1,0:T(1,128)S(1)} %copy-done.48), custom_call_target="tpu_custom_call" | custom-call | flops 1024 | bytes 1024 | tf_op jit(solution)/shard_map/cond/branch_6_fun/pallas_call | solution.py:269
  21.5 0.0 copy-start.27
  21.5 0.0 copy-start.34
  21.5 0.5 branch_6_fun.11.x0
  22.0 1.5 %collective-permute-done.40.xb = bf16[144,512]{1,0:T(8,128)(2,1)S(1)} collective-permute-done((bf16[144,512]{1,0:T(8,128)(2,1)S(1)}, bf16[144,512]{1,0:T(8,128)(2,1)S(1)}, u32[]{:S(2)}, u32[]{:S(2)}) %collective-permute-start.40) | collective-permute-done | bytes 147488 | tf_op jit(solution)/shard_map/cond/branch_6_fun/ppermute | solution.py:321
  23.5 0.0 collective-permute-done.39.xa
  23.5 0.0 copy-done.27
  23.5 0.0 copy-done.34
  23.6 2.9 %branch_6_fun.12 = (bf16[1,192,256]{2,1,0:T(8,128)(2,1)S(1)}, bf16[1,384,256]{2,1,0:T(8,128)(2,1)S(1)}, f32[3,512,256]{2,1,0:T(8,128)S(1)}) custom-call(f32[3,512,256]{2,1,0:T(8,128)S(1)} %branch_6_fun.11.x0, f32[3,512,256]{2,1,0:T(8,128)S(1)} %branch_6_fun.9.g1, bf16[240,512]{1,0:T(8,128)(2,1)S(1)} %collective-permute-done.39.xa, ...), custom_call_target="tpu_custom_call" | custom-call | flops 1024 | bytes 1024 | tf_op jit(solution)/shard_map/cond/branch_6_fun/pallas_call | solution.py:269
  26.5 2.9 %collective-permute-start.41 = (bf16[192,256]{1,0:T(8,128)(2,1)S(1)}, bf16[192,256]{1,0:T(8,128)(2,1)}, u32[]{:S(2)}, u32[]{:S(2)}) collective-permute-start(bf16[192,256]{1,0:T(8,128)(2,1)S(1)} %bitcast.33), channel_id=1, source_target_pairs={{0,2},{1,3},{2,0},{3,1},{4,6},{5,7},{6,4},{7,5},{8,10},{9,11},{10,... | collective-permute-start | bytes 294920 | tf_op jit(solution)/shard_map/cond/branch_6_fun/ppermute | solution.py:350
  29.4 1.9 %branch_6_fun.13 = (f32[192,256]{1,0:T(8,128)S(1)}, f32[384,256]{1,0:T(8,128)S(1)}) custom-call(f32[3,512,256]{2,1,0:T(8,128)S(1)} %branch_6_fun.7.g0, f32[3,512,256]{2,1,0:T(8,128)S(1)} %branch_6_fun.10.h0, f32[3,512,256]{2,1,0:T(8,128)S(1)} %branch_6_fun.9.g1, f32[3,512,256]{2,1,0:T(8,128)S(1)} %get-tuple-element.281.h1, bf16[256,512]{1,0:T(8,128)(2,1)S(1)} %copy-done.34, ...), custom_call_target="tpu_custom_call" | custom-call | flops 1024 | bytes 1024 | tf_op jit(solution)/shard_map/cond/branch_6_fun/pallas_call | solution.py:269
  31.3 3.4 %collective-permute-done.41 = bf16[192,256]{1,0:T(8,128)(2,1)} collective-permute-done((bf16[192,256]{1,0:T(8,128)(2,1)S(1)}, bf16[192,256]{1,0:T(8,128)(2,1)}, u32[]{:S(2)}, u32[]{:S(2)}) %collective-permute-start.41) | collective-permute-done | bytes 98336 | tf_op jit(solution)/shard_map/cond/branch_6_fun/ppermute | solution.py:350
  34.7 0.6 %collective-permute-start.46 = (bf16[384,256]{1,0:T(8,128)(2,1)S(1)}, bf16[384,256]{1,0:T(8,128)(2,1)S(1)}, u32[]{:S(2)}, u32[]{:S(2)}) collective-permute-start(bf16[384,256]{1,0:T(8,128)(2,1)S(1)} %bitcast.41), channel_id=1, source_target_pairs={{0,2},{1,3},{2,0},{3,1},{4,6},{5,7},{6,4},{7,5},{8,10},{9,11},{10,... | collective-permute-start | bytes 589832 | tf_op jit(solution)/shard_map/ppermute | solution.py:350
  35.3 0.9 %shard_map.109.total = bf16[192,256]{1,0:T(8,128)(2,1)S(1)} custom-call(f32[192,256]{1,0:T(8,128)S(1)} %get-tuple-element.301.own, bf16[1,192,256]{2,1,0:T(8,128)(2,1)} %get-tuple-element.302.received), custom_call_target="tpu_custom_call" | custom-call | flops 1024 | bytes 1024 | tf_op jit(solution)/shard_map/pallas_call | solution.py:269
  36.3 0.1 collective-permute-start.42
  36.3 1.3 %collective-permute-done.42.other = bf16[192,256]{1,0:T(8,128)(2,1)S(1)} collective-permute-done((bf16[192,256]{1,0:T(8,128)(2,1)S(1)}, bf16[192,256]{1,0:T(8,128)(2,1)S(1)}, u32[]{:S(2)}, u32[]{:S(2)}) %collective-permute-start.42) | collective-permute-done | bytes 98336 | tf_op jit(solution)/shard_map/ppermute | solution.py:365
  37.6 0.3 shard_map.110
  38.0 0.6 %collective-permute-start.43 = (bf16[192,128]{1,0:T(8,128)(2,1)S(1)}, bf16[192,128]{1,0:T(8,128)(2,1)S(1)}, u32[]{:S(2)}, u32[]{:S(2)}) collective-permute-start(bf16[192,128]{1,0:T(8,128)(2,1)S(1)} %get-tuple-element.305), channel_id=1, source_target_pairs={{0,8},{4,12},{8,0},{12,4},{16,24},{20,28},{24,16},{28,20},{1,9},{5... | collective-permute-start | bytes 147464 | tf_op jit(solution)/shard_map/ppermute | solution.py:367
  38.5 1.6 %collective-permute-start.44 = (bf16[192,128]{1,0:T(8,128)(2,1)S(1)}, bf16[192,128]{1,0:T(8,128)(2,1)S(1)}, u32[]{:S(2)}, u32[]{:S(2)}) collective-permute-start(bf16[192,128]{1,0:T(8,128)(2,1)S(1)} %get-tuple-element.306), channel_id=1, source_target_pairs={{0,16},{4,20},{8,24},{12,28},{16,0},{20,4},{24,8},{28,12},{1,17},{... | collective-permute-start | bytes 147464 | tf_op jit(solution)/shard_map/ppermute | solution.py:367
  40.1 1.4 %collective-permute-start.45 = (bf16[192,128]{1,0:T(8,128)(2,1)S(1)}, bf16[192,128]{1,0:T(8,128)(2,1)S(1)}, u32[]{:S(2)}, u32[]{:S(2)}) collective-permute-start(bf16[192,128]{1,0:T(8,128)(2,1)S(1)} %get-tuple-element.307), channel_id=1, source_target_pairs={{0,24},{4,28},{8,16},{12,20},{16,8},{20,12},{24,0},{28,4},{1,25},{... | collective-permute-start | bytes 147464 | tf_op jit(solution)/shard_map/ppermute | solution.py:367
  41.5 0.6 %collective-permute-done.43.refs_1_ = bf16[192,128]{1,0:T(8,128)(2,1)S(1)} collective-permute-done((bf16[192,128]{1,0:T(8,128)(2,1)S(1)}, bf16[192,128]{1,0:T(8,128)(2,1)S(1)}, u32[]{:S(2)}, u32[]{:S(2)}) %collective-permute-start.43) | collective-permute-done | bytes 49184 | tf_op jit(solution)/shard_map/ppermute | solution.py:367
  42.1 0.5 collective-permute-done.44.refs_2_
  42.6 2.5 %collective-permute-done.45.refs_3_ = bf16[192,128]{1,0:T(8,128)(2,1)S(1)} collective-permute-done((bf16[192,128]{1,0:T(8,128)(2,1)S(1)}, bf16[192,128]{1,0:T(8,128)(2,1)S(1)}, u32[]{:S(2)}, u32[]{:S(2)}) %collective-permute-start.45) | collective-permute-done | bytes 49184 | tf_op jit(solution)/shard_map/ppermute | solution.py:367
  45.1 1.0 %collective-permute-done.46 = bf16[384,256]{1,0:T(8,128)(2,1)S(1)} collective-permute-done((bf16[384,256]{1,0:T(8,128)(2,1)S(1)}, bf16[384,256]{1,0:T(8,128)(2,1)S(1)}, u32[]{:S(2)}, u32[]{:S(2)}) %collective-permute-start.46) | collective-permute-done | bytes 196640 | tf_op jit(solution)/shard_map/ppermute | solution.py:350
  46.2 0.1 collective-permute-start.47
  46.3 1.4 %collective-permute-done.47.other = bf16[384,256]{1,0:T(8,128)(2,1)S(1)} collective-permute-done((bf16[384,256]{1,0:T(8,128)(2,1)S(1)}, bf16[384,256]{1,0:T(8,128)(2,1)S(1)}, u32[]{:S(2)}, u32[]{:S(2)}) %collective-permute-start.47) | collective-permute-done | bytes 196640 | tf_op jit(solution)/shard_map/ppermute | solution.py:365
  47.7 0.4 shard_map.112
  48.1 0.1 collective-permute-start.48
  48.2 0.9 %collective-permute-start.49 = (bf16[384,128]{1,0:T(8,128)(2,1)S(1)}, bf16[384,128]{1,0:T(8,128)(2,1)S(1)}, u32[]{:S(2)}, u32[]{:S(2)}) collective-permute-start(bf16[384,128]{1,0:T(8,128)(2,1)S(1)} %get-tuple-element.312), channel_id=1, source_target_pairs={{0,16},{4,20},{8,24},{12,28},{16,0},{20,4},{24,8},{28,12},{1,17},{... | collective-permute-start | bytes 294920 | tf_op jit(solution)/shard_map/ppermute | solution.py:367
  49.1 2.6 %collective-permute-start.50 = (bf16[384,128]{1,0:T(8,128)(2,1)S(1)}, bf16[384,128]{1,0:T(8,128)(2,1)S(1)}, u32[]{:S(2)}, u32[]{:S(2)}) collective-permute-start(bf16[384,128]{1,0:T(8,128)(2,1)S(1)} %get-tuple-element.313), channel_id=1, source_target_pairs={{0,24},{4,28},{8,16},{12,20},{16,8},{20,12},{24,0},{28,4},{1,25},{... | collective-permute-start | bytes 294920 | tf_op jit(solution)/shard_map/ppermute | solution.py:367
  51.7 0.8 %shard_map.113.refs_4_ = f32[576,512]{1,0:T(8,128)} custom-call(bf16[192,128]{1,0:T(8,128)(2,1)S(1)} %get-tuple-element.304.refs_0_, bf16[192,128]{1,0:T(8,128)(2,1)S(1)} %collective-permute-done.43.refs_1_, bf16[192,128]{1,0:T(8,128)(2,1)S(1)} %collective-permute-done.44.refs_2_, bf16[192,128]{1,0:T(8,128)(2,1)S(1)} %collective-permute-done.45.refs_3_), custom_call_target="tpu_custom_call" | custom-call | flops 1024 | bytes 1024 | tf_op jit(solution)/shard_map/pallas_call | solution.py:255
  52.5 1.4 %collective-permute-done.48.refs_1_ = bf16[384,128]{1,0:T(8,128)(2,1)S(1)} collective-permute-done((bf16[384,128]{1,0:T(8,128)(2,1)S(1)}, bf16[384,128]{1,0:T(8,128)(2,1)S(1)}, u32[]{:S(2)}, u32[]{:S(2)}) %collective-permute-start.48) | collective-permute-done | bytes 98336 | tf_op jit(solution)/shard_map/ppermute | solution.py:367
  53.8 1.4 %collective-permute-done.49.refs_2_ = bf16[384,128]{1,0:T(8,128)(2,1)S(1)} collective-permute-done((bf16[384,128]{1,0:T(8,128)(2,1)S(1)}, bf16[384,128]{1,0:T(8,128)(2,1)S(1)}, u32[]{:S(2)}, u32[]{:S(2)}) %collective-permute-start.49) | collective-permute-done | bytes 98336 | tf_op jit(solution)/shard_map/ppermute | solution.py:367
  55.2 0.0 collective-permute-done.50.refs_3_
  55.2 0.9 %shard_map.114 = f32[576,512]{1,0:T(8,128)} custom-call(bf16[384,128]{1,0:T(8,128)(2,1)S(1)} %get-tuple-element.310.refs_0_, bf16[384,128]{1,0:T(8,128)(2,1)S(1)} %collective-permute-done.48.refs_1_, bf16[384,128]{1,0:T(8,128)(2,1)S(1)} %collective-permute-done.49.refs_2_, ...), custom_call_target="tpu_custom_call", output_to_operand_aliasing={{}: (4, {})} | custom-call | flops 1024 | bytes 1024 | tf_op jit(solution)/shard_map/pallas_call | solution.py:255
  (3 shorter events, 0.1 us)
Async XLA Ops:
  2.1 12.4 %collective-permute-start.36 = (bf16[384,512]{1,0:T(8,128)(2,1)}, bf16[384,512]{1,0:T(8,128)(2,1)S(1)}, u32[]{:S(2)}, u32[]{:S(2)}) collective-permute-start(bf16[384,512]{1,0:T(8,128)(2,1)} %get-tuple-element.266.x), channel_id=1, source_target_pairs={{0,1},{1,0},{2,3},{3,2},{4,5},{5,4},{6,7},{7,6},{8,9},{9,8},{10,11... | collective-permute-start | bytes 1179656 | tf_op jit(solution)/shard_map/cond/branch_6_fun/ppermute | solution.py:310
  5.2 12.4 %collective-permute-start.38 = (bf16[384,512]{1,0:T(8,128)(2,1)}, bf16[384,512]{1,0:T(8,128)(2,1)S(1)}, u32[]{:S(2)}, u32[]{:S(2)}) collective-permute-start(bf16[384,512]{1,0:T(8,128)(2,1)} %get-tuple-element.266.x), channel_id=1, source_target_pairs={{0,28},{4,24},{8,20},{12,16},{16,12},{20,8},{24,4},{28,0},{1,29},{... | collective-permute-start | bytes 1179656 | tf_op jit(solution)/shard_map/cond/branch_6_fun/ppermute | solution.py:309
  8.1 4.1 %collective-permute-start.37 = (s32[1,256]{1,0:T(1,128)S(1)}, s32[1,256]{1,0:T(1,128)S(1)}, u32[]{:S(2)}, u32[]{:S(2)}) collective-permute-start(s32[1,256]{1,0:T(1,128)S(1)} %compare_select_fusion.6.owner), channel_id=1, source_target_pairs={{0,4},{4,0},{8,12},{12,8},{16,20},{20,16},{24,28},{28,24},{1,5},{5... | collective-permute-start | bytes 3080 | tf_op jit(solution)/shard_map/cond/branch_6_fun/ppermute | solution.py:313
  9.1 8.6 %copy-start.6 = (bf16[512,512]{1,0:T(8,128)(2,1)S(1)}, bf16[512,512]{1,0:T(8,128)(2,1)}, u32[]{:S(2)}) copy-start(bf16[512,512]{1,0:T(8,128)(2,1)} %get-tuple-element.267.dft) | copy-start | bytes 1572868 | tf_op jit(solution)/shard_map/cond
  9.1 8.6 %copy-start.13 = (f32[256,128]{1,0:T(8,128)S(1)}, f32[256,128]{1,0:T(8,128)}, u32[]{:S(2)}) copy-start(f32[256,128]{1,0:T(8,128)} %get-tuple-element.269.inverse) | copy-start | bytes 393220 | tf_op jit(solution)/shard_map/cond
  9.1 8.6 %copy-start.20 = (bf16[256,256]{1,0:T(8,128)(2,1)S(1)}, bf16[256,256]{1,0:T(8,128)(2,1)}, u32[]{:S(2)}) copy-start(bf16[256,256]{1,0:T(8,128)(2,1)} %get-tuple-element.268.band) | copy-start | bytes 393220 | tf_op jit(solution)/shard_map/cond
  9.1 8.6 %copy-start.41 = (s32[1,256]{1,0:T(1,128)S(1)}, s32[1,256]{1,0:T(1,128)}, u32[]{:S(2)}) copy-start(s32[1,256]{1,0:T(1,128)} %get-tuple-element.270.index) | copy-start | bytes 3076 | tf_op jit(solution)/shard_map/cond
  14.6 5.0 %copy-start.48 = (s32[1,256]{1,0:T(1,128)S(1)}, s32[1,256]{1,0:T(1,128)}, u32[]{:S(2)}) copy-start(s32[1,256]{1,0:T(1,128)} %get-tuple-element.275.index) | copy-start | bytes 3076 | tf_op jit(solution)/shard_map/cond
  14.6 9.0 %collective-permute-start.39 = (bf16[240,512]{1,0:T(8,128)(2,1)S(1)}, bf16[240,512]{1,0:T(8,128)(2,1)S(1)}, u32[]{:S(2)}, u32[]{:S(2)}) collective-permute-start(bf16[240,512]{1,0:T(8,128)(2,1)S(1)} %slice.58), channel_id=1, source_target_pairs={{0,28},{4,24},{8,20},{12,16},{16,12},{20,8},{24,4},{28,0},{1,29},{... | collective-permute-start | bytes 737288 | tf_op jit(solution)/shard_map/cond/branch_6_fun/ppermute | solution.py:320
  17.6 5.9 %collective-permute-start.40 = (bf16[144,512]{1,0:T(8,128)(2,1)S(1)}, bf16[144,512]{1,0:T(8,128)(2,1)S(1)}, u32[]{:S(2)}, u32[]{:S(2)}) collective-permute-start(bf16[144,512]{1,0:T(8,128)(2,1)S(1)} %slice.59), channel_id=1, source_target_pairs={{0,1},{1,0},{2,3},{3,2},{4,5},{5,4},{6,7},{7,6},{8,9},{9,8},{10,11... | collective-permute-start | bytes 442376 | tf_op jit(solution)/shard_map/cond/branch_6_fun/ppermute | solution.py:321
  21.5 2.1 %copy-start.27 = (bf16[256,512]{1,0:T(8,128)(2,1)S(1)}, bf16[256,512]{1,0:T(8,128)(2,1)}, u32[]{:S(2)}) copy-start(bf16[256,512]{1,0:T(8,128)(2,1)} %get-tuple-element.279.low_table) | copy-start | bytes 786436 | tf_op jit(solution)/shard_map/cond
  21.5 2.1 %copy-start.34 = (bf16[256,512]{1,0:T(8,128)(2,1)S(1)}, bf16[256,512]{1,0:T(8,128)(2,1)}, u32[]{:S(2)}) copy-start(bf16[256,512]{1,0:T(8,128)(2,1)} %get-tuple-element.278.high_table) | copy-start | bytes 786436 | tf_op jit(solution)/shard_map/cond
  26.5 8.2 %collective-permute-start.41 = (bf16[192,256]{1,0:T(8,128)(2,1)S(1)}, bf16[192,256]{1,0:T(8,128)(2,1)}, u32[]{:S(2)}, u32[]{:S(2)}) collective-permute-start(bf16[192,256]{1,0:T(8,128)(2,1)S(1)} %bitcast.33), channel_id=1, source_target_pairs={{0,2},{1,3},{2,0},{3,1},{4,6},{5,7},{6,4},{7,5},{8,10},{9,11},{10,... | collective-permute-start | bytes 294920 | tf_op jit(solution)/shard_map/cond/branch_6_fun/ppermute | solution.py:350
  34.7 11.5 %collective-permute-start.46 = (bf16[384,256]{1,0:T(8,128)(2,1)S(1)}, bf16[384,256]{1,0:T(8,128)(2,1)S(1)}, u32[]{:S(2)}, u32[]{:S(2)}) collective-permute-start(bf16[384,256]{1,0:T(8,128)(2,1)S(1)} %bitcast.41), channel_id=1, source_target_pairs={{0,2},{1,3},{2,0},{3,1},{4,6},{5,7},{6,4},{7,5},{8,10},{9,11},{10,... | collective-permute-start | bytes 589832 | tf_op jit(solution)/shard_map/ppermute | solution.py:350
  36.3 1.4 %collective-permute-start.42 = (bf16[192,256]{1,0:T(8,128)(2,1)S(1)}, bf16[192,256]{1,0:T(8,128)(2,1)S(1)}, u32[]{:S(2)}, u32[]{:S(2)}) collective-permute-start(bf16[192,256]{1,0:T(8,128)(2,1)S(1)} %shard_map.109.total), channel_id=1, source_target_pairs={{0,4},{4,0},{8,12},{12,8},{16,20},{20,16},{24,28},{28,24},{1,5},{5... | collective-permute-start | bytes 294920 | tf_op jit(solution)/shard_map/ppermute | solution.py:365
  38.0 4.2 %collective-permute-start.43 = (bf16[192,128]{1,0:T(8,128)(2,1)S(1)}, bf16[192,128]{1,0:T(8,128)(2,1)S(1)}, u32[]{:S(2)}, u32[]{:S(2)}) collective-permute-start(bf16[192,128]{1,0:T(8,128)(2,1)S(1)} %get-tuple-element.305), channel_id=1, source_target_pairs={{0,8},{4,12},{8,0},{12,4},{16,24},{20,28},{24,16},{28,20},{1,9},{5... | collective-permute-start | bytes 147464 | tf_op jit(solution)/shard_map/ppermute | solution.py:367
  38.5 4.1 %collective-permute-start.44 = (bf16[192,128]{1,0:T(8,128)(2,1)S(1)}, bf16[192,128]{1,0:T(8,128)(2,1)S(1)}, u32[]{:S(2)}, u32[]{:S(2)}) collective-permute-start(bf16[192,128]{1,0:T(8,128)(2,1)S(1)} %get-tuple-element.306), channel_id=1, source_target_pairs={{0,16},{4,20},{8,24},{12,28},{16,0},{20,4},{24,8},{28,12},{1,17},{... | collective-permute-start | bytes 147464 | tf_op jit(solution)/shard_map/ppermute | solution.py:367
  40.1 5.0 %collective-permute-start.45 = (bf16[192,128]{1,0:T(8,128)(2,1)S(1)}, bf16[192,128]{1,0:T(8,128)(2,1)S(1)}, u32[]{:S(2)}, u32[]{:S(2)}) collective-permute-start(bf16[192,128]{1,0:T(8,128)(2,1)S(1)} %get-tuple-element.307), channel_id=1, source_target_pairs={{0,24},{4,28},{8,16},{12,20},{16,8},{20,12},{24,0},{28,4},{1,25},{... | collective-permute-start | bytes 147464 | tf_op jit(solution)/shard_map/ppermute | solution.py:367
  46.2 1.5 %collective-permute-start.47 = (bf16[384,256]{1,0:T(8,128)(2,1)S(1)}, bf16[384,256]{1,0:T(8,128)(2,1)S(1)}, u32[]{:S(2)}, u32[]{:S(2)}) collective-permute-start(bf16[384,256]{1,0:T(8,128)(2,1)S(1)} %shard_map.111.total), channel_id=1, source_target_pairs={{0,4},{4,0},{8,12},{12,8},{16,20},{20,16},{24,28},{28,24},{1,5},{5... | collective-permute-start | bytes 589832 | tf_op jit(solution)/shard_map/ppermute | solution.py:365
  48.1 5.7 %collective-permute-start.48 = (bf16[384,128]{1,0:T(8,128)(2,1)S(1)}, bf16[384,128]{1,0:T(8,128)(2,1)S(1)}, u32[]{:S(2)}, u32[]{:S(2)}) collective-permute-start(bf16[384,128]{1,0:T(8,128)(2,1)S(1)} %get-tuple-element.311), channel_id=1, source_target_pairs={{0,8},{4,12},{8,0},{12,4},{16,24},{20,28},{24,16},{28,20},{1,9},{5... | collective-permute-start | bytes 294920 | tf_op jit(solution)/shard_map/ppermute | solution.py:367
  48.2 7.0 %collective-permute-start.49 = (bf16[384,128]{1,0:T(8,128)(2,1)S(1)}, bf16[384,128]{1,0:T(8,128)(2,1)S(1)}, u32[]{:S(2)}, u32[]{:S(2)}) collective-permute-start(bf16[384,128]{1,0:T(8,128)(2,1)S(1)} %get-tuple-element.312), channel_id=1, source_target_pairs={{0,16},{4,20},{8,24},{12,28},{16,0},{20,4},{24,8},{28,12},{1,17},{... | collective-permute-start | bytes 294920 | tf_op jit(solution)/shard_map/ppermute | solution.py:367
  49.1 6.1 %collective-permute-start.50 = (bf16[384,128]{1,0:T(8,128)(2,1)S(1)}, bf16[384,128]{1,0:T(8,128)(2,1)S(1)}, u32[]{:S(2)}, u32[]{:S(2)}) collective-permute-start(bf16[384,128]{1,0:T(8,128)(2,1)S(1)} %get-tuple-element.313), channel_id=1, source_target_pairs={{0,24},{4,28},{8,16},{12,20},{16,8},{20,12},{24,0},{28,4},{1,25},{... | collective-permute-start | bytes 294920 | tf_op jit(solution)/shard_map/ppermute | solution.py:367

commit v4 on v3

--- a/solution.py
+++ b/solution.py
@@ -110,12 +110,17 @@
     return ac // 3, ac % 3
 
 
-def over_rows(freqs, body):
+def over(count, size, body, unrolled=False):
+    if unrolled:
+        for i in range(count):
+            body(i, i * size)
+        return
+
     def step(i, carry):
-        body(pl.multiple_of(i * STEP, STEP))
+        body(i, pl.multiple_of(i * size, size))
         return carry
 
-    lax.fori_loop(0, freqs // STEP, step, 0)
+    lax.fori_loop(0, count, step, 0)
 
 
 def cross_kernel(width, blocks, sends, g0, h0, out):
@@ -125,28 +130,28 @@
         first = ((lax.axis_index("tm") ^ (2 * (i // blocks + 1))) * width) // LAGS
         a, c = component_pair(first, i % blocks)
 
-        def rows(r):
+        def rows(_, r):
             real, imag = cross_rows((g0,), (h0,), a, c, r, 0.0, 0.0)
             out[i, pl.ds(r, STEP)] = real
             out[i, pl.ds(freqs + r, STEP)] = imag
 
-        over_rows(freqs, rows)
+        over(freqs // STEP, STEP, rows)
         return carry
 
     lax.fori_loop(0, sends * blocks, block, 0)
 
 
-def lag_block(lefts, rights, base, a, c, high_table, low_table, cross_high, cross_low):
+def lag_block(lefts, rights, base, a, c, high_table, low_table, cross_high, cross_low, unrolled):
     freqs = lefts[0].shape[1] // 2
 
-    def rows(r):
+    def rows(_, r):
         near, far = pl.ds(r, STEP), pl.ds(freqs + r, STEP)
         real, imag = (0.0, 0.0) if base is None else (base[near], base[far])
         real, imag = cross_rows(lefts, rights, a, c, r, real, imag)
         cross_high[near], cross_low[near] = split(real)
         cross_high[far], cross_low[far] = split(imag)
 
-    over_rows(freqs, rows)
+    over(freqs // STEP, STEP, rows, unrolled)
     return (
         jnp.dot(high_table[...], cross_high[...], preferred_element_type=F32)
         + jnp.dot(low_table[...], cross_high[...], preferred_element_type=F32)
@@ -154,18 +159,20 @@
     )
 
 
-def piece(k_piece, width, blocks, lefts, rights, base, lagged, high_table, low_table, cross_high, cross_low):
-    start = k_piece * width
+def piece(
+    number, width, blocks, lefts, rights, base, lagged, high_table, low_table, cross_high, cross_low, unrolled
+):
+    start = number * width
     first = start // LAGS
 
-    def block(j, carry):
+    def block(j, row):
         a, c = component_pair(first, j)
-        lagged[pl.ds(pl.multiple_of(j * LAGS, LAGS), LAGS)] = lag_block(
-            lefts, rights, None if base is None else base.at[j], a, c, high_table, low_table, cross_high, cross_low
-        )
-        return carry
-
-    lax.fori_loop(0, blocks, block, 0)
+        lagged[pl.ds(row, LAGS)] = lag_block(
+            lefts, rights, None if base is None else base.at[j], a, c,
+            high_table, low_table, cross_high, cross_low, unrolled,
+        )
+
+    over(blocks, LAGS, block, unrolled)
     return start - first * LAGS
 
 
@@ -182,7 +189,7 @@
         base = x0.at[k * blocks : (k + 1) * blocks]
         shift = piece(
             lax.axis_index("tm") ^ (2 * (k + 1)), width, blocks, (g1,), (h1,), base, lagged,
-            high_table, low_table, cross_high, cross_low,
+            high_table, low_table, cross_high, cross_low, sends == 1,
         )
         out[k] = lagged[pl.ds(pl.multiple_of(shift, 16), rows)].astype(BF16)
         rest[k] = lagged[pl.ds(pl.multiple_of(shift + rows, 16), width - rows)].astype(BF16)
@@ -192,7 +199,8 @@
     width, blocks, g0, h0, g1, h1, high_table, low_table, out, rest, cross_high, cross_low, lagged
 ):
     shift = piece(
-        lax.axis_index("tm"), width, blocks, (g0, g1), (h0, h1), None, lagged, high_table, low_table, cross_high, cross_low
+        lax.axis_index("tm"), width, blocks, (g0, g1), (h0, h1), None, lagged,
+        high_table, low_table, cross_high, cross_low, False,
     )
     rows = out.shape[0]
     out[...] = lagged[pl.ds(pl.multiple_of(shift, 16), rows)]
@@ -289,7 +297,7 @@
     sends = tm_count // 2 - 1
     top = LAGS - math.gcd(width, LAGS)
     blocks = -(-(top + width) // LAGS)
-    rows = -(-width // 48) * 16
+    rows = width * 7 // 144 * 16
     scale = 1.0 / math.sqrt(freqs * seg_local * tm_count)
     dft, high_table, low_table, band, inverse = (jnp.asarray(a) for a in tables(samples, freqs, scale))
 
@@ -344,26 +352,28 @@
             (g0, h0, g1, h1, high_table, low_table),
             scratch,
         )
-        return received, rest, own, pick
+        return total(own[0], received), rest, own[1], pick
+
+    def total(mine, received):
+        shape = jax.ShapeDtypeStruct(mine.shape, BF16)
+        return call(total_kernel, shape, (mine, jnp.stack(received)))
 
     def exchange(part):
         return [lax.ppermute(part[j], "tm", xor_pairs(tm_count, 2 * (j + 1))) for j in range(sends)]
 
     scratch = [pltpu.VMEM((2 * freqs, pairs), BF16)] * 2 + [pltpu.VMEM((blocks * LAGS, pairs), F32)]
     branches = [functools.partial(gather, k) for k in range(1, sta_count)]
-    received, rest, own, pick = lax.switch(
-        partner[0, 0] - 1, branches, x, left_station, right_station, owner, pair_count
+    first, rest, own, pick = lax.switch(
+        partner.reshape(-1)[0] - 1, branches, x, left_station, right_station, owner, pair_count
     )
-    received = [received, exchange(rest)]
+    second = total(own, exchange(rest))
     lanes = 2 * capacity
     shape = jax.ShapeDtypeStruct((width, sta_count * capacity), F32)
-    parts, arrived, result = [], [], None
-    for got, mine in zip(received, own):
-        mine = lax.optimization_barrier((mine, *arrived))[0]
-        size = mine.shape[0]
-        total = call(total_kernel, jax.ShapeDtypeStruct((size, pairs), BF16), (mine, jnp.stack(got)))
-        other = lax.ppermute(total, "sta", xor_pairs(sta_count, 1))
-        routed = call(route_kernel, [jax.ShapeDtypeStruct((size, lanes), BF16)] * chips, (total, other, pick))
+    parts, result = [], None
+    for summed in (first, second):
+        size = summed.shape[0]
+        other = lax.ppermute(summed, "sta", xor_pairs(sta_count, 1))
+        routed = call(route_kernel, [jax.ShapeDtypeStruct((size, lanes), BF16)] * chips, (summed, other, pick))
         arrived = [lax.ppermute(routed[j], "sta", xor_pairs(sta_count, 2 * j)) for j in range(chips - 1, 0, -1)]
         arrived = [routed[0]] + arrived[::-1]
         if lanes % 128 == 0:

time: 56.6 us -> 54.9 us (0.970)
  Pallas kernels: 15.9 us -> 14.5 us
  waiting for transfers between devices: 18.7 us -> 19.9 us
  starting transfers between devices: 17.8 us -> 17.2 us
  between operations: 0.92 us -> 0.35 us
    ppermute x2, waiting for transfers between devices: 4.41 us -> 10.2 us  [exchange(): lax.ppermute(part[j], 'tm', xor_pairs(tm_count, 2 * (j + 1)))]
    ppermute x6, waiting for transfers between devices: 6.37 us -> 1.8 us  [local(): lax.ppermute(routed[j], 'sta', xor_pairs(sta_count, 2 * j))]
    pallas_call x11, Pallas kernels: 14.2 us -> 12.8 us  [call(): pl.pallas_call(kernel, out_shape=out_shape, in_specs=[pl.BlockSpec(memory...]
    slice x1 -> x0, local copies, waits for them, and re-layouts: 1.2 us -> none  [local(): partner[0, 0] - 1]
    reshape x0 -> x1, local copies, waits for them, and re-layouts: none -> 0.76 us  [local(): partner.reshape(-1)[0] - 1]
  transfers between devices with their start and end apart: 15 -> 15, of which waited for: 12 -> 8; matrix products, arithmetic and copies ran while one was open for 2% -> 2% of each run, Pallas kernels for 21% -> 21%
where the time goes in v4:
time: 54.9 us; the launch traced here: 55.1 us
  waiting for transfers between devices  19.9 us (36%)
  starting transfers between devices  17.2 us (31%)
  Pallas kernels  14.5 us (26%)
  other arithmetic  1.33 us (2%)
  loops' own time  0.97 us (2%)
  local copies, waits for them, and re-layouts  0.83 us (2%)
    pallas_call x11, Pallas kernels, call(): pl.pallas_call(kernel, out_shape=out_shape, in_specs=[pl.BlockSpec(memory...  12.8 us
    ppermute x2, waiting for transfers between devices, exchange(): lax.ppermute(part[j], 'tm', xor_pairs(tm_count, 2 * (j + 1)))  10.2 us
    ppermute x6, starting transfers between devices, local(): lax.ppermute(routed[j], 'sta', xor_pairs(sta_count, 2 * j))  7.11 us
    ppermute x1, starting transfers between devices, gather(): x_next = swap(x)  3.09 us
    ppermute x2, starting transfers between devices, exchange(): lax.ppermute(part[j], 'tm', xor_pairs(tm_count, 2 * (j + 1)))  3.01 us
    ppermute x2, waiting for transfers between devices, local(): other = lax.ppermute(summed, 'sta', xor_pairs(sta_count, 1))  2.64 us
    ppermute x1, waiting for transfers between devices, gather(): x_next = swap(x)  1.88 us
    ppermute x6, waiting for transfers between devices, local(): lax.ppermute(routed[j], 'sta', xor_pairs(sta_count, 2 * j))  1.8 us
  transfers between devices with their start and end apart: 15, of which 8 were waited for; matrix products, arithmetic and copies ran while one was open for 2% of the time, Pallas kernels for 21%

profile of v4, /device:TPU:0, one launch (start us, length us, event | category | flops | bytes accessed | tf_op | source)
XLA Modules:
  0.0 55.1 jit_solution(15889792506331175197)
XLA Ops:
  0.0 0.8 %reshape.67 = s32[56]{0:T(128)S(1)} reshape(s32[7,8]{1,0:T(8,128)} %param.19) | data formatting | bytes 448 | tf_op jit(solution)/shard_map/reshape | solution.py:367
  0.8 38.4 %conditional.1 = (bf16[448,256]{1,0:T(8,128)(2,1)S(1)}, bf16[1,128,256]{2,1,0:T(8,128)(2,1)S(1)}, f32[128,256]{1,0:T(8,128)S(1)}, bf16[512,512]{1,0:T(8,128)(2,1)S(1)}) conditional(s32[]{:T(128)} %bitcast.21, (bf16[384,512]{1,0:T(8,128)(2,1)}, bf16[512,512]{1,0:T(8,128)(2,1)}, bf16[256,256]{1,0:T(8,128)(2,1)}, ...), branch_computations={%region_0.1_spmd, %region_1.2_spmd, %region_2.3_spmd, %region_3.4_... | conditional | flops 8704 | bytes 11688408 | solution.py:366
  1.3 3.1 %collective-permute-start.36 = (bf16[384,512]{1,0:T(8,128)(2,1)}, bf16[384,512]{1,0:T(8,128)(2,1)S(1)}, u32[]{:S(2)}, u32[]{:S(2)}) collective-permute-start(bf16[384,512]{1,0:T(8,128)(2,1)} %get-tuple-element.265.x), channel_id=1, source_target_pairs={{0,1},{1,0},{2,3},{3,2},{4,5},{5,4},{6,7},{7,6},{8,9},{9,8},{10,11... | collective-permute-start | bytes 1179656 | tf_op jit(solution)/shard_map/cond/branch_6_fun/ppermute | solution.py:318
  4.4 1.6 %collective-permute-start.38 = (bf16[384,512]{1,0:T(8,128)(2,1)}, bf16[384,512]{1,0:T(8,128)(2,1)S(1)}, u32[]{:S(2)}, u32[]{:S(2)}) collective-permute-start(bf16[384,512]{1,0:T(8,128)(2,1)} %get-tuple-element.265.x), channel_id=1, source_target_pairs={{0,28},{4,24},{8,20},{12,16},{16,12},{20,8},{24,4},{28,0},{1,29},{... | collective-permute-start | bytes 1179656 | tf_op jit(solution)/shard_map/cond/branch_6_fun/ppermute | solution.py:317
  6.0 1.3 %compare_select_fusion.6.owner = s32[1,256]{1,0:T(1,128)S(1)} fusion(s32[1,256]{1,0:T(1,128)} %get-tuple-element.271, s32[]{:T(128)} %bitcast.18), kind=kLoop, calls=%fused_computation.6 | loop fusion | flops 512 | bytes 2052 | tf_op jit(solution)/shard_map/cond/branch_6_fun/jit(_where)/select_n | solution.py:320
  7.4 1.0 %collective-permute-start.37 = (s32[1,256]{1,0:T(1,128)S(1)}, s32[1,256]{1,0:T(1,128)S(1)}, u32[]{:S(2)}, u32[]{:S(2)}) collective-permute-start(s32[1,256]{1,0:T(1,128)S(1)} %compare_select_fusion.6.owner), channel_id=1, source_target_pairs={{0,4},{4,0},{8,12},{12,8},{16,20},{20,16},{24,28},{28,24},{1,5},{5... | collective-permute-start | bytes 3080 | tf_op jit(solution)/shard_map/cond/branch_6_fun/ppermute | solution.py:321
  8.3 0.0 copy-start.6
  8.3 0.0 copy-start.13
  8.3 0.0 copy-start.20
  8.3 0.0 copy-start.41
  8.3 3.2 %branch_6_fun.8.g0 = f32[3,512,256]{2,1,0:T(8,128)S(1)} custom-call(bf16[384,512]{1,0:T(8,128)(2,1)} %get-tuple-element.265.x, bf16[512,512]{1,0:T(8,128)(2,1)} %get-tuple-element.266.dft, bf16[256,256]{1,0:T(8,128)(2,1)} %get-tuple-element.267.band, f32[256,128]{1,0:T(8,128)} %get-tuple-element.268.inverse, s32[1,256]{1,0:T(1,128)} %get-tuple-element.269.index), custom_call_target="tpu_custom_call" | custom-call | flops 1024 | bytes 1024 | tf_op jit(solution)/shard_map/cond/branch_6_fun/pallas_call | solution.py:277
  11.5 0.0 collective-permute-done.37.other_owner
  11.5 0.4 branch_6_fun.9
  11.9 1.9 %collective-permute-done.36.x = bf16[384,512]{1,0:T(8,128)(2,1)S(1)} collective-permute-done((bf16[384,512]{1,0:T(8,128)(2,1)}, bf16[384,512]{1,0:T(8,128)(2,1)S(1)}, u32[]{:S(2)}, u32[]{:S(2)}) %collective-permute-start.36) | collective-permute-done | bytes 393248 | tf_op jit(solution)/shard_map/cond/branch_6_fun/ppermute | solution.py:318
  13.8 0.0 copy-start.48
  13.8 1.2 %collective-permute-start.39 = (bf16[240,512]{1,0:T(8,128)(2,1)S(1)}, bf16[240,512]{1,0:T(8,128)(2,1)S(1)}, u32[]{:S(2)}, u32[]{:S(2)}) collective-permute-start(bf16[240,512]{1,0:T(8,128)(2,1)S(1)} %slice.58), channel_id=1, source_target_pairs={{0,28},{4,24},{8,20},{12,16},{16,12},{20,8},{24,4},{28,0},{1,29},{... | collective-permute-start | bytes 737288 | tf_op jit(solution)/shard_map/cond/branch_6_fun/ppermute | solution.py:328
  15.0 1.8 %collective-permute-done.38.x = bf16[384,512]{1,0:T(8,128)(2,1)S(1)} collective-permute-done((bf16[384,512]{1,0:T(8,128)(2,1)}, bf16[384,512]{1,0:T(8,128)(2,1)S(1)}, u32[]{:S(2)}, u32[]{:S(2)}) %collective-permute-start.38) | collective-permute-done | bytes 393248 | tf_op jit(solution)/shard_map/cond/branch_6_fun/ppermute | solution.py:317
  16.8 0.1 collective-permute-start.40
  16.9 0.0 copy-done.6
  16.9 0.0 copy-done.13
  16.9 0.0 copy-done.20
  16.9 0.0 copy-done.41
  16.9 1.9 %branch_6_fun.10.g1 = f32[3,512,256]{2,1,0:T(8,128)S(1)} custom-call(bf16[384,512]{1,0:T(8,128)(2,1)S(1)} %collective-permute-done.36.x, bf16[512,512]{1,0:T(8,128)(2,1)S(1)} %copy-done.6, bf16[256,256]{1,0:T(8,128)(2,1)S(1)} %copy-done.20, f32[256,128]{1,0:T(8,128)S(1)} %copy-done.13, s32[1,256]{1,0:T(1,128)S(1)} %copy-done.41), custom_call_target="tpu_custom_call" | custom-call | flops 1024 | bytes 1024 | tf_op jit(solution)/shard_map/cond/branch_6_fun/pallas_call | solution.py:277
  18.8 0.0 copy-done.48
  18.8 1.9 %branch_6_fun.11.h0 = f32[3,512,256]{2,1,0:T(8,128)S(1)} custom-call(bf16[384,512]{1,0:T(8,128)(2,1)S(1)} %collective-permute-done.38.x, bf16[512,512]{1,0:T(8,128)(2,1)S(1)} %copy-done.6, bf16[256,256]{1,0:T(8,128)(2,1)S(1)} %copy-done.20, f32[256,128]{1,0:T(8,128)S(1)} %copy-done.13, s32[1,256]{1,0:T(1,128)S(1)} %copy-done.48), custom_call_target="tpu_custom_call" | custom-call | flops 1024 | bytes 1024 | tf_op jit(solution)/shard_map/cond/branch_6_fun/pallas_call | solution.py:277
  20.7 0.0 copy-start.27
  20.7 0.0 copy-start.34
  20.7 0.5 branch_6_fun.12.x0
  21.2 1.5 %collective-permute-done.40.xb = bf16[144,512]{1,0:T(8,128)(2,1)S(1)} collective-permute-done((bf16[144,512]{1,0:T(8,128)(2,1)S(1)}, bf16[144,512]{1,0:T(8,128)(2,1)S(1)}, u32[]{:S(2)}, u32[]{:S(2)}) %collective-permute-start.40) | collective-permute-done | bytes 147488 | tf_op jit(solution)/shard_map/cond/branch_6_fun/ppermute | solution.py:329
  22.8 0.0 collective-permute-done.39.xa
  22.8 0.0 copy-done.27
  22.8 0.0 copy-done.34
  22.8 2.3 %branch_6_fun.13 = (bf16[1,448,256]{2,1,0:T(8,128)(2,1)S(1)}, bf16[1,128,256]{2,1,0:T(8,128)(2,1)S(1)}, f32[3,512,256]{2,1,0:T(8,128)S(1)}) custom-call(f32[3,512,256]{2,1,0:T(8,128)S(1)} %branch_6_fun.12.x0, f32[3,512,256]{2,1,0:T(8,128)S(1)} %branch_6_fun.10.g1, bf16[240,512]{1,0:T(8,128)(2,1)S(1)} %collective-permute-done.39.xa, ...), custom_call_target="tpu_custom_call" | custom-call | flops 1024 | bytes 1024 | tf_op jit(solution)/shard_map/cond/branch_6_fun/pallas_call | solution.py:277
  25.1 2.9 %collective-permute-start.41 = (bf16[448,256]{1,0:T(8,128)(2,1)S(1)}, bf16[448,256]{1,0:T(8,128)(2,1)S(1)}, u32[]{:S(2)}, u32[]{:S(2)}) collective-permute-start(bf16[448,256]{1,0:T(8,128)(2,1)S(1)} %bitcast.41), channel_id=1, source_target_pairs={{0,2},{1,3},{2,0},{3,1},{4,6},{5,7},{6,4},{7,5},{8,10},{9,11},{10,... | collective-permute-start | bytes 688136 | tf_op jit(solution)/shard_map/cond/branch_6_fun/ppermute | solution.py:362
  28.1 1.9 %branch_6_fun.14 = (f32[448,256]{1,0:T(8,128)S(1)}, f32[128,256]{1,0:T(8,128)S(1)}) custom-call(f32[3,512,256]{2,1,0:T(8,128)S(1)} %branch_6_fun.8.g0, f32[3,512,256]{2,1,0:T(8,128)S(1)} %branch_6_fun.11.h0, f32[3,512,256]{2,1,0:T(8,128)S(1)} %branch_6_fun.10.g1, f32[3,512,256]{2,1,0:T(8,128)S(1)} %get-tuple-element.279.h1, bf16[256,512]{1,0:T(8,128)(2,1)S(1)} %copy-done.34, ...), custom_call_target="tpu_custom_call" | custom-call | flops 1024 | bytes 1024 | tf_op jit(solution)/shard_map/cond/branch_6_fun/pallas_call | solution.py:277
  30.0 8.9 %collective-permute-done.41 = bf16[448,256]{1,0:T(8,128)(2,1)S(1)} collective-permute-done((bf16[448,256]{1,0:T(8,128)(2,1)S(1)}, bf16[448,256]{1,0:T(8,128)(2,1)S(1)}, u32[]{:S(2)}, u32[]{:S(2)}) %collective-permute-start.41) | collective-permute-done | bytes 229408 | tf_op jit(solution)/shard_map/cond/branch_6_fun/ppermute | solution.py:362
  39.2 0.1 collective-permute-start.47
  39.3 0.1 collective-permute-start.42
  39.4 1.4 %collective-permute-done.47.other = bf16[448,256]{1,0:T(8,128)(2,1)S(1)} collective-permute-done((bf16[448,256]{1,0:T(8,128)(2,1)S(1)}, bf16[448,256]{1,0:T(8,128)(2,1)S(1)}, u32[]{:S(2)}, u32[]{:S(2)}) %collective-permute-start.47) | collective-permute-done | bytes 229408 | tf_op jit(solution)/shard_map/ppermute | solution.py:375
  40.8 0.4 shard_map.111
  41.2 0.2 collective-permute-start.48
  41.4 1.3 %collective-permute-start.49 = (bf16[448,128]{1,0:T(8,128)(2,1)S(1)}, bf16[448,128]{1,0:T(8,128)(2,1)S(1)}, u32[]{:S(2)}, u32[]{:S(2)}) collective-permute-start(bf16[448,128]{1,0:T(8,128)(2,1)S(1)} %get-tuple-element.307), channel_id=1, source_target_pairs={{0,16},{4,20},{8,24},{12,28},{16,0},{20,4},{24,8},{28,12},{1,17},{... | collective-permute-start | bytes 344072 | tf_op jit(solution)/shard_map/ppermute | solution.py:377
  42.7 2.0 %collective-permute-start.50 = (bf16[448,128]{1,0:T(8,128)(2,1)S(1)}, bf16[448,128]{1,0:T(8,128)(2,1)S(1)}, u32[]{:S(2)}, u32[]{:S(2)}) collective-permute-start(bf16[448,128]{1,0:T(8,128)(2,1)S(1)} %get-tuple-element.308), channel_id=1, source_target_pairs={{0,24},{4,28},{8,16},{12,20},{16,8},{20,12},{24,0},{28,4},{1,25},{... | collective-permute-start | bytes 344072 | tf_op jit(solution)/shard_map/ppermute | solution.py:377
  44.8 1.3 %collective-permute-done.42 = bf16[128,256]{1,0:T(8,128)(2,1)S(1)} collective-permute-done((bf16[128,256]{1,0:T(8,128)(2,1)S(1)}, bf16[128,256]{1,0:T(8,128)(2,1)S(1)}, u32[]{:S(2)}, u32[]{:S(2)}) %collective-permute-start.42) | collective-permute-done | bytes 65568 | tf_op jit(solution)/shard_map/ppermute | solution.py:362
  46.1 0.1 collective-permute-start.43
  46.2 1.2 %collective-permute-done.43.other = bf16[128,256]{1,0:T(8,128)(2,1)S(1)} collective-permute-done((bf16[128,256]{1,0:T(8,128)(2,1)S(1)}, bf16[128,256]{1,0:T(8,128)(2,1)S(1)}, u32[]{:S(2)}, u32[]{:S(2)}) %collective-permute-start.43) | collective-permute-done | bytes 65568 | tf_op jit(solution)/shard_map/ppermute | solution.py:375
  47.4 0.3 shard_map.110
  47.8 0.2 collective-permute-start.44
  48.0 1.3 %collective-permute-start.45 = (bf16[128,128]{1,0:T(8,128)(2,1)S(1)}, bf16[128,128]{1,0:T(8,128)(2,1)S(1)}, u32[]{:S(2)}, u32[]{:S(2)}) collective-permute-start(bf16[128,128]{1,0:T(8,128)(2,1)S(1)} %get-tuple-element.302), channel_id=1, source_target_pairs={{0,16},{4,20},{8,24},{12,28},{16,0},{20,4},{24,8},{28,12},{1,17},{... | collective-permute-start | bytes 98312 | tf_op jit(solution)/shard_map/ppermute | solution.py:377
  49.3 0.0 collective-permute-done.48.refs_1_
  49.3 2.0 %collective-permute-start.46 = (bf16[128,128]{1,0:T(8,128)(2,1)S(1)}, bf16[128,128]{1,0:T(8,128)(2,1)S(1)}, u32[]{:S(2)}, u32[]{:S(2)}) collective-permute-start(bf16[128,128]{1,0:T(8,128)(2,1)S(1)} %get-tuple-element.303), channel_id=1, source_target_pairs={{0,24},{4,28},{8,16},{12,20},{16,8},{20,12},{24,0},{28,4},{1,25},{... | collective-permute-start | bytes 98312 | tf_op jit(solution)/shard_map/ppermute | solution.py:377
  51.3 0.0 collective-permute-done.49.refs_2_
  51.3 0.0 collective-permute-done.50.refs_3_
  51.3 1.0 %shard_map.112.refs_4_ = f32[576,512]{1,0:T(8,128)} custom-call(bf16[448,128]{1,0:T(8,128)(2,1)S(1)} %get-tuple-element.305.refs_0_, bf16[448,128]{1,0:T(8,128)(2,1)S(1)} %collective-permute-done.48.refs_1_, bf16[448,128]{1,0:T(8,128)(2,1)S(1)} %collective-permute-done.49.refs_2_, bf16[448,128]{1,0:T(8,128)(2,1)S(1)} %collective-permute-done.50.refs_3_), custom_call_target="tpu_custom_call" | custom-call | flops 1024 | bytes 1024 | tf_op jit(solution)/shard_map/pallas_call | solution.py:263
  52.3 0.0 collective-permute-done.44.refs_1_
  52.3 0.0 collective-permute-done.45.refs_2_
  52.3 1.8 %collective-permute-done.46.refs_3_ = bf16[128,128]{1,0:T(8,128)(2,1)S(1)} collective-permute-done((bf16[128,128]{1,0:T(8,128)(2,1)S(1)}, bf16[128,128]{1,0:T(8,128)(2,1)S(1)}, u32[]{:S(2)}, u32[]{:S(2)}) %collective-permute-start.46) | collective-permute-done | bytes 32800 | tf_op jit(solution)/shard_map/ppermute | solution.py:377
  54.1 0.7 %shard_map.113 = f32[576,512]{1,0:T(8,128)} custom-call(bf16[128,128]{1,0:T(8,128)(2,1)S(1)} %get-tuple-element.300.refs_0_, bf16[128,128]{1,0:T(8,128)(2,1)S(1)} %collective-permute-done.44.refs_1_, bf16[128,128]{1,0:T(8,128)(2,1)S(1)} %collective-permute-done.45.refs_2_, ...), custom_call_target="tpu_custom_call", output_to_operand_aliasing={{}: (4, {})} | custom-call | flops 1024 | bytes 1024 | tf_op jit(solution)/shard_map/pallas_call | solution.py:263
  (4 shorter events, 0.1 us)
Async XLA Ops:
  1.3 12.4 %collective-permute-start.36 = (bf16[384,512]{1,0:T(8,128)(2,1)}, bf16[384,512]{1,0:T(8,128)(2,1)S(1)}, u32[]{:S(2)}, u32[]{:S(2)}) collective-permute-start(bf16[384,512]{1,0:T(8,128)(2,1)} %get-tuple-element.265.x), channel_id=1, source_target_pairs={{0,1},{1,0},{2,3},{3,2},{4,5},{5,4},{6,7},{7,6},{8,9},{9,8},{10,11... | collective-permute-start | bytes 1179656 | tf_op jit(solution)/shard_map/cond/branch_6_fun/ppermute | solution.py:318
  4.4 12.4 %collective-permute-start.38 = (bf16[384,512]{1,0:T(8,128)(2,1)}, bf16[384,512]{1,0:T(8,128)(2,1)S(1)}, u32[]{:S(2)}, u32[]{:S(2)}) collective-permute-start(bf16[384,512]{1,0:T(8,128)(2,1)} %get-tuple-element.265.x), channel_id=1, source_target_pairs={{0,28},{4,24},{8,20},{12,16},{16,12},{20,8},{24,4},{28,0},{1,29},{... | collective-permute-start | bytes 1179656 | tf_op jit(solution)/shard_map/cond/branch_6_fun/ppermute | solution.py:317
  7.4 4.1 %collective-permute-start.37 = (s32[1,256]{1,0:T(1,128)S(1)}, s32[1,256]{1,0:T(1,128)S(1)}, u32[]{:S(2)}, u32[]{:S(2)}) collective-permute-start(s32[1,256]{1,0:T(1,128)S(1)} %compare_select_fusion.6.owner), channel_id=1, source_target_pairs={{0,4},{4,0},{8,12},{12,8},{16,20},{20,16},{24,28},{28,24},{1,5},{5... | collective-permute-start | bytes 3080 | tf_op jit(solution)/shard_map/cond/branch_6_fun/ppermute | solution.py:321
  8.3 8.6 %copy-start.6 = (bf16[512,512]{1,0:T(8,128)(2,1)S(1)}, bf16[512,512]{1,0:T(8,128)(2,1)}, u32[]{:S(2)}) copy-start(bf16[512,512]{1,0:T(8,128)(2,1)} %get-tuple-element.266.dft) | copy-start | bytes 1572868 | tf_op jit(solution)/shard_map/cond
  8.3 8.6 %copy-start.13 = (f32[256,128]{1,0:T(8,128)S(1)}, f32[256,128]{1,0:T(8,128)}, u32[]{:S(2)}) copy-start(f32[256,128]{1,0:T(8,128)} %get-tuple-element.268.inverse) | copy-start | bytes 393220 | tf_op jit(solution)/shard_map/cond
  8.3 8.6 %copy-start.20 = (bf16[256,256]{1,0:T(8,128)(2,1)S(1)}, bf16[256,256]{1,0:T(8,128)(2,1)}, u32[]{:S(2)}) copy-start(bf16[256,256]{1,0:T(8,128)(2,1)} %get-tuple-element.267.band) | copy-start | bytes 393220 | tf_op jit(solution)/shard_map/cond
  8.3 8.6 %copy-start.41 = (s32[1,256]{1,0:T(1,128)S(1)}, s32[1,256]{1,0:T(1,128)}, u32[]{:S(2)}) copy-start(s32[1,256]{1,0:T(1,128)} %get-tuple-element.269.index) | copy-start | bytes 3076 | tf_op jit(solution)/shard_map/cond
  13.8 5.0 %copy-start.48 = (s32[1,256]{1,0:T(1,128)S(1)}, s32[1,256]{1,0:T(1,128)}, u32[]{:S(2)}) copy-start(s32[1,256]{1,0:T(1,128)} %get-tuple-element.274.index) | copy-start | bytes 3076 | tf_op jit(solution)/shard_map/cond
  13.8 9.0 %collective-permute-start.39 = (bf16[240,512]{1,0:T(8,128)(2,1)S(1)}, bf16[240,512]{1,0:T(8,128)(2,1)S(1)}, u32[]{:S(2)}, u32[]{:S(2)}) collective-permute-start(bf16[240,512]{1,0:T(8,128)(2,1)S(1)} %slice.58), channel_id=1, source_target_pairs={{0,28},{4,24},{8,20},{12,16},{16,12},{20,8},{24,4},{28,0},{1,29},{... | collective-permute-start | bytes 737288 | tf_op jit(solution)/shard_map/cond/branch_6_fun/ppermute | solution.py:328
  16.8 5.9 %collective-permute-start.40 = (bf16[144,512]{1,0:T(8,128)(2,1)S(1)}, bf16[144,512]{1,0:T(8,128)(2,1)S(1)}, u32[]{:S(2)}, u32[]{:S(2)}) collective-permute-start(bf16[144,512]{1,0:T(8,128)(2,1)S(1)} %slice.59), channel_id=1, source_target_pairs={{0,1},{1,0},{2,3},{3,2},{4,5},{5,4},{6,7},{7,6},{8,9},{9,8},{10,11... | collective-permute-start | bytes 442376 | tf_op jit(solution)/shard_map/cond/branch_6_fun/ppermute | solution.py:329
  20.7 2.1 %copy-start.27 = (bf16[256,512]{1,0:T(8,128)(2,1)S(1)}, bf16[256,512]{1,0:T(8,128)(2,1)}, u32[]{:S(2)}) copy-start(bf16[256,512]{1,0:T(8,128)(2,1)} %get-tuple-element.278.low_table) | copy-start | bytes 786436 | tf_op jit(solution)/shard_map/cond
  20.7 2.1 %copy-start.34 = (bf16[256,512]{1,0:T(8,128)(2,1)S(1)}, bf16[256,512]{1,0:T(8,128)(2,1)}, u32[]{:S(2)}) copy-start(bf16[256,512]{1,0:T(8,128)(2,1)} %get-tuple-element.277.high_table) | copy-start | bytes 786436 | tf_op jit(solution)/shard_map/cond
  25.1 13.7 %collective-permute-start.41 = (bf16[448,256]{1,0:T(8,128)(2,1)S(1)}, bf16[448,256]{1,0:T(8,128)(2,1)S(1)}, u32[]{:S(2)}, u32[]{:S(2)}) collective-permute-start(bf16[448,256]{1,0:T(8,128)(2,1)S(1)} %bitcast.41), channel_id=1, source_target_pairs={{0,2},{1,3},{2,0},{3,1},{4,6},{5,7},{6,4},{7,5},{8,10},{9,11},{10,... | collective-permute-start | bytes 688136 | tf_op jit(solution)/shard_map/cond/branch_6_fun/ppermute | solution.py:362
  39.2 1.6 %collective-permute-start.47 = (bf16[448,256]{1,0:T(8,128)(2,1)S(1)}, bf16[448,256]{1,0:T(8,128)(2,1)S(1)}, u32[]{:S(2)}, u32[]{:S(2)}) collective-permute-start(bf16[448,256]{1,0:T(8,128)(2,1)S(1)} %get-tuple-element.304.total), channel_id=1, source_target_pairs={{0,4},{4,0},{8,12},{12,8},{16,20},{20,16},{24,28},{28,24},{1,5},{5... | collective-permute-start | bytes 688136 | tf_op jit(solution)/shard_map/ppermute | solution.py:375
  39.3 6.8 %collective-permute-start.42 = (bf16[128,256]{1,0:T(8,128)(2,1)S(1)}, bf16[128,256]{1,0:T(8,128)(2,1)S(1)}, u32[]{:S(2)}, u32[]{:S(2)}) collective-permute-start(bf16[128,256]{1,0:T(8,128)(2,1)S(1)} %bitcast.50), channel_id=1, source_target_pairs={{0,2},{1,3},{2,0},{3,1},{4,6},{5,7},{6,4},{7,5},{8,10},{9,11},{10,... | collective-permute-start | bytes 196616 | tf_op jit(solution)/shard_map/ppermute | solution.py:362
  41.2 8.1 %collective-permute-start.48 = (bf16[448,128]{1,0:T(8,128)(2,1)S(1)}, bf16[448,128]{1,0:T(8,128)(2,1)S(1)}, u32[]{:S(2)}, u32[]{:S(2)}) collective-permute-start(bf16[448,128]{1,0:T(8,128)(2,1)S(1)} %get-tuple-element.306), channel_id=1, source_target_pairs={{0,8},{4,12},{8,0},{12,4},{16,24},{20,28},{24,16},{28,20},{1,9},{5... | collective-permute-start | bytes 344072 | tf_op jit(solution)/shard_map/ppermute | solution.py:377
  41.4 9.9 %collective-permute-start.49 = (bf16[448,128]{1,0:T(8,128)(2,1)S(1)}, bf16[448,128]{1,0:T(8,128)(2,1)S(1)}, u32[]{:S(2)}, u32[]{:S(2)}) collective-permute-start(bf16[448,128]{1,0:T(8,128)(2,1)S(1)} %get-tuple-element.307), channel_id=1, source_target_pairs={{0,16},{4,20},{8,24},{12,28},{16,0},{20,4},{24,8},{28,12},{1,17},{... | collective-permute-start | bytes 344072 | tf_op jit(solution)/shard_map/ppermute | solution.py:377
  42.7 8.6 %collective-permute-start.50 = (bf16[448,128]{1,0:T(8,128)(2,1)S(1)}, bf16[448,128]{1,0:T(8,128)(2,1)S(1)}, u32[]{:S(2)}, u32[]{:S(2)}) collective-permute-start(bf16[448,128]{1,0:T(8,128)(2,1)S(1)} %get-tuple-element.308), channel_id=1, source_target_pairs={{0,24},{4,28},{8,16},{12,20},{16,8},{20,12},{24,0},{28,4},{1,25},{... | collective-permute-start | bytes 344072 | tf_op jit(solution)/shard_map/ppermute | solution.py:377
  46.1 1.3 %collective-permute-start.43 = (bf16[128,256]{1,0:T(8,128)(2,1)S(1)}, bf16[128,256]{1,0:T(8,128)(2,1)S(1)}, u32[]{:S(2)}, u32[]{:S(2)}) collective-permute-start(bf16[128,256]{1,0:T(8,128)(2,1)S(1)} %shard_map.109.total), channel_id=1, source_target_pairs={{0,4},{4,0},{8,12},{12,8},{16,20},{20,16},{24,28},{28,24},{1,5},{5... | collective-permute-start | bytes 196616 | tf_op jit(solution)/shard_map/ppermute | solution.py:375
  47.8 4.5 %collective-permute-start.44 = (bf16[128,128]{1,0:T(8,128)(2,1)S(1)}, bf16[128,128]{1,0:T(8,128)(2,1)S(1)}, u32[]{:S(2)}, u32[]{:S(2)}) collective-permute-start(bf16[128,128]{1,0:T(8,128)(2,1)S(1)} %get-tuple-element.301), channel_id=1, source_target_pairs={{0,8},{4,12},{8,0},{12,4},{16,24},{20,28},{24,16},{28,20},{1,9},{5... | collective-permute-start | bytes 98312 | tf_op jit(solution)/shard_map/ppermute | solution.py:377
  48.0 4.3 %collective-permute-start.45 = (bf16[128,128]{1,0:T(8,128)(2,1)S(1)}, bf16[128,128]{1,0:T(8,128)(2,1)S(1)}, u32[]{:S(2)}, u32[]{:S(2)}) collective-permute-start(bf16[128,128]{1,0:T(8,128)(2,1)S(1)} %get-tuple-element.302), channel_id=1, source_target_pairs={{0,16},{4,20},{8,24},{12,28},{16,0},{20,4},{24,8},{28,12},{1,17},{... | collective-permute-start | bytes 98312 | tf_op jit(solution)/shard_map/ppermute | solution.py:377
  49.3 4.8 %collective-permute-start.46 = (bf16[128,128]{1,0:T(8,128)(2,1)S(1)}, bf16[128,128]{1,0:T(8,128)(2,1)S(1)}, u32[]{:S(2)}, u32[]{:S(2)}) collective-permute-start(bf16[128,128]{1,0:T(8,128)(2,1)S(1)} %get-tuple-element.303), channel_id=1, source_target_pairs={{0,24},{4,28},{8,16},{12,20},{16,8},{20,12},{24,0},{28,4},{1,25},{... | collective-permute-start | bytes 98312 | tf_op jit(solution)/shard_map/ppermute | solution.py:377

commit v5 on v4

--- a/solution.py
+++ b/solution.py
@@ -178,33 +178,29 @@
 
 def send_kernel(
     width, blocks, sends, x0, g1, xa, xb, dft, band, inverse, index, high_table, low_table,
-    out, rest, h1, cross_high, cross_low, lagged,
+    out, h1, cross_high, cross_low, lagged,
 ):
     x = jnp.concatenate([xa[...], xb[...]], axis=0)
     white = whiten_rows(x, dft[...], band[...], inverse[...], index[...])
     for c in range(3):
         h1[c] = white[c]
-    rows = out.shape[1]
     for k in range(sends):
         base = x0.at[k * blocks : (k + 1) * blocks]
         shift = piece(
             lax.axis_index("tm") ^ (2 * (k + 1)), width, blocks, (g1,), (h1,), base, lagged,
             high_table, low_table, cross_high, cross_low, sends == 1,
         )
-        out[k] = lagged[pl.ds(pl.multiple_of(shift, 16), rows)].astype(BF16)
-        rest[k] = lagged[pl.ds(pl.multiple_of(shift + rows, 16), width - rows)].astype(BF16)
+        out[k] = lagged[pl.ds(pl.multiple_of(shift, 16), width)].astype(BF16)
 
 
 def own_kernel(
-    width, blocks, g0, h0, g1, h1, high_table, low_table, out, rest, cross_high, cross_low, lagged
+    width, blocks, g0, h0, g1, h1, high_table, low_table, out, cross_high, cross_low, lagged
 ):
     shift = piece(
         lax.axis_index("tm"), width, blocks, (g0, g1), (h0, h1), None, lagged,
         high_table, low_table, cross_high, cross_low, False,
     )
-    rows = out.shape[0]
-    out[...] = lagged[pl.ds(pl.multiple_of(shift, 16), rows)]
-    rest[...] = lagged[pl.ds(pl.multiple_of(shift + rows, 16), width - rows)]
+    out[...] = lagged[pl.ds(pl.multiple_of(shift, 16), width)]
 
 
 def total_kernel(own, received, out):
@@ -297,7 +293,6 @@
     sends = tm_count // 2 - 1
     top = LAGS - math.gcd(width, LAGS)
     blocks = -(-(top + width) // LAGS)
-    rows = width * 7 // 144 * 16
     scale = 1.0 / math.sqrt(freqs * seg_local * tm_count)
     dft, high_table, low_table, band, inverse = (jnp.asarray(a) for a in tables(samples, freqs, scale))
 
@@ -335,54 +330,41 @@
             jax.ShapeDtypeStruct((sends * blocks, 2 * freqs, pairs), F32),
             (g0, h0),
         )
-        first, rest, h1 = call(
+        sent, h1 = call(
             functools.partial(send_kernel, width, blocks, sends),
             (
-                jax.ShapeDtypeStruct((sends, rows, pairs), BF16),
-                jax.ShapeDtypeStruct((sends, width - rows, pairs), BF16),
+                jax.ShapeDtypeStruct((sends, width, pairs), BF16),
                 rows_shape,
             ),
             (x0, g1, pa, pb, dft, band, inverse, right, high_table, low_table),
             scratch,
         )
-        received = exchange(first)
+        received = [lax.ppermute(sent[j], "tm", xor_pairs(tm_count, 2 * (j + 1))) for j in range(sends)]
         own = call(
             functools.partial(own_kernel, width, blocks),
-            (jax.ShapeDtypeStruct((rows, pairs), F32), jax.ShapeDtypeStruct((width - rows, pairs), F32)),
+            jax.ShapeDtypeStruct((width, pairs), F32),
             (g0, h0, g1, h1, high_table, low_table),
             scratch,
         )
-        return total(own[0], received), rest, own[1], pick
-
-    def total(mine, received):
-        shape = jax.ShapeDtypeStruct(mine.shape, BF16)
-        return call(total_kernel, shape, (mine, jnp.stack(received)))
-
-    def exchange(part):
-        return [lax.ppermute(part[j], "tm", xor_pairs(tm_count, 2 * (j + 1))) for j in range(sends)]
+        shape = jax.ShapeDtypeStruct((width, pairs), BF16)
+        return call(total_kernel, shape, (own, jnp.stack(received))), pick
 
     scratch = [pltpu.VMEM((2 * freqs, pairs), BF16)] * 2 + [pltpu.VMEM((blocks * LAGS, pairs), F32)]
     branches = [functools.partial(gather, k) for k in range(1, sta_count)]
-    first, rest, own, pick = lax.switch(
+    summed, pick = lax.switch(
         partner.reshape(-1)[0] - 1, branches, x, left_station, right_station, owner, pair_count
     )
-    second = total(own, exchange(rest))
     lanes = 2 * capacity
-    shape = jax.ShapeDtypeStruct((width, sta_count * capacity), F32)
-    parts, result = [], None
-    for summed in (first, second):
-        size = summed.shape[0]
-        other = lax.ppermute(summed, "sta", xor_pairs(sta_count, 1))
-        routed = call(route_kernel, [jax.ShapeDtypeStruct((size, lanes), BF16)] * chips, (summed, other, pick))
-        arrived = [lax.ppermute(routed[j], "sta", xor_pairs(sta_count, 2 * j)) for j in range(chips - 1, 0, -1)]
-        arrived = [routed[0]] + arrived[::-1]
-        if lanes % 128 == 0:
-            result = place(lanes, 0 if result is None else rows, shape, arrived, result)
-        else:
-            order = jnp.bitwise_xor(lax.axis_index("sta") // 2, jnp.arange(chips, dtype=jnp.int32))
-            arrived = jnp.take(jnp.stack(arrived), order, axis=0).astype(F32)
-            parts.append(jnp.transpose(arrived, (1, 0, 2)).reshape(size, sta_count * capacity))
-            result = jnp.concatenate(parts, axis=0)
+    other = lax.ppermute(summed, "sta", xor_pairs(sta_count, 1))
+    routed = call(route_kernel, [jax.ShapeDtypeStruct((width, lanes), BF16)] * chips, (summed, other, pick))
+    arrived = [lax.ppermute(routed[j], "sta", xor_pairs(sta_count, 2 * j)) for j in range(chips - 1, 0, -1)]
+    arrived = [routed[0]] + arrived[::-1]
+    if lanes % 128 == 0:
+        result = place(lanes, 0, jax.ShapeDtypeStruct((width, sta_count * capacity), F32), arrived, None)
+    else:
+        order = jnp.bitwise_xor(lax.axis_index("sta") // 2, jnp.arange(chips, dtype=jnp.int32))
+        result = jnp.take(jnp.stack(arrived), order, axis=0).astype(F32)
+        result = jnp.transpose(result, (1, 0, 2)).reshape(width, sta_count * capacity)
     return result.T
 
 

time: 54.9 us -> 54.1 us (0.985)
  waiting for transfers between devices: 19.9 us -> 24.1 us
  starting transfers between devices: 17.2 us -> 13.5 us
  Pallas kernels: 14.5 us -> 13.6 us
    ppermute x6 -> x3, waiting for transfers between devices: 1.8 us -> 5.64 us  [local(): lax.ppermute(routed[j], 'sta', xor_pairs(sta_count, 2 * j))]
    ppermute x6 -> x3, starting transfers between devices: 7.11 us -> 3.55 us  [local(): lax.ppermute(routed[j], 'sta', xor_pairs(sta_count, 2 * j))]
    ppermute x2 -> x1, waiting for transfers between devices: 10.2 us -> 11.7 us  [gather(): lax.ppermute(sent[j], 'tm', xor_pairs(tm_count, 2 * (j + 1)))]
    ppermute x2 -> x1, waiting for transfers between devices: 2.64 us -> 1.57 us  [local(): other = lax.ppermute(summed, 'sta', xor_pairs(sta_count, 1))]
    pallas_call x2 -> x1, Pallas kernels: 1.71 us -> 1.06 us  [place(): pl.pallas_call(functools.partial(place_kernel, lanes, top), out_shape=sha...]
    pallas_call x11 -> x9, Pallas kernels: 12.8 us -> 12.5 us  [call(): pl.pallas_call(kernel, out_shape=out_shape, in_specs=[pl.BlockSpec(memory...]
    ppermute x2 -> x1, starting transfers between devices: 3.01 us -> 2.94 us  [gather(): lax.ppermute(sent[j], 'tm', xor_pairs(tm_count, 2 * (j + 1)))]
  transfers between devices with their start and end apart: 15 -> 10, of which waited for: 8 -> 7; matrix products, arithmetic and copies ran while one was open for 2% -> 2% of each run, Pallas kernels for 21% -> 18%
where the time goes in v5:
time: 54.1 us; the launch traced here: 54.7 us
  waiting for transfers between devices  24.1 us (45%)
  Pallas kernels  13.6 us (25%)
  starting transfers between devices  13.5 us (25%)
  other arithmetic  1.33 us (2%)
  loops' own time  0.97 us (2%)
  local copies, waits for them, and re-layouts  0.83 us (2%)
    pallas_call x9, Pallas kernels, call(): pl.pallas_call(kernel, out_shape=out_shape, in_specs=[pl.BlockSpec(memory...  12.5 us
    ppermute x1, waiting for transfers between devices, gather(): lax.ppermute(sent[j], 'tm', xor_pairs(tm_count, 2 * (j + 1)))  11.7 us
    ppermute x3, waiting for transfers between devices, local(): lax.ppermute(routed[j], 'sta', xor_pairs(sta_count, 2 * j))  5.64 us
    ppermute x3, starting transfers between devices, local(): lax.ppermute(routed[j], 'sta', xor_pairs(sta_count, 2 * j))  3.55 us
    ppermute x1, starting transfers between devices, gather(): x_next = swap(x)  3.09 us
    ppermute x1, starting transfers between devices, gather(): lax.ppermute(sent[j], 'tm', xor_pairs(tm_count, 2 * (j + 1)))  2.94 us
    ppermute x1, waiting for transfers between devices, gather(): x_next = swap(x)  1.88 us
    ppermute x1, waiting for transfers between devices, gather(): p = cross(x)  1.79 us
  transfers between devices with their start and end apart: 10, of which 7 were waited for; matrix products, arithmetic and copies ran while one was open for 2% of the time, Pallas kernels for 18%

profile of v5, /device:TPU:0, one launch (start us, length us, event | category | flops | bytes accessed | tf_op | source)
XLA Modules:
  0.0 54.7 jit_solution(7220026011080772548)
XLA Ops:
  0.0 0.8 %reshape.67 = s32[56]{0:T(128)S(1)} reshape(s32[7,8]{1,0:T(8,128)} %param.19) | data formatting | bytes 448 | tf_op jit(solution)/shard_map/reshape | solution.py:355
  0.8 41.2 %conditional.1 = (bf16[576,256]{1,0:T(8,128)(2,1)S(1)}, bf16[512,512]{1,0:T(8,128)(2,1)S(1)}) conditional(s32[]{:T(128)} %bitcast.21, (bf16[384,512]{1,0:T(8,128)(2,1)}, bf16[512,512]{1,0:T(8,128)(2,1)}, bf16[256,256]{1,0:T(8,128)(2,1)}, f32[256,128]{1,0:T(8,128)}, s32[1,256]{1,0:T(1,128)}, /*index=5*/s32[1]{0:T(128)}, ...), branch_computations={%region_0.1_spmd, %region_1.2_spmd, %region_2.3_spmd, %region_3.4_... | conditional | flops 8704 | bytes 11950536 | solution.py:354
  1.3 3.1 %collective-permute-start.36 = (bf16[384,512]{1,0:T(8,128)(2,1)}, bf16[384,512]{1,0:T(8,128)(2,1)S(1)}, u32[]{:S(2)}, u32[]{:S(2)}) collective-permute-start(bf16[384,512]{1,0:T(8,128)(2,1)} %get-tuple-element.247.x), channel_id=1, source_target_pairs={{0,1},{1,0},{2,3},{3,2},{4,5},{5,4},{6,7},{7,6},{8,9},{9,8},{10,11... | collective-permute-start | bytes 1179656 | tf_op jit(solution)/shard_map/cond/branch_6_fun/ppermute | solution.py:313
  4.4 1.6 %collective-permute-start.38 = (bf16[384,512]{1,0:T(8,128)(2,1)}, bf16[384,512]{1,0:T(8,128)(2,1)S(1)}, u32[]{:S(2)}, u32[]{:S(2)}) collective-permute-start(bf16[384,512]{1,0:T(8,128)(2,1)} %get-tuple-element.247.x), channel_id=1, source_target_pairs={{0,28},{4,24},{8,20},{12,16},{16,12},{20,8},{24,4},{28,0},{1,29},{... | collective-permute-start | bytes 1179656 | tf_op jit(solution)/shard_map/cond/branch_6_fun/ppermute | solution.py:312
  6.0 1.3 %compare_select_fusion.6.owner = s32[1,256]{1,0:T(1,128)S(1)} fusion(s32[1,256]{1,0:T(1,128)} %get-tuple-element.253, s32[]{:T(128)} %bitcast.18), kind=kLoop, calls=%fused_computation.6 | loop fusion | flops 512 | bytes 2052 | tf_op jit(solution)/shard_map/cond/branch_6_fun/jit(_where)/select_n | solution.py:315
  7.4 1.0 %collective-permute-start.37 = (s32[1,256]{1,0:T(1,128)S(1)}, s32[1,256]{1,0:T(1,128)S(1)}, u32[]{:S(2)}, u32[]{:S(2)}) collective-permute-start(s32[1,256]{1,0:T(1,128)S(1)} %compare_select_fusion.6.owner), channel_id=1, source_target_pairs={{0,4},{4,0},{8,12},{12,8},{16,20},{20,16},{24,28},{28,24},{1,5},{5... | collective-permute-start | bytes 3080 | tf_op jit(solution)/shard_map/cond/branch_6_fun/ppermute | solution.py:316
  8.3 0.0 copy-start.6
  8.3 0.0 copy-start.13
  8.3 0.0 copy-start.20
  8.3 0.0 copy-start.41
  8.3 3.2 %branch_6_fun.8.g0 = f32[3,512,256]{2,1,0:T(8,128)S(1)} custom-call(bf16[384,512]{1,0:T(8,128)(2,1)} %get-tuple-element.247.x, bf16[512,512]{1,0:T(8,128)(2,1)} %get-tuple-element.248.dft, bf16[256,256]{1,0:T(8,128)(2,1)} %get-tuple-element.249.band, f32[256,128]{1,0:T(8,128)} %get-tuple-element.250.inverse, s32[1,256]{1,0:T(1,128)} %get-tuple-element.251.index), custom_call_target="tpu_custom_call" | custom-call | flops 1024 | bytes 1024 | tf_op jit(solution)/shard_map/cond/branch_6_fun/pallas_call | solution.py:273
  11.5 0.0 collective-permute-done.37.other_owner
  11.5 0.4 branch_6_fun.9
  11.9 1.9 %collective-permute-done.36.x = bf16[384,512]{1,0:T(8,128)(2,1)S(1)} collective-permute-done((bf16[384,512]{1,0:T(8,128)(2,1)}, bf16[384,512]{1,0:T(8,128)(2,1)S(1)}, u32[]{:S(2)}, u32[]{:S(2)}) %collective-permute-start.36) | collective-permute-done | bytes 393248 | tf_op jit(solution)/shard_map/cond/branch_6_fun/ppermute | solution.py:313
  13.8 0.0 copy-start.48
  13.8 1.2 %collective-permute-start.39 = (bf16[240,512]{1,0:T(8,128)(2,1)S(1)}, bf16[240,512]{1,0:T(8,128)(2,1)S(1)}, u32[]{:S(2)}, u32[]{:S(2)}) collective-permute-start(bf16[240,512]{1,0:T(8,128)(2,1)S(1)} %slice.58), channel_id=1, source_target_pairs={{0,28},{4,24},{8,20},{12,16},{16,12},{20,8},{24,4},{28,0},{1,29},{... | collective-permute-start | bytes 737288 | tf_op jit(solution)/shard_map/cond/branch_6_fun/ppermute | solution.py:323
  15.0 1.8 %collective-permute-done.38.x = bf16[384,512]{1,0:T(8,128)(2,1)S(1)} collective-permute-done((bf16[384,512]{1,0:T(8,128)(2,1)}, bf16[384,512]{1,0:T(8,128)(2,1)S(1)}, u32[]{:S(2)}, u32[]{:S(2)}) %collective-permute-start.38) | collective-permute-done | bytes 393248 | tf_op jit(solution)/shard_map/cond/branch_6_fun/ppermute | solution.py:312
  16.8 0.1 collective-permute-start.40
  16.9 0.0 copy-done.6
  16.9 0.0 copy-done.13
  16.9 0.0 copy-done.20
  16.9 0.0 copy-done.41
  16.9 1.9 %branch_6_fun.10.g1 = f32[3,512,256]{2,1,0:T(8,128)S(1)} custom-call(bf16[384,512]{1,0:T(8,128)(2,1)S(1)} %collective-permute-done.36.x, bf16[512,512]{1,0:T(8,128)(2,1)S(1)} %copy-done.6, bf16[256,256]{1,0:T(8,128)(2,1)S(1)} %copy-done.20, f32[256,128]{1,0:T(8,128)S(1)} %copy-done.13, s32[1,256]{1,0:T(1,128)S(1)} %copy-done.41), custom_call_target="tpu_custom_call" | custom-call | flops 1024 | bytes 1024 | tf_op jit(solution)/shard_map/cond/branch_6_fun/pallas_call | solution.py:273
  18.8 0.0 copy-done.48
  18.8 1.9 %branch_6_fun.11.h0 = f32[3,512,256]{2,1,0:T(8,128)S(1)} custom-call(bf16[384,512]{1,0:T(8,128)(2,1)S(1)} %collective-permute-done.38.x, bf16[512,512]{1,0:T(8,128)(2,1)S(1)} %copy-done.6, bf16[256,256]{1,0:T(8,128)(2,1)S(1)} %copy-done.20, f32[256,128]{1,0:T(8,128)S(1)} %copy-done.13, s32[1,256]{1,0:T(1,128)S(1)} %copy-done.48), custom_call_target="tpu_custom_call" | custom-call | flops 1024 | bytes 1024 | tf_op jit(solution)/shard_map/cond/branch_6_fun/pallas_call | solution.py:273
  20.7 0.0 copy-start.27
  20.7 0.0 copy-start.34
  20.7 0.5 branch_6_fun.12.x0
  21.2 1.5 %collective-permute-done.40.xb = bf16[144,512]{1,0:T(8,128)(2,1)S(1)} collective-permute-done((bf16[144,512]{1,0:T(8,128)(2,1)S(1)}, bf16[144,512]{1,0:T(8,128)(2,1)S(1)}, u32[]{:S(2)}, u32[]{:S(2)}) %collective-permute-start.40) | collective-permute-done | bytes 147488 | tf_op jit(solution)/shard_map/cond/branch_6_fun/ppermute | solution.py:324
  22.8 0.0 collective-permute-done.39.xa
  22.8 0.0 copy-done.27
  22.8 0.0 copy-done.34
  22.8 2.3 %branch_6_fun.13 = (bf16[1,576,256]{2,1,0:T(8,128)(2,1)S(1)}, f32[3,512,256]{2,1,0:T(8,128)S(1)}) custom-call(f32[3,512,256]{2,1,0:T(8,128)S(1)} %branch_6_fun.12.x0, f32[3,512,256]{2,1,0:T(8,128)S(1)} %branch_6_fun.10.g1, bf16[240,512]{1,0:T(8,128)(2,1)S(1)} %collective-permute-done.39.xa, bf16[144,512]{1,0:T(8,128)(2,1)S(1)} %collective-permute-done.40.xb, ...), custom_call_target="tpu_custom_call" | custom-call | flops 1024 | bytes 1024 | tf_op jit(solution)/shard_map/cond/branch_6_fun/pallas_call | solution.py:273
  25.1 2.9 %collective-permute-start.41 = (bf16[576,256]{1,0:T(8,128)(2,1)S(1)}, bf16[576,256]{1,0:T(8,128)(2,1)S(1)}, u32[]{:S(2)}, u32[]{:S(2)}) collective-permute-start(bf16[576,256]{1,0:T(8,128)(2,1)S(1)} %bitcast.38), channel_id=1, source_target_pairs={{0,2},{1,3},{2,0},{3,1},{4,6},{5,7},{6,4},{7,5},{8,10},{9,11},{10,... | collective-permute-start | bytes 884744 | tf_op jit(solution)/shard_map/cond/branch_6_fun/ppermute | solution.py:342
  28.1 1.9 %branch_6_fun.14.own = f32[576,256]{1,0:T(8,128)S(1)} custom-call(f32[3,512,256]{2,1,0:T(8,128)S(1)} %branch_6_fun.8.g0, f32[3,512,256]{2,1,0:T(8,128)S(1)} %branch_6_fun.11.h0, f32[3,512,256]{2,1,0:T(8,128)S(1)} %branch_6_fun.10.g1, f32[3,512,256]{2,1,0:T(8,128)S(1)} %get-tuple-element.261.h1, bf16[256,512]{1,0:T(8,128)(2,1)S(1)} %copy-done.34, ...), custom_call_target="tpu_custom_call" | custom-call | flops 1024 | bytes 1024 | tf_op jit(solution)/shard_map/cond/branch_6_fun/pallas_call | solution.py:273
  30.0 11.7 %collective-permute-done.41 = bf16[576,256]{1,0:T(8,128)(2,1)S(1)} collective-permute-done((bf16[576,256]{1,0:T(8,128)(2,1)S(1)}, bf16[576,256]{1,0:T(8,128)(2,1)S(1)}, u32[]{:S(2)}, u32[]{:S(2)}) %collective-permute-start.41) | collective-permute-done | bytes 294944 | tf_op jit(solution)/shard_map/cond/branch_6_fun/ppermute | solution.py:342
  41.7 0.1 branch_6_fun.15
  42.0 0.1 collective-permute-start.42
  42.1 1.6 %collective-permute-done.42.other = bf16[576,256]{1,0:T(8,128)(2,1)S(1)} collective-permute-done((bf16[576,256]{1,0:T(8,128)(2,1)S(1)}, bf16[576,256]{1,0:T(8,128)(2,1)S(1)}, u32[]{:S(2)}, u32[]{:S(2)}) %collective-permute-start.42) | collective-permute-done | bytes 294944 | tf_op jit(solution)/shard_map/ppermute | solution.py:358
  43.7 0.5 shard_map.109
  44.2 0.2 collective-permute-start.43
  44.4 1.3 %collective-permute-start.44 = (bf16[576,128]{1,0:T(8,128)(2,1)S(1)}, bf16[576,128]{1,0:T(8,128)(2,1)S(1)}, u32[]{:S(2)}, u32[]{:S(2)}) collective-permute-start(bf16[576,128]{1,0:T(8,128)(2,1)S(1)} %get-tuple-element.274), channel_id=1, source_target_pairs={{0,16},{4,20},{8,24},{12,28},{16,0},{20,4},{24,8},{28,12},{1,17},{... | collective-permute-start | bytes 442376 | tf_op jit(solution)/shard_map/ppermute | solution.py:360
  45.7 2.0 %collective-permute-start.45 = (bf16[576,128]{1,0:T(8,128)(2,1)S(1)}, bf16[576,128]{1,0:T(8,128)(2,1)S(1)}, u32[]{:S(2)}, u32[]{:S(2)}) collective-permute-start(bf16[576,128]{1,0:T(8,128)(2,1)S(1)} %get-tuple-element.275), channel_id=1, source_target_pairs={{0,24},{4,28},{8,16},{12,20},{16,8},{20,12},{24,0},{28,4},{1,25},{... | collective-permute-start | bytes 442376 | tf_op jit(solution)/shard_map/ppermute | solution.py:360
  47.7 3.2 %collective-permute-done.43.refs_1_ = bf16[576,128]{1,0:T(8,128)(2,1)S(1)} collective-permute-done((bf16[576,128]{1,0:T(8,128)(2,1)S(1)}, bf16[576,128]{1,0:T(8,128)(2,1)S(1)}, u32[]{:S(2)}, u32[]{:S(2)}) %collective-permute-start.43) | collective-permute-done | bytes 147488 | tf_op jit(solution)/shard_map/ppermute | solution.py:360
  50.9 2.4 %collective-permute-done.44.refs_2_ = bf16[576,128]{1,0:T(8,128)(2,1)S(1)} collective-permute-done((bf16[576,128]{1,0:T(8,128)(2,1)S(1)}, bf16[576,128]{1,0:T(8,128)(2,1)S(1)}, u32[]{:S(2)}, u32[]{:S(2)}) %collective-permute-start.44) | collective-permute-done | bytes 147488 | tf_op jit(solution)/shard_map/ppermute | solution.py:360
  53.4 0.0 collective-permute-done.45.refs_3_
  53.4 1.1 %shard_map.110 = f32[576,512]{1,0:T(8,128)} custom-call(bf16[576,128]{1,0:T(8,128)(2,1)S(1)} %get-tuple-element.272.refs_0_, bf16[576,128]{1,0:T(8,128)(2,1)S(1)} %collective-permute-done.43.refs_1_, bf16[576,128]{1,0:T(8,128)(2,1)S(1)} %collective-permute-done.44.refs_2_, bf16[576,128]{1,0:T(8,128)(2,1)S(1)} %collective-permute-done.45.refs_3_), custom_call_target="tpu_custom_call" | custom-call | flops 1024 | bytes 1024 | tf_op jit(solution)/shard_map/pallas_call | solution.py:259
  (2 shorter events, 0.0 us)
Async XLA Ops:
  1.3 12.4 %collective-permute-start.36 = (bf16[384,512]{1,0:T(8,128)(2,1)}, bf16[384,512]{1,0:T(8,128)(2,1)S(1)}, u32[]{:S(2)}, u32[]{:S(2)}) collective-permute-start(bf16[384,512]{1,0:T(8,128)(2,1)} %get-tuple-element.247.x), channel_id=1, source_target_pairs={{0,1},{1,0},{2,3},{3,2},{4,5},{5,4},{6,7},{7,6},{8,9},{9,8},{10,11... | collective-permute-start | bytes 1179656 | tf_op jit(solution)/shard_map/cond/branch_6_fun/ppermute | solution.py:313
  4.4 12.4 %collective-permute-start.38 = (bf16[384,512]{1,0:T(8,128)(2,1)}, bf16[384,512]{1,0:T(8,128)(2,1)S(1)}, u32[]{:S(2)}, u32[]{:S(2)}) collective-permute-start(bf16[384,512]{1,0:T(8,128)(2,1)} %get-tuple-element.247.x), channel_id=1, source_target_pairs={{0,28},{4,24},{8,20},{12,16},{16,12},{20,8},{24,4},{28,0},{1,29},{... | collective-permute-start | bytes 1179656 | tf_op jit(solution)/shard_map/cond/branch_6_fun/ppermute | solution.py:312
  7.4 4.1 %collective-permute-start.37 = (s32[1,256]{1,0:T(1,128)S(1)}, s32[1,256]{1,0:T(1,128)S(1)}, u32[]{:S(2)}, u32[]{:S(2)}) collective-permute-start(s32[1,256]{1,0:T(1,128)S(1)} %compare_select_fusion.6.owner), channel_id=1, source_target_pairs={{0,4},{4,0},{8,12},{12,8},{16,20},{20,16},{24,28},{28,24},{1,5},{5... | collective-permute-start | bytes 3080 | tf_op jit(solution)/shard_map/cond/branch_6_fun/ppermute | solution.py:316
  8.3 8.6 %copy-start.6 = (bf16[512,512]{1,0:T(8,128)(2,1)S(1)}, bf16[512,512]{1,0:T(8,128)(2,1)}, u32[]{:S(2)}) copy-start(bf16[512,512]{1,0:T(8,128)(2,1)} %get-tuple-element.248.dft) | copy-start | bytes 1572868 | tf_op jit(solution)/shard_map/cond
  8.3 8.6 %copy-start.13 = (f32[256,128]{1,0:T(8,128)S(1)}, f32[256,128]{1,0:T(8,128)}, u32[]{:S(2)}) copy-start(f32[256,128]{1,0:T(8,128)} %get-tuple-element.250.inverse) | copy-start | bytes 393220 | tf_op jit(solution)/shard_map/cond
  8.3 8.6 %copy-start.20 = (bf16[256,256]{1,0:T(8,128)(2,1)S(1)}, bf16[256,256]{1,0:T(8,128)(2,1)}, u32[]{:S(2)}) copy-start(bf16[256,256]{1,0:T(8,128)(2,1)} %get-tuple-element.249.band) | copy-start | bytes 393220 | tf_op jit(solution)/shard_map/cond
  8.3 8.6 %copy-start.41 = (s32[1,256]{1,0:T(1,128)S(1)}, s32[1,256]{1,0:T(1,128)}, u32[]{:S(2)}) copy-start(s32[1,256]{1,0:T(1,128)} %get-tuple-element.251.index) | copy-start | bytes 3076 | tf_op jit(solution)/shard_map/cond
  13.8 5.0 %copy-start.48 = (s32[1,256]{1,0:T(1,128)S(1)}, s32[1,256]{1,0:T(1,128)}, u32[]{:S(2)}) copy-start(s32[1,256]{1,0:T(1,128)} %get-tuple-element.256.index) | copy-start | bytes 3076 | tf_op jit(solution)/shard_map/cond
  13.8 9.0 %collective-permute-start.39 = (bf16[240,512]{1,0:T(8,128)(2,1)S(1)}, bf16[240,512]{1,0:T(8,128)(2,1)S(1)}, u32[]{:S(2)}, u32[]{:S(2)}) collective-permute-start(bf16[240,512]{1,0:T(8,128)(2,1)S(1)} %slice.58), channel_id=1, source_target_pairs={{0,28},{4,24},{8,20},{12,16},{16,12},{20,8},{24,4},{28,0},{1,29},{... | collective-permute-start | bytes 737288 | tf_op jit(solution)/shard_map/cond/branch_6_fun/ppermute | solution.py:323
  16.8 5.9 %collective-permute-start.40 = (bf16[144,512]{1,0:T(8,128)(2,1)S(1)}, bf16[144,512]{1,0:T(8,128)(2,1)S(1)}, u32[]{:S(2)}, u32[]{:S(2)}) collective-permute-start(bf16[144,512]{1,0:T(8,128)(2,1)S(1)} %slice.59), channel_id=1, source_target_pairs={{0,1},{1,0},{2,3},{3,2},{4,5},{5,4},{6,7},{7,6},{8,9},{9,8},{10,11... | collective-permute-start | bytes 442376 | tf_op jit(solution)/shard_map/cond/branch_6_fun/ppermute | solution.py:324
  20.7 2.1 %copy-start.27 = (bf16[256,512]{1,0:T(8,128)(2,1)S(1)}, bf16[256,512]{1,0:T(8,128)(2,1)}, u32[]{:S(2)}) copy-start(bf16[256,512]{1,0:T(8,128)(2,1)} %get-tuple-element.260.low_table) | copy-start | bytes 786436 | tf_op jit(solution)/shard_map/cond
  20.7 2.1 %copy-start.34 = (bf16[256,512]{1,0:T(8,128)(2,1)S(1)}, bf16[256,512]{1,0:T(8,128)(2,1)}, u32[]{:S(2)}) copy-start(bf16[256,512]{1,0:T(8,128)(2,1)} %get-tuple-element.259.high_table) | copy-start | bytes 786436 | tf_op jit(solution)/shard_map/cond
  25.1 16.6 %collective-permute-start.41 = (bf16[576,256]{1,0:T(8,128)(2,1)S(1)}, bf16[576,256]{1,0:T(8,128)(2,1)S(1)}, u32[]{:S(2)}, u32[]{:S(2)}) collective-permute-start(bf16[576,256]{1,0:T(8,128)(2,1)S(1)} %bitcast.38), channel_id=1, source_target_pairs={{0,2},{1,3},{2,0},{3,1},{4,6},{5,7},{6,4},{7,5},{8,10},{9,11},{10,... | collective-permute-start | bytes 884744 | tf_op jit(solution)/shard_map/cond/branch_6_fun/ppermute | solution.py:342
  42.0 1.6 %collective-permute-start.42 = (bf16[576,256]{1,0:T(8,128)(2,1)S(1)}, bf16[576,256]{1,0:T(8,128)(2,1)S(1)}, u32[]{:S(2)}, u32[]{:S(2)}) collective-permute-start(bf16[576,256]{1,0:T(8,128)(2,1)S(1)} %get-tuple-element.270.total), channel_id=1, source_target_pairs={{0,4},{4,0},{8,12},{12,8},{16,20},{20,16},{24,28},{28,24},{1,5},{5... | collective-permute-start | bytes 884744 | tf_op jit(solution)/shard_map/ppermute | solution.py:358
  44.2 6.8 %collective-permute-start.43 = (bf16[576,128]{1,0:T(8,128)(2,1)S(1)}, bf16[576,128]{1,0:T(8,128)(2,1)S(1)}, u32[]{:S(2)}, u32[]{:S(2)}) collective-permute-start(bf16[576,128]{1,0:T(8,128)(2,1)S(1)} %get-tuple-element.273), channel_id=1, source_target_pairs={{0,8},{4,12},{8,0},{12,4},{16,24},{20,28},{24,16},{28,20},{1,9},{5... | collective-permute-start | bytes 442376 | tf_op jit(solution)/shard_map/ppermute | solution.py:360
  44.4 9.0 %collective-permute-start.44 = (bf16[576,128]{1,0:T(8,128)(2,1)S(1)}, bf16[576,128]{1,0:T(8,128)(2,1)S(1)}, u32[]{:S(2)}, u32[]{:S(2)}) collective-permute-start(bf16[576,128]{1,0:T(8,128)(2,1)S(1)} %get-tuple-element.274), channel_id=1, source_target_pairs={{0,16},{4,20},{8,24},{12,28},{16,0},{20,4},{24,8},{28,12},{1,17},{... | collective-permute-start | bytes 442376 | tf_op jit(solution)/shard_map/ppermute | solution.py:360
  45.7 7.7 %collective-permute-start.45 = (bf16[576,128]{1,0:T(8,128)(2,1)S(1)}, bf16[576,128]{1,0:T(8,128)(2,1)S(1)}, u32[]{:S(2)}, u32[]{:S(2)}) collective-permute-start(bf16[576,128]{1,0:T(8,128)(2,1)S(1)} %get-tuple-element.275), channel_id=1, source_target_pairs={{0,24},{4,28},{8,16},{12,20},{16,8},{20,12},{24,0},{28,4},{1,25},{... | collective-permute-start | bytes 442376 | tf_op jit(solution)/shard_map/ppermute | solution.py:360
